TPU v7x, 128 devices: a whole 4x4x4 slice. The times are simulated.
128 devices in a mesh: ctx: 16 (over x, y), exp: 8 (over z, core).
Axes of the slice: x: 4, y: 4, z: 4, core: 2. Of those that a mesh axis runs over, the one named last changes fastest.
Arguments:
- mixer_in: bfloat16 [2048, 16384], P('ctx', 'exp'), may hold values from -6 to 6
- gate_in: bfloat16 [2048, 16384], P('ctx', 'exp'), may hold values from -6 to 6
- delta_in: bfloat16 [2048, 16384], P('ctx', 'exp'), may hold values from -3 to 3
- b_proj: float32 [16, 2048], P(None, 'ctx'), may hold values from -0.6 to 0.6
- c_proj: float32 [16, 2048], P(None, 'ctx'), may hold values from -1.8 to 1.8
- conv_kernel: float32 [4, 16384], P(None, 'exp'), may hold values from -3 to 3
- conv_bias: float32 [16384], P('exp'), may hold values from -0.5 to 0.5
- delta_bias: float32 [16384], P('exp'), may hold values from -1 to 0
- decay_log: float32 [16, 16384], P(None, 'exp'), may hold values from -12 to -2
- skip_gain: float32 [16384], P('exp'), may hold values from 0.5 to 1.5
- prefix_state: float32 [16, 16384], P(None, 'exp'), may hold values from -6 to 6
- prefix_tail: bfloat16 [3, 16384], P(None, 'exp'), may hold values from -6 to 6
- out_proj: bfloat16 [16384, 8192], P('exp', 'ctx'), may hold values from -0.046875 to 0.046875
- residual: bfloat16 [2048, 8192], P('exp', 'ctx'), may hold values from -40 to 40
- norm_gain: float32 [8192], P('ctx'), may hold values from 0.1 to 1.9
- expert_gate: bfloat16 [8, 8192, 6144], P('exp', None, 'ctx'), may hold values from -0.0625 to 0.0625
- expert_up: bfloat16 [8, 8192, 6144], P('exp', None, 'ctx'), may hold values from -0.0625 to 0.0625
- expert_down: bfloat16 [8, 6144, 8192], P('exp', 'ctx'), may hold values from -0.109375 to 0.109375
- expert_ids: int32 [2048, 2], P('exp'), may hold values from 0 to 7, all different within a row; in each aligned block of 256 rows (0 to 255, 256 to 511, ...) at most 96 rows name the same one
- route_gates: float32 [2048, 2], P('exp'), may hold values from 0.2 to 1
Outputs:
- mixer_out: bfloat16 [2048, 8192], P('exp', 'ctx')
- block_out: bfloat16 [2048, 8192], P('exp', 'ctx')
Inputs may be any that keep to these rules, and one draw needn't show every extreme that they name: `expert_ids`: each row names 2 different experts. Within each aligned block of 256 rows (the rows of one index of exp) no expert is named more than 96 times, and in every draw some expert is named exactly 96 times in some block.
All inputs are finite; a program needn't handle non-finite values.
Results may differ from a plain program's by a relative error of at most 0.015.
Values may be sent and summed in bfloat16 or wider, within the bound.
A program may use at most 128 MiB of HBM per device.

v0:
```python
import jax
import jax.numpy as jnp
from jax import lax
from jax.sharding import PartitionSpec as P

D = 8192


def from_behind(array, axis, by):
    length = lax.axis_size(axis)
    pairs = [(i, i + by) for i in range(length) if 0 <= i + by < length]
    return lax.ppermute(array, axis, pairs)


def shards(
    mixer_in,
    gate_in,
    delta_in,
    b_proj,
    c_proj,
    conv_kernel,
    conv_bias,
    delta_bias,
    decay_log,
    skip_gain,
    prefix_state,
    prefix_tail,
    out_proj,
    residual,
    norm_gain,
    expert_gate,
    expert_up,
    expert_down,
    expert_ids,
    route_gates,
):
    tokens = mixer_in.shape[0]
    width = prefix_tail.shape[0]
    leading = lax.axis_index("ctx") == 0
    rim_rows = from_behind(mixer_in[tokens - width :], "ctx", 1)
    rim_rows = jnp.where(leading, prefix_tail, rim_rows)
    padded = jnp.concatenate([rim_rows, mixer_in], axis=0).astype(jnp.float32)
    convolved = conv_bias[None, :] + sum(
        (
            conv_kernel[tap_index][None, :] * padded[tap_index : tap_index + tokens]
            for tap_index in range(width + 1)
        )
    )
    conv_act = jax.nn.silu(convolved)
    step_size = jax.nn.softplus(delta_in.astype(jnp.float32) + delta_bias[None, :])
    decay_rate = -jnp.exp(decay_log)
    driving = step_size * conv_act
    b_rows = b_proj.T
    c_rows = c_proj.T
    group_len = 8
    group_count = tokens // group_len

    def advance(carry_state, inputs):
        step_group, drive_group, b_group, c_group = inputs
        outputs = []
        for offset in range(group_len):
            carry_state = (
                jnp.exp(step_group[offset][None, :] * decay_rate) * carry_state
                + b_group[offset][:, None] * drive_group[offset][None, :]
            )
            outputs.append(jnp.sum(c_group[offset][:, None] * carry_state, axis=0))
        return (carry_state, jnp.stack(outputs))

    local_end, local_out = lax.scan(
        advance,
        jnp.zeros_like(prefix_state),
        (
            step_size.reshape(group_count, group_len, -1),
            driving.reshape(group_count, group_len, -1),
            b_rows.reshape(group_count, group_len, -1),
            c_rows.reshape(group_count, group_len, -1),
        ),
    )
    local_out = local_out.reshape(tokens, -1)
    elapsed = jnp.cumsum(step_size, axis=0)
    through = jnp.exp(decay_rate * elapsed[tokens - 1][None, :])

    def relay_step(step_number, entry_state):
        passed = from_behind(
            (through * entry_state + local_end).astype(jnp.bfloat16), "ctx", 1
        ).astype(jnp.float32)
        return jnp.where(leading, prefix_state, passed)

    entry_state = lax.fori_loop(0, lax.axis_size("ctx") - 1, relay_step, prefix_state)
    carried = jnp.exp(decay_rate[None, :, :] * elapsed[:, None, :]) * entry_state[None, :, :]
    mixed_out = (
        local_out + jnp.sum(c_rows[:, :, None] * carried, axis=1) + skip_gain[None, :] * conv_act
    )
    gated_rows = (mixed_out * jax.nn.silu(gate_in.astype(jnp.float32))).astype(jnp.bfloat16)
    gathered = lax.all_gather(gated_rows, "ctx", axis=0, tiled=True)
    block_rows = residual.shape[0]
    projected = lax.psum_scatter(
        jnp.dot(
            lax.slice_in_dim(gathered, 0, lax.axis_size("exp") * block_rows, axis=0),
            out_proj,
            preferred_element_type=jnp.float32,
        ).astype(jnp.bfloat16),
        "exp",
        scatter_dimension=0,
        tiled=True,
    ).astype(jnp.float32)
    mixer_out = (residual.astype(jnp.float32) + projected).astype(jnp.bfloat16)
    mixer_wide = mixer_out.astype(jnp.float32)
    squares = lax.psum(jnp.sum(mixer_wide * mixer_wide, axis=1), "ctx")
    norm_scale = lax.rsqrt(squares / D + 1e-05)
    normed = (mixer_wide * norm_scale[:, None] * norm_gain[None, :]).astype(jnp.bfloat16)
    experts = expert_gate.shape[0] * lax.axis_size("exp")
    top_count = expert_ids.shape[1]
    capacity = 3 * block_rows * top_count // (2 * experts)
    flat_choice = expert_ids.reshape(-1)
    owner_hot = (flat_choice[:, None] == jnp.arange(experts, dtype=jnp.int32)[None, :]).astype(
        jnp.int32
    )
    earlier_count = jnp.cumsum(owner_hot, axis=0) - owner_hot
    slot_index = jnp.sum(earlier_count * owner_hot, axis=1)
    matches = (
        flat_choice[:, None, None] == jnp.arange(experts, dtype=jnp.int32)[None, :, None]
    ) & (slot_index[:, None, None] == jnp.arange(capacity, dtype=jnp.int32)[None, None, :])
    picks = matches.reshape(block_rows, top_count, experts, capacity)
    selector = jnp.any(picks, axis=1).astype(jnp.bfloat16)
    weights = jnp.sum(picks.astype(jnp.float32) * route_gates[:, :, None, None], axis=1)
    slot_total = experts * capacity
    outgoing = jnp.einsum(
        "tec,td->ecd", selector, normed, preferred_element_type=jnp.float32
    ).astype(jnp.bfloat16)
    received = lax.all_to_all(outgoing, "exp", split_axis=0, concat_axis=0, tiled=True)
    arrived = received.reshape(slot_total, -1)
    piece_rows = lax.all_gather(arrived, "ctx", axis=1, tiled=True)
    feature_count = piece_rows.shape[1]
    gate_rows = lax.slice_in_dim(expert_gate[0], 0, feature_count, axis=0)
    up_rows = lax.slice_in_dim(expert_up[0], 0, feature_count, axis=0)
    gate_act = jnp.dot(piece_rows, gate_rows, preferred_element_type=jnp.float32)
    up_act = jnp.dot(piece_rows, up_rows, preferred_element_type=jnp.float32)
    hidden = (jax.nn.silu(gate_act) * up_act).astype(jnp.bfloat16)
    partial_value = jnp.dot(hidden, expert_down[0], preferred_element_type=jnp.float32)
    summed = lax.psum_scatter(
        partial_value.astype(jnp.bfloat16), "ctx", scatter_dimension=1, tiled=True
    )
    answer = summed.reshape(experts, capacity, -1)
    returned = lax.all_to_all(answer, "exp", split_axis=0, concat_axis=0, tiled=True)
    expert_mix = jnp.einsum(
        "tec,ecd->td", weights, returned.astype(jnp.float32), preferred_element_type=jnp.float32
    )
    block_out = (mixer_wide + expert_mix).astype(jnp.bfloat16)
    return (mixer_out, block_out)


def solution(mesh):
    placed = (
        P("ctx", "exp"),
        P("ctx", "exp"),
        P("ctx", "exp"),
        P(None, "ctx"),
        P(None, "ctx"),
        P(None, "exp"),
        P("exp"),
        P("exp"),
        P(None, "exp"),
        P("exp"),
        P(None, "exp"),
        P(None, "exp"),
        P("exp", "ctx"),
        P("exp", "ctx"),
        P("ctx"),
        P("exp", None, "ctx"),
        P("exp", None, "ctx"),
        P("exp", "ctx", None),
        P("exp", None),
        P("exp", None),
    )
    return jax.shard_map(
        shards,
        mesh=mesh,
        in_specs=placed,
        out_specs=(P("exp", "ctx"), P("exp", "ctx")),
        check_vma=False,
    )
```

profile of v0, /device:TPU:1, one launch (start us, length us, event | category | flops | bytes accessed | tf_op | source)
XLA Modules:
  0.0 631.0 jit_solution(2872491774888158628)
XLA Ops:
  8.1 4.0 collective-permute-start.1
  17.6 4.0 multiply_bitcast_fusion
  21.7 3.1 reduce_window_sum.26
  25.7 51.6 %while.24 = (s32[]{:T(128)}, f32[16,2048]{1,0:T(8,128)S(1)}, f32[16,8,2048]{2,1,0:T(8,128)}, f32[16,8,2048]{2,1,0:T(8,128)}, f32[16,2048]{1,0:T(8,128)S(1)}, /*i...) while((s32[]{:T(128)}, f32[16,2048]{1,0:T(8,128)S(1)}, ...), condition=%wide.region_9.10_spmd.clone, body=%wide.region_0.9_spmd.clone.sunk | while | flops 2277386 | bytes 2381920 | solution.py:69
  25.7 1.6 constant_dynamic-slice_fusion.21
  28.9 1.9 constant_dynamic-slice_fusion.21
  38.6 1.6 constant_dynamic-slice_fusion.21
  41.7 1.6 constant_dynamic-slice_fusion.21
  44.9 1.9 constant_dynamic-slice_fusion.21
  48.3 1.9 constant_dynamic-slice_fusion.21
  51.7 1.6 constant_dynamic-slice_fusion.21
  57.9 1.6 constant_dynamic-slice_fusion.21
  61.1 1.9 constant_dynamic-slice_fusion.21
  64.5 1.9 constant_dynamic-slice_fusion.21
  71.0 1.6 constant_dynamic-slice_fusion.21
  74.2 1.6 constant_dynamic-slice_fusion.21
  77.3 96.9 %while.23 = (s32[]{:T(128)}, f32[16,2048]{1,0:T(8,128)S(1)}, pred[]{:T(512)}, f32[16,2048]{1,0:T(8,128)S(1)}, f32[16,2048]{1,0:T(8,128)S(1)}, /*index=5*/f32[16,2048]{1,0:T(8,128)S(1)}, s32[]{:T(128)}) while((s32[]{:T(128)}, f32[16,2048]{1,0:T(8,128)S(1)}, pred[]{:T(512)}, f32[16,2048]{1,0:T(8,128)S(1)}, f32[16,2048]{1,0:T(8,128)S(1)}, ...), condition=%wide.region_12.13_spmd, body=%wide.region_11.12_spmd.sunk | while | flops 163842 | bytes 1048694 | solution.py:89
  77.4 2.6 collective-permute-start
  81.4 3.7 collective-permute-start
  86.5 3.7 collective-permute-start
  91.5 3.7 collective-permute-start
  96.6 3.7 collective-permute-start
  100.3 1.7 collective-permute-done
  102.1 5.4 collective-permute-start
  108.8 5.8 collective-permute-start
  114.6 1.8 collective-permute-done
  116.5 5.8 collective-permute-start
  123.6 5.6 collective-permute-start
  130.5 5.9 collective-permute-start
  137.8 5.8 collective-permute-start
  145.0 5.8 collective-permute-start
  152.2 5.8 collective-permute-start
  159.4 5.8 collective-permute-start
  166.8 6.1 collective-permute-start
  174.3 6.9 %multiply_reduce_fusion.8 = f32[128,2048]{1,0:T(8,128)S(1)} fusion(f32[16,2048]{1,0:T(8,128)S(1)} %get-tuple-element.79, f32[128,2048]{1,0:T(8,128)} %reduce_window_sum.26, f32[16,2048]{1,0:T(8,128)S(1)} %get-tuple-element.452, f32[128,16]{1,0:T(8,128)S(1)} %bitcast.210), kind=kLoop, calls=%fused_computation.54 | loop fusion | flops 16515072 | bytes 2367488 | tf_op jit(solution)/shard_map/reduce_sum | solution.py:92
  182.6 99.6 %all-gather.3.cloned.1.call-done = bf16[2048,2048]{1,0:T(8,128)(2,1)} async-done(((bf16[128,2048]{1,0:T(8,128)(2,1)}), bf16[2048,2048]{1,0:T(8,128)(2,1)}) %all-gather.3.cloned.1.call-update) | async-done | bytes 8388624 | tf_op jit(solution)/shard_map/all_gather | solution.py:95
  282.2 9.2 %convolution_convert_fusion.1 = bf16[2048,512]{1,0:T(8,128)(2,1)} fusion(bf16[2048,2048]{1,0:T(8,128)(2,1)} %all-gather.3.cloned.1.call-done, bf16[2048,512]{1,0:T(8,128)(2,1)S(1)} %copy-done), kind=kOutput, calls=%fused_computation.62 | convolution fusion | flops 4296015872 | bytes 12582912 | tf_op jit(solution)/shard_map/dot_general | solution.py:98
  293.8 28.1 %reduce-scatter.3.cloned.1.call-done = bf16[256,512]{1,0:T(8,128)(2,1)} async-done(((bf16[2048,512]{1,0:T(8,128)(2,1)}), bf16[256,512]{1,0:T(8,128)(2,1)}) %reduce-scatter.3.cloned.1.call-update) | async-done | bytes 262160 | tf_op jit(solution)/shard_map/reduce_scatter | solution.py:97
  323.1 33.5 %psum.7 = f32[256]{0:T(256)S(1)} all-reduce(f32[256]{0:T(256)S(1)} %get-tuple-element.146), channel_id=1, replica_groups=mesh['ctx'=16,'exp'=8] {'ctx'}, use_global_device_ids=true, to_apply=%region_21.22 | all-reduce | flops 256 | bytes 2048 | tf_op jit(solution)/shard_map/psum | solution.py:109
  357.1 25.9 %all_to_all.10 = bf16[8,96,512]{2,1,0:T(8,128)(2,1)} all-to-all(bf16[8,96,512]{2,1,0:T(8,128)(2,1)S(1)} %convolution_convert_fusion.2), channel_id=1, replica_groups=mesh['ctx'=16,'exp'=8] {'exp'}, dimensions={0} | all-to-all | bytes 1572864 | tf_op jit(solution)/shard_map/all_to_all | solution.py:131
  383.3 93.4 %all-gather.5.cloned.1.call-done = bf16[768,8192]{1,0:T(8,128)(2,1)} async-done(((bf16[768,512]{1,0:T(8,128)(2,1)}), bf16[768,8192]{1,0:T(8,128)(2,1)}) %all-gather.5.cloned.1.call-update) | async-done | bytes 12582928 | tf_op jit(solution)/shard_map/all_gather | solution.py:133
  476.6 12.0 %fusion.4 = f32[768,384]{1,0:T(8,128)S(1)} fusion(bf16[768,8192]{1,0:T(8,128)(2,1)} %all-gather.5.cloned.1.call-done, bf16[1,8192,384]{2,1,0:T(8,128)(2,1)} %param.39), kind=kOutput, calls=%fused_computation.59 | convolution fusion | flops 4831838208 | bytes 20054016 | tf_op jit(solution)/shard_map/dot_general | solution.py:137
  488.7 9.2 %fusion.10 = bf16[768,384]{1,0:T(8,128)(2,1)S(1)} fusion(bf16[768,8192]{1,0:T(8,128)(2,1)S(1)} %copy-done.12, bf16[1,8192,384]{2,1,0:T(8,128)(2,1)} %param.40, f32[768,384]{1,0:T(8,128)S(1)} %fusion.4), kind=kOutput, calls=%fused_computation.68 | convolution fusion | flops 4833607680 | bytes 20643840 | tf_op jit(solution)/shard_map/dot_general | solution.py:138
  497.9 12.3 %convolution_convert_fusion = bf16[768,8192]{1,0:T(8,128)(2,1)} fusion(bf16[768,384]{1,0:T(8,128)(2,1)S(1)} %fusion.10, bf16[1,384,8192]{2,1,0:T(8,128)(2,1)} %param.41), kind=kOutput, calls=%fused_computation.55 | convolution fusion | flops 4838129664 | bytes 19464192 | tf_op jit(solution)/shard_map/dot_general | solution.py:140
  510.2 94.6 %reduce-scatter.5.cloned.1.call-done = bf16[768,512]{1,0:T(8,128)(2,1)} async-done(((bf16[768,8192]{1,0:T(8,128)(2,1)}), bf16[768,512]{1,0:T(8,128)(2,1)}) %reduce-scatter.5.cloned.1.call-update) | async-done | bytes 786448 | tf_op jit(solution)/shard_map/reduce_scatter | solution.py:141
  604.8 5.3 all-to-all-start.1
  610.4 12.1 %all-to-all-done.1 = bf16[8,96,512]{2,1,0:T(8,128)(2,1)S(1)} async-done(((bf16[8,96,512]{2,1,0:T(8,128)(2,1)}), bf16[8,96,512]{2,1,0:T(8,128)(2,1)S(1)}, u32[]{:S(2)}, u32[]{:S(2)}) %all-to-all-start.1) | async-done | bytes 786464 | tf_op jit(solution)/shard_map/all_to_all | solution.py:145
  622.4 2.0 fusion.14
  (258 shorter events, 60.7 us)
Async XLA Ops:
  7.2 275.0 %copy-start = (bf16[2048,512]{1,0:T(8,128)(2,1)S(1)}, bf16[2048,512]{1,0:T(8,128)(2,1)}, u32[]{:S(2)}) copy-start(bf16[2048,512]{1,0:T(8,128)(2,1)} %param.36) | copy-start | bytes 6291460
  7.2 275.0 %all-gather.3.cloned.1.call-start = ((), (), s32[]{:S(2)}) async-start(), calls=%async_computation.4 | async-start | bytes 8912896 | tf_op jit(solution)/shard_map/all_gather | solution.py:95
  8.1 7.5 %collective-permute-start.1 = (bf16[3,2048]{1,0:T(4,128)(2,1)S(1)}, bf16[3,2048]{1,0:T(4,128)(2,1)S(1)}, u32[]{:S(2)}, u32[]{:S(2)}) collective-permute-start(bf16[3,2048]{1,0:T(4,128)(2,1)S(1)} %slice.165), channel_id=1, source_target_pairs={{0,8},{8,16},{16,24},{24,32},{32,40},{40,48},{48,56},{56,64},{64,7... | collective-permute-start | bytes 36872 | tf_op jit(solution)/shard_map/ppermute | solution.py:12
  16.4 9.3 %copy-start.8 = (f32[16,2048]{1,0:T(8,128)S(1)}, f32[16,2048]{1,0:T(8,128)}, u32[]{:S(2)}) copy-start(f32[16,2048]{1,0:T(8,128)} %param.32) | copy-start | bytes 393220
  25.7 51.6 %copy-start.2 = (f32[16,2048]{1,0:T(8,128)S(1)}, f32[16,2048]{1,0:T(8,128)}, u32[]{:S(2)}) copy-start(f32[16,2048]{1,0:T(8,128)} %param.34) | copy-start | bytes 393220
  77.3 103.9 %copy-start.5 = (bf16[128,2048]{1,0:T(8,128)(2,1)S(1)}, bf16[128,2048]{1,0:T(8,128)(2,1)}, u32[]{:S(2)}) copy-start(bf16[128,2048]{1,0:T(8,128)(2,1)} %param.25) | copy-start | bytes 1572868
  77.3 103.9 %copy-start.9 = (f32[2048]{0:T(1024)S(1)}, f32[2048]{0:T(1024)}, u32[]{:S(2)}) copy-start(f32[2048]{0:T(1024)} %param.33) | copy-start | bytes 24580
  77.4 3.9 collective-permute-start
  81.4 5.0 collective-permute-start
  86.5 5.0 collective-permute-start
  91.5 5.0 collective-permute-start
  96.6 5.4 collective-permute-start
  102.1 6.7 %collective-permute-start = (bf16[16,2048]{1,0:T(8,128)(2,1)S(1)}, bf16[16,2048]{1,0:T(8,128)(2,1)S(1)}, u32[]{:S(2)}, u32[]{:S(2)}) collective-permute-start(bf16[16,2048]{1,0:T(8,128)(2,1)S(1)} %add_convert_fusion.4), channel_id=1, source_target_pairs={{0,8},{8,16},{16,24},{24,32},{32,40},{40,48},{48,56},{56,64},{64,7... | collective-permute-start | bytes 196616 | tf_op jit(solution)/shard_map/while/body/eval_jaxpr/ppermute | solution.py:12
  108.8 7.6 %collective-permute-start = (bf16[16,2048]{1,0:T(8,128)(2,1)S(1)}, bf16[16,2048]{1,0:T(8,128)(2,1)S(1)}, u32[]{:S(2)}, u32[]{:S(2)}) collective-permute-start(bf16[16,2048]{1,0:T(8,128)(2,1)S(1)} %add_convert_fusion.4), channel_id=1, source_target_pairs={{0,8},{8,16},{16,24},{24,32},{32,40},{40,48},{48,56},{56,64},{64,7... | collective-permute-start | bytes 196616 | tf_op jit(solution)/shard_map/while/body/eval_jaxpr/ppermute | solution.py:12
  116.5 7.1 %collective-permute-start = (bf16[16,2048]{1,0:T(8,128)(2,1)S(1)}, bf16[16,2048]{1,0:T(8,128)(2,1)S(1)}, u32[]{:S(2)}, u32[]{:S(2)}) collective-permute-start(bf16[16,2048]{1,0:T(8,128)(2,1)S(1)} %add_convert_fusion.4), channel_id=1, source_target_pairs={{0,8},{8,16},{16,24},{24,32},{32,40},{40,48},{48,56},{56,64},{64,7... | collective-permute-start | bytes 196616 | tf_op jit(solution)/shard_map/while/body/eval_jaxpr/ppermute | solution.py:12
  123.6 6.9 %collective-permute-start = (bf16[16,2048]{1,0:T(8,128)(2,1)S(1)}, bf16[16,2048]{1,0:T(8,128)(2,1)S(1)}, u32[]{:S(2)}, u32[]{:S(2)}) collective-permute-start(bf16[16,2048]{1,0:T(8,128)(2,1)S(1)} %add_convert_fusion.4), channel_id=1, source_target_pairs={{0,8},{8,16},{16,24},{24,32},{32,40},{40,48},{48,56},{56,64},{64,7... | collective-permute-start | bytes 196616 | tf_op jit(solution)/shard_map/while/body/eval_jaxpr/ppermute | solution.py:12
  130.5 7.2 %collective-permute-start = (bf16[16,2048]{1,0:T(8,128)(2,1)S(1)}, bf16[16,2048]{1,0:T(8,128)(2,1)S(1)}, u32[]{:S(2)}, u32[]{:S(2)}) collective-permute-start(bf16[16,2048]{1,0:T(8,128)(2,1)S(1)} %add_convert_fusion.4), channel_id=1, source_target_pairs={{0,8},{8,16},{16,24},{24,32},{32,40},{40,48},{48,56},{56,64},{64,7... | collective-permute-start | bytes 196616 | tf_op jit(solution)/shard_map/while/body/eval_jaxpr/ppermute | solution.py:12
  137.8 7.1 %collective-permute-start = (bf16[16,2048]{1,0:T(8,128)(2,1)S(1)}, bf16[16,2048]{1,0:T(8,128)(2,1)S(1)}, u32[]{:S(2)}, u32[]{:S(2)}) collective-permute-start(bf16[16,2048]{1,0:T(8,128)(2,1)S(1)} %add_convert_fusion.4), channel_id=1, source_target_pairs={{0,8},{8,16},{16,24},{24,32},{32,40},{40,48},{48,56},{56,64},{64,7... | collective-permute-start | bytes 196616 | tf_op jit(solution)/shard_map/while/body/eval_jaxpr/ppermute | solution.py:12
  145.0 7.1 %collective-permute-start = (bf16[16,2048]{1,0:T(8,128)(2,1)S(1)}, bf16[16,2048]{1,0:T(8,128)(2,1)S(1)}, u32[]{:S(2)}, u32[]{:S(2)}) collective-permute-start(bf16[16,2048]{1,0:T(8,128)(2,1)S(1)} %add_convert_fusion.4), channel_id=1, source_target_pairs={{0,8},{8,16},{16,24},{24,32},{32,40},{40,48},{48,56},{56,64},{64,7... | collective-permute-start | bytes 196616 | tf_op jit(solution)/shard_map/while/body/eval_jaxpr/ppermute | solution.py:12
  152.2 7.1 %collective-permute-start = (bf16[16,2048]{1,0:T(8,128)(2,1)S(1)}, bf16[16,2048]{1,0:T(8,128)(2,1)S(1)}, u32[]{:S(2)}, u32[]{:S(2)}) collective-permute-start(bf16[16,2048]{1,0:T(8,128)(2,1)S(1)} %add_convert_fusion.4), channel_id=1, source_target_pairs={{0,8},{8,16},{16,24},{24,32},{32,40},{40,48},{48,56},{56,64},{64,7... | collective-permute-start | bytes 196616 | tf_op jit(solution)/shard_map/while/body/eval_jaxpr/ppermute | solution.py:12
  159.4 7.4 %collective-permute-start = (bf16[16,2048]{1,0:T(8,128)(2,1)S(1)}, bf16[16,2048]{1,0:T(8,128)(2,1)S(1)}, u32[]{:S(2)}, u32[]{:S(2)}) collective-permute-start(bf16[16,2048]{1,0:T(8,128)(2,1)S(1)} %add_convert_fusion.4), channel_id=1, source_target_pairs={{0,8},{8,16},{16,24},{24,32},{32,40},{40,48},{48,56},{56,64},{64,7... | collective-permute-start | bytes 196616 | tf_op jit(solution)/shard_map/while/body/eval_jaxpr/ppermute | solution.py:12
  166.8 7.5 %collective-permute-start = (bf16[16,2048]{1,0:T(8,128)(2,1)S(1)}, bf16[16,2048]{1,0:T(8,128)(2,1)S(1)}, u32[]{:S(2)}, u32[]{:S(2)}) collective-permute-start(bf16[16,2048]{1,0:T(8,128)(2,1)S(1)} %add_convert_fusion.4), channel_id=1, source_target_pairs={{0,8},{8,16},{16,24},{24,32},{32,40},{40,48},{48,56},{56,64},{64,7... | collective-permute-start | bytes 196616 | tf_op jit(solution)/shard_map/while/body/eval_jaxpr/ppermute | solution.py:12
  174.3 6.9 %copy-start.3 = (f32[128,2048]{1,0:T(8,128)S(1)}, f32[128,2048]{1,0:T(8,128)}, u32[]{:S(2)}) copy-start(f32[128,2048]{1,0:T(8,128)} %get-tuple-element.149) | copy-start | bytes 3145732
  174.3 6.9 %copy-start.4 = (f32[16,8,2048]{2,1,0:T(8,128)S(1)}, f32[16,8,2048]{2,1,0:T(8,128)}, u32[]{:S(2)}) copy-start(f32[16,8,2048]{2,1,0:T(8,128)} %get-tuple-element.77) | copy-start | bytes 3145732
  182.5 108.9 %copy-start.10 = (s32[256,2]{0,1:T(2,128)S(1)}, s32[256,2]{0,1:T(2,128)}, u32[]{:S(2)}) copy-start(s32[256,2]{0,1:T(2,128)} %param.42) | copy-start | bytes 6148
  182.5 139.4 %copy-start.6 = (bf16[256,512]{1,0:T(8,128)(2,1)S(1)}, bf16[256,512]{1,0:T(8,128)(2,1)}, u32[]{:S(2)}) copy-start(bf16[256,512]{1,0:T(8,128)(2,1)} %param.37) | copy-start | bytes 786436
  182.5 174.1 %copy-start.13 = (f32[512]{0:T(512)S(1)}, f32[512]{0:T(512)}, u32[]{:S(2)}) copy-start(f32[512]{0:T(512)} %param.38) | copy-start | bytes 6148
  182.6 139.4 %reduce-scatter.3.cloned.1.call-start = ((), (), s32[]{:S(2)}) async-start(), calls=%async_computation.5 | async-start | bytes 2359296 | tf_op jit(solution)/shard_map/reduce_scatter | solution.py:97
  291.4 185.2 %all-gather.5.cloned.1.call-start = ((), (), s32[]{:S(2)}) async-start(), calls=%async_computation.6 | async-start | bytes 13369344 | tf_op jit(solution)/shard_map/all_gather | solution.py:133
  323.1 165.5 %copy-start.7 = (bf16[256,512]{1,0:T(8,128)(2,1)}, bf16[256,512]{1,0:T(8,128)(2,1)S(1)}, u32[]{:S(2)}) copy-start(bf16[256,512]{1,0:T(8,128)(2,1)S(1)} %get-tuple-element.147) | copy-start | bytes 786436
  383.1 221.8 %reduce-scatter.5.cloned.1.call-start = ((), (), s32[]{:S(2)}) async-start(), calls=%async_computation.7 | async-start | bytes 13369344 | tf_op jit(solution)/shard_map/reduce_scatter | solution.py:141
  476.6 12.0 %copy-start.12 = (bf16[768,8192]{1,0:T(8,128)(2,1)S(1)}, bf16[768,8192]{1,0:T(8,128)(2,1)}, u32[]{:S(2)}) copy-start(bf16[768,8192]{1,0:T(8,128)(2,1)} %all-gather.5.cloned.1.call-done) | copy-start | bytes 37748740
  510.2 114.3 %copy-start.1 = (bf16[2048,512]{1,0:T(8,128)(2,1)S(1)}, bf16[2048,512]{1,0:T(8,128)(2,1)}, u32[]{:S(2)}) copy-start(bf16[2048,512]{1,0:T(8,128)(2,1)} %param.36) | copy-start | bytes 6291460
  510.2 99.9 %copy-start.11 = (f32[256,2]{0,1:T(2,128)S(1)}, f32[256,2]{0,1:T(2,128)}, u32[]{:S(2)}) copy-start(f32[256,2]{0,1:T(2,128)} %param.43) | copy-start | bytes 6148
  604.8 17.6 %all-to-all-start.1 = ((bf16[8,96,512]{2,1,0:T(8,128)(2,1)}), bf16[8,96,512]{2,1,0:T(8,128)(2,1)S(1)}, u32[]{:S(2)}, u32[]{:S(2)}) async-start(bf16[8,96,512]{2,1,0:T(8,128)(2,1)} %bitcast.208), calls=%async_computation.3 | async-start | bytes 1572864 | tf_op jit(solution)/shard_map/all_to_all | solution.py:145
Sparse Core Ops, SparseCore 0:
  182.6 99.5 all-gather.2
  291.5 30.4 reduce-scatter.2
  383.2 93.4 all-gather.4
  510.4 94.4 reduce-scatter.4
where the time goes:
time: 634 us; the launch traced here: 631 us
  waiting for transfers between devices  349 us (55%)
  starting transfers between devices  84.8 us (13%)
  blocking collectives  59.4 us (9%)
  local copies, waits for them, and re-layouts  45.9 us (7%)
  matrix products  45.2 us (7%)
  other arithmetic  31.5 us (5%)
  between operations  14.1 us (2%)
    all_gather x1, waiting for transfers between devices, shards(): gathered = lax.all_gather(gated_rows, 'ctx', axis=0, tiled=True)  99.6 us
    reduce_scatter x1, waiting for transfers between devices, shards(): lax.psum_scatter(partial_value.astype(jnp.bfloat16), 'ctx', scatter_dimen...  94.6 us
    all_gather x1, waiting for transfers between devices, shards(): piece_rows = lax.all_gather(arrived, 'ctx', axis=1, tiled=True)  93.4 us
    ppermute x16, starting transfers between devices, from_behind(): return lax.ppermute(array, axis, pairs)  79.2 us
    psum x1, blocking collectives, shards(): squares = lax.psum(jnp.sum(mixer_wide * mixer_wide, axis=1), 'ctx')  33.5 us
    reduce_scatter x1, waiting for transfers between devices, shards(): lax.psum_scatter(jnp.dot(lax.slice_in_dim(gathered, 0, lax.axis_size('exp...  28.1 us
    slice x16, local copies, waits for them, and re-layouts, advance(): drive_group[offset][None, :]  27.4 us
    all_to_all x1, blocking collectives, shards(): lax.all_to_all(outgoing, 'exp', split_axis=0, concat_axis=0, tiled=True)  25.9 us
  transfers between devices with their start and end apart: 21, of which 20 were waited for; matrix products, arithmetic and copies ran while one was open for 1% of the time, Pallas kernels for 0%

commit v1 on v0

--- a/solution.py
+++ b/solution.py
@@ -1,9 +1,294 @@
+import functools
+import math
+
 import jax
 import jax.numpy as jnp
 from jax import lax
+from jax.experimental import pallas as pl
+from jax.experimental.pallas import tpu as pltpu
 from jax.sharding import PartitionSpec as P
 
 D = 8192
+SIDE = 4
+STATES = 16
+LANES = 128
+STRIP = 512
+LOG2E = math.log2(math.e)
+MESH = pl.DeviceIdType.MESH
+
+
+def strip_spec(rows):
+    return pl.BlockSpec((rows, STRIP), lambda i: (0, i))
+
+
+def whole_spec(shape):
+    return pl.BlockSpec(shape, lambda i: (0,) * len(shape))
+
+
+def lane_parts(value):
+    return tuple(value[:, k * LANES : (k + 1) * LANES] for k in range(STRIP // LANES))
+
+
+def prepare_kernel(
+    rim_ref, mixer_ref, delta_ref, taps_ref, bias_ref, delta_bias_ref, decay_ref, b_ref,
+    act_out, step_out, total_out, end_out, padded, drive,
+):
+    tokens = mixer_ref.shape[0]
+    padded[0:8] = rim_ref[...]
+    padded[8 : 8 + tokens] = mixer_ref[...].astype(jnp.float32)
+    convolved = bias_ref[...]
+    for k in range(4):
+        convolved = convolved + taps_ref[k : k + 1] * padded[5 + k : 5 + k + tokens]
+    act = convolved / (1.0 + jnp.exp(-convolved))
+    step = jnp.log(1.0 + jnp.exp(delta_ref[...].astype(jnp.float32) + delta_bias_ref[...]))
+    act_out[...] = act
+    step_out[...] = step
+    drive[...] = act * step
+    total_out[...] = jnp.sum(step, axis=0, keepdims=True)
+    rate = lane_parts(-jnp.exp(decay_ref[...]) * LOG2E)
+
+    def group(index, state):
+        base = pl.multiple_of(index * 8, 8)
+        steps = step_out[pl.ds(base, 8), :]
+        drives = drive[pl.ds(base, 8), :]
+        for i in range(8):
+            b_column = b_ref[base + i]
+            step_row, drive_row = lane_parts(steps[i : i + 1]), lane_parts(drives[i : i + 1])
+            state = tuple(
+                jnp.exp2(r * s) * h + b_column * d
+                for r, s, h, d in zip(rate, step_row, state, drive_row)
+            )
+        return state
+
+    zero = jnp.zeros((STATES, LANES), jnp.float32)
+    state = lax.fori_loop(0, tokens // 8, group, (zero,) * (STRIP // LANES))
+    end_out[...] = jnp.concatenate(state, axis=1).astype(end_out.dtype)
+
+
+def scan_kernel(
+    place_ref, act_ref, step_ref, gate_ref, decay_ref, prefix_ref, gain_ref, b_ref, c_ref,
+    totals_ref, ends_ref, out_ref, summed, drive,
+):
+    tokens = act_ref.shape[0]
+    rate_whole = -jnp.exp(decay_ref[...]) * LOG2E
+    rate = lane_parts(rate_whole)
+
+    def enter(source, state):
+        return (
+            jnp.exp2(rate_whole * totals_ref[source]) * state
+            + ends_ref[source].astype(jnp.float32)
+        )
+
+    drive[...] = act_ref[...] * step_ref[...]
+    entry = lane_parts(lax.fori_loop(0, place_ref[0], enter, prefix_ref[...]))
+
+    def group(index, state):
+        base = pl.multiple_of(index * 8, 8)
+        steps = step_ref[pl.ds(base, 8), :]
+        drives = drive[pl.ds(base, 8), :]
+        rows = []
+        for i in range(8):
+            b_column, c_column = b_ref[base + i], c_ref[base + i]
+            step_row, drive_row = lane_parts(steps[i : i + 1]), lane_parts(drives[i : i + 1])
+            state = tuple(
+                jnp.exp2(r * s) * h + b_column * d
+                for r, s, h, d in zip(rate, step_row, state, drive_row)
+            )
+            rows.append(
+                jnp.concatenate(
+                    [jnp.sum(c_column * h, axis=0, keepdims=True) for h in state], axis=1
+                )
+            )
+        summed[pl.ds(base, 8), :] = jnp.concatenate(rows, axis=0)
+        return state
+
+    lax.fori_loop(0, tokens // 8, group, entry)
+    gate = gate_ref[...].astype(jnp.float32)
+    mixed = summed[...] + gain_ref[...] * act_ref[...]
+    out_ref[...] = (mixed * (gate / (1.0 + jnp.exp(-gate)))).astype(out_ref.dtype)
+
+
+def exchange_kernel(count, ends_ref, total_ref, all_ends, all_totals, send_sems, recv_sems):
+    me = lax.axis_index("ctx")
+    barrier = pltpu.get_barrier_semaphore()
+    for k in range(1, count):
+
+        @pl.when(me >= k)
+        def _():
+            pl.semaphore_signal(barrier, inc=1, device_id={"ctx": me - k}, device_id_type=MESH)
+
+    @pl.when(me < count - 1)
+    def _():
+        pl.semaphore_wait(barrier, count - 1 - me)
+
+    def copies(k, source, target):
+        return [
+            pltpu.make_async_remote_copy(
+                src_ref=mine,
+                dst_ref=whole.at[source],
+                send_sem=send_sems.at[k - 1, part],
+                recv_sem=recv_sems.at[k - 1, part],
+                device_id={"ctx": target},
+                device_id_type=MESH,
+            )
+            for part, (mine, whole) in enumerate(((ends_ref, all_ends), (total_ref, all_totals)))
+        ]
+
+    for k in range(1, count):
+
+        @pl.when(me + k < count)
+        def _():
+            for copy in copies(k, me, me + k):
+                copy.start()
+
+    for k in range(1, count):
+
+        @pl.when(me >= k)
+        def _():
+            for copy in copies(k, me - k, me):
+                copy.wait_recv()
+
+        @pl.when(me + k < count)
+        def _():
+            for copy in copies(k, me, me + k):
+                copy.wait_send()
+
+
+def exchange(count, ends, total):
+    return pl.pallas_call(
+        functools.partial(exchange_kernel, count),
+        out_shape=(
+            jax.ShapeDtypeStruct((count,) + ends.shape, ends.dtype),
+            jax.ShapeDtypeStruct((count,) + total.shape, total.dtype),
+        ),
+        in_specs=[pl.BlockSpec(memory_space=pltpu.VMEM)] * 2,
+        out_specs=(pl.BlockSpec(memory_space=pltpu.VMEM),) * 2,
+        scratch_shapes=[
+            pltpu.SemaphoreType.DMA((count - 1, 2)),
+            pltpu.SemaphoreType.DMA((count - 1, 2)),
+        ],
+        compiler_params=pltpu.CompilerParams(collective_id=1, has_side_effects=True),
+        name="state_exchange",
+    )(ends, total)
+
+
+PIECES = 20
+
+
+def gather_kernel(by_columns, block_ref, out_ref, send_sems, recv_sems, own_sem):
+    me = lax.axis_index("ctx")
+    place = (me // SIDE, me % SIDE)
+    rows, columns = block_ref.shape
+    half, quarter = rows // 2, rows // 4
+
+    def index(half_number, first, second):
+        a = lax.rem(place[half_number] + first + 2 * SIDE, SIDE)
+        b = lax.rem(place[1 - half_number] + second + 2 * SIDE, SIDE)
+        return a * SIDE + b if half_number == 0 else b * SIDE + a
+
+    def window(owner, start, size):
+        if by_columns:
+            return out_ref.at[pl.ds(start, size), pl.ds(pl.multiple_of(owner * columns, columns), columns)]
+        return out_ref.at[pl.ds(pl.multiple_of(owner * rows + start, 16), size), :]
+
+    def copy(number, sem, owner, start, size, target, own=False):
+        return pltpu.make_async_remote_copy(
+            src_ref=block_ref.at[pl.ds(start, size), :] if own else window(owner, start, size),
+            dst_ref=window(owner, start, size),
+            send_sem=send_sems.at[number, sem],
+            recv_sem=recv_sems.at[number, sem],
+            device_id={"ctx": target},
+            device_id_type=MESH,
+        )
+
+    barrier = pltpu.get_barrier_semaphore()
+    for first, second in ((1, 0), (-1, 0), (0, 1), (0, -1)):
+        pl.semaphore_signal(
+            barrier, inc=1, device_id={"ctx": index(0, first, second)}, device_id_type=MESH
+        )
+    pl.semaphore_wait(barrier, 4)
+    own_copy = pltpu.make_async_copy(block_ref, window(me, 0, rows), own_sem)
+    own_copy.start()
+
+    RING = {(-1, None): 0, (1, None): 1, (2, 0): 2, (2, 1): 3}
+    LINE = {0: 4, -1: 8, 1: 12, 2: 16}
+    sent = []
+
+    def span(number, part):
+        start = number * half
+        return (start, half) if part is None else (start + part * quarter, quarter)
+
+    def send(number, sem, first, second, part, towards, own=False):
+        one = copy(
+            number, sem, index(number, first, second), *span(number, part),
+            index(number, *towards), own,
+        )
+        one.start()
+        sent.append(one)
+
+    def arrived(number, sem, first, second, part):
+        copy(number, sem, index(number, first, second), *span(number, part), me).wait_recv()
+
+    def send_line(number, first, own=False):
+        send(number, LINE[first] + RING[-1, None], first, 0, None, (0, 1), own)
+        send(number, LINE[first] + RING[1, None], first, 0, None, (0, -1), own)
+
+    def pass_on(number, first):
+        arrived(number, LINE[first] + 0, first, -1, None)
+        send(number, LINE[first] + 2, first, -1, 0, (0, 1))
+        arrived(number, LINE[first] + 1, first, 1, None)
+        send(number, LINE[first] + 3, first, 1, 1, (0, -1))
+
+    for number in (0, 1):
+        send(number, RING[-1, None], 0, 0, None, (1, 0), True)
+        send(number, RING[1, None], 0, 0, None, (-1, 0), True)
+    for number in (0, 1):
+        send_line(number, 0, True)
+    for number in (0, 1):
+        arrived(number, 0, -1, 0, None)
+        send(number, RING[2, 0], -1, 0, 0, (1, 0))
+        arrived(number, 1, 1, 0, None)
+        send(number, RING[2, 1], 1, 0, 1, (-1, 0))
+    for number in (0, 1):
+        send_line(number, -1)
+        send_line(number, 1)
+    for number in (0, 1):
+        pass_on(number, 0)
+    for number in (0, 1):
+        arrived(number, 2, 2, 0, 0)
+        arrived(number, 3, 2, 0, 1)
+        send_line(number, 2)
+    for first in (-1, 1, 2):
+        for number in (0, 1):
+            pass_on(number, first)
+    for first in (0, -1, 1, 2):
+        for number in (0, 1):
+            arrived(number, LINE[first] + 2, first, 2, 0)
+            arrived(number, LINE[first] + 3, first, 2, 1)
+    for one in sent:
+        one.wait_send()
+    own_copy.wait()
+
+
+def gather(block, by_columns, collective_id):
+    rows, columns = block.shape
+    count = SIDE * SIDE
+    shape = (rows, count * columns) if by_columns else (count * rows, columns)
+    return pl.pallas_call(
+        functools.partial(gather_kernel, by_columns),
+        out_shape=jax.ShapeDtypeStruct(shape, block.dtype),
+        in_specs=[pl.BlockSpec(memory_space=pl.ANY)],
+        out_specs=pl.BlockSpec(memory_space=pl.ANY),
+        scratch_shapes=[
+            pltpu.SemaphoreType.DMA((2, PIECES)),
+            pltpu.SemaphoreType.DMA((2, PIECES)),
+            pltpu.SemaphoreType.DMA,
+        ],
+        compiler_params=pltpu.CompilerParams(
+            collective_id=collective_id, has_side_effects=True
+        ),
+        name="gather_columns" if by_columns else "gather_rows",
+    )(block)
 
 
 def from_behind(array, axis, by):
@@ -39,60 +324,89 @@
     leading = lax.axis_index("ctx") == 0
     rim_rows = from_behind(mixer_in[tokens - width :], "ctx", 1)
     rim_rows = jnp.where(leading, prefix_tail, rim_rows)
-    padded = jnp.concatenate([rim_rows, mixer_in], axis=0).astype(jnp.float32)
-    convolved = conv_bias[None, :] + sum(
-        (
-            conv_kernel[tap_index][None, :] * padded[tap_index : tap_index + tokens]
-            for tap_index in range(width + 1)
-        )
-    )
-    conv_act = jax.nn.silu(convolved)
-    step_size = jax.nn.softplus(delta_in.astype(jnp.float32) + delta_bias[None, :])
-    decay_rate = -jnp.exp(decay_log)
-    driving = step_size * conv_act
-    b_rows = b_proj.T
-    c_rows = c_proj.T
-    group_len = 8
-    group_count = tokens // group_len
-
-    def advance(carry_state, inputs):
-        step_group, drive_group, b_group, c_group = inputs
-        outputs = []
-        for offset in range(group_len):
-            carry_state = (
-                jnp.exp(step_group[offset][None, :] * decay_rate) * carry_state
-                + b_group[offset][:, None] * drive_group[offset][None, :]
-            )
-            outputs.append(jnp.sum(c_group[offset][:, None] * carry_state, axis=0))
-        return (carry_state, jnp.stack(outputs))
-
-    local_end, local_out = lax.scan(
-        advance,
-        jnp.zeros_like(prefix_state),
-        (
-            step_size.reshape(group_count, group_len, -1),
-            driving.reshape(group_count, group_len, -1),
-            b_rows.reshape(group_count, group_len, -1),
-            c_rows.reshape(group_count, group_len, -1),
+    rim = jnp.concatenate(
+        [jnp.zeros((8 - width, rim_rows.shape[1]), jnp.float32), rim_rows.astype(jnp.float32)]
+    )
+    channels = mixer_in.shape[1]
+    b_wide = jnp.broadcast_to(b_proj.T[:, :, None], (tokens, STATES, LANES))
+    c_wide = jnp.broadcast_to(c_proj.T[:, :, None], (tokens, STATES, LANES))
+    f32 = functools.partial(jax.ShapeDtypeStruct, dtype=jnp.float32)
+    strips = (channels // STRIP,)
+    limit = pltpu.CompilerParams(vmem_limit_bytes=32 * 1024 * 1024)
+    conv_act, step_size, total, local_end = pl.pallas_call(
+        prepare_kernel,
+        grid=strips,
+        out_shape=(
+            f32((tokens, channels)),
+            f32((tokens, channels)),
+            f32((1, channels)),
+            jax.ShapeDtypeStruct((STATES, channels), jnp.bfloat16),
         ),
-    )
-    local_out = local_out.reshape(tokens, -1)
-    elapsed = jnp.cumsum(step_size, axis=0)
-    through = jnp.exp(decay_rate * elapsed[tokens - 1][None, :])
-
-    def relay_step(step_number, entry_state):
-        passed = from_behind(
-            (through * entry_state + local_end).astype(jnp.bfloat16), "ctx", 1
-        ).astype(jnp.float32)
-        return jnp.where(leading, prefix_state, passed)
-
-    entry_state = lax.fori_loop(0, lax.axis_size("ctx") - 1, relay_step, prefix_state)
-    carried = jnp.exp(decay_rate[None, :, :] * elapsed[:, None, :]) * entry_state[None, :, :]
-    mixed_out = (
-        local_out + jnp.sum(c_rows[:, :, None] * carried, axis=1) + skip_gain[None, :] * conv_act
-    )
-    gated_rows = (mixed_out * jax.nn.silu(gate_in.astype(jnp.float32))).astype(jnp.bfloat16)
-    gathered = lax.all_gather(gated_rows, "ctx", axis=0, tiled=True)
+        in_specs=[
+            strip_spec(8),
+            strip_spec(tokens),
+            strip_spec(tokens),
+            strip_spec(4),
+            strip_spec(1),
+            strip_spec(1),
+            strip_spec(STATES),
+            whole_spec((tokens, STATES, LANES)),
+        ],
+        out_specs=(
+            strip_spec(tokens),
+            strip_spec(tokens),
+            strip_spec(1),
+            strip_spec(STATES),
+        ),
+        scratch_shapes=[
+            pltpu.VMEM((8 + tokens, STRIP), jnp.float32),
+            pltpu.VMEM((tokens, STRIP), jnp.float32),
+        ],
+        compiler_params=limit,
+        name="prepare",
+    )(
+        rim, mixer_in, delta_in, conv_kernel, conv_bias[None], delta_bias[None], decay_log, b_wide
+    )
+    count = lax.axis_size("ctx")
+    all_ends, all_totals = exchange(count, local_end, total.reshape(channels // LANES, LANES))
+    gated_rows = pl.pallas_call(
+        scan_kernel,
+        grid=strips,
+        out_shape=jax.ShapeDtypeStruct((tokens, channels), jnp.bfloat16),
+        in_specs=[
+            pl.BlockSpec(memory_space=pltpu.SMEM),
+            strip_spec(tokens),
+            strip_spec(tokens),
+            strip_spec(tokens),
+            strip_spec(STATES),
+            strip_spec(STATES),
+            strip_spec(1),
+            whole_spec((tokens, STATES, LANES)),
+            whole_spec((tokens, STATES, LANES)),
+            pl.BlockSpec((count, 1, STRIP), lambda i: (0, 0, i)),
+            pl.BlockSpec((count, STATES, STRIP), lambda i: (0, 0, i)),
+        ],
+        out_specs=strip_spec(tokens),
+        scratch_shapes=[
+            pltpu.VMEM((tokens, STRIP), jnp.float32),
+            pltpu.VMEM((tokens, STRIP), jnp.float32),
+        ],
+        compiler_params=limit,
+        name="scan",
+    )(
+        lax.axis_index("ctx").reshape(1),
+        conv_act,
+        step_size,
+        gate_in,
+        decay_log,
+        prefix_state,
+        skip_gain[None],
+        b_wide,
+        c_wide,
+        all_totals.reshape(count, 1, channels),
+        all_ends,
+    )
+    gathered = gather(gated_rows, False, 2)
     block_rows = residual.shape[0]
     projected = lax.psum_scatter(
         jnp.dot(
@@ -106,7 +420,9 @@
     ).astype(jnp.float32)
     mixer_out = (residual.astype(jnp.float32) + projected).astype(jnp.bfloat16)
     mixer_wide = mixer_out.astype(jnp.float32)
-    squares = lax.psum(jnp.sum(mixer_wide * mixer_wide, axis=1), "ctx")
+    squares = jnp.sum(
+        lax.all_gather(jnp.sum(mixer_wide * mixer_wide, axis=1), "ctx", axis=0), axis=0
+    )
     norm_scale = lax.rsqrt(squares / D + 1e-05)
     normed = (mixer_wide * norm_scale[:, None] * norm_gain[None, :]).astype(jnp.bfloat16)
     experts = expert_gate.shape[0] * lax.axis_size("exp")
@@ -130,7 +446,7 @@
     ).astype(jnp.bfloat16)
     received = lax.all_to_all(outgoing, "exp", split_axis=0, concat_axis=0, tiled=True)
     arrived = received.reshape(slot_total, -1)
-    piece_rows = lax.all_gather(arrived, "ctx", axis=1, tiled=True)
+    piece_rows = gather(arrived, True, 3)
     feature_count = piece_rows.shape[1]
     gate_rows = lax.slice_in_dim(expert_gate[0], 0, feature_count, axis=0)
     up_rows = lax.slice_in_dim(expert_up[0], 0, feature_count, axis=0)

time: 634 us -> 421 us (0.66)
  waiting for transfers between devices: 349 us -> 134 us
  Pallas kernels: 0 us -> 150 us
  starting transfers between devices: 84.8 us -> 9.38 us
  other arithmetic: 31.5 us -> 3.63 us
  local copies, waits for them, and re-layouts: 45.9 us -> 21.4 us
  blocking collectives: 59.4 us -> 42.3 us
    all_gather x2 -> x0, waiting for transfers between devices: 193 us -> none  [the longest x1 99.6 us: shards(): gathered = lax.all_gather(gated_rows, 'ctx', axis=0, tiled=True)]
    pallas_call x0 -> x5, Pallas kernels: none -> 150 us  [the longest x2 118 us: gather(): pl.pallas_call(functools.partial(gather_kernel, by_columns), out_shape=ja...]
    ppermute x16 -> x1, starting transfers between devices: 79.2 us -> 4.03 us  [from_behind(): return lax.ppermute(array, axis, pairs)]
    psum x1 -> x0, blocking collectives: 33.5 us -> none  [shards(): squares = lax.psum(jnp.sum(mixer_wide * mixer_wide, axis=1), 'ctx')]
    slice x19 -> x1, local copies, waits for them, and re-layouts: 29.4 us -> 0.21 us  [the longest x16 27.4 us: advance(): drive_group[offset][None, :]]
    ppermute x16 -> x1, waiting for transfers between devices: 20.8 us -> 0.01 us  [from_behind(): return lax.ppermute(array, axis, pairs)]
    all_gather x0 -> x1, blocking collectives: none -> 18 us  [shards(): lax.all_gather(jnp.sum(mixer_wide * mixer_wide, axis=1), 'ctx', axis=0)]
    reduce_sum x50 -> x2, other arithmetic: 18.8 us -> 1.16 us  [the longest x1 1.12 us: shards(): jnp.sum(mixer_wide * mixer_wide, axis=1)]
  transfers between devices with their start and end apart: 21 -> 4, of which waited for: 20 -> 3; matrix products, arithmetic and copies ran while one was open for 1% -> 1% of each run, Pallas kernels for 0% -> 0%
where the time goes in v1:
time: 421 us; the launch traced here: 420 us
  Pallas kernels  150 us (36%)
  waiting for transfers between devices  134 us (32%)
  matrix products  45.2 us (11%)
  blocking collectives  42.3 us (10%)
  local copies, waits for them, and re-layouts  21.4 us (5%)
  between operations  14.3 us (3%)
  starting transfers between devices  9.38 us (2%)
    pallas_call x2, Pallas kernels, gather(): pl.pallas_call(functools.partial(gather_kernel, by_columns), out_shape=ja...  118 us
    reduce_scatter x1, waiting for transfers between devices, shards(): lax.psum_scatter(partial_value.astype(jnp.bfloat16), 'ctx', scatter_dimen...  92.8 us
    reduce_scatter x1, waiting for transfers between devices, shards(): lax.psum_scatter(jnp.dot(lax.slice_in_dim(gathered, 0, lax.axis_size('exp...  28.9 us
    all_to_all x1, blocking collectives, shards(): lax.all_to_all(outgoing, 'exp', split_axis=0, concat_axis=0, tiled=True)  24.4 us
    pallas_call x1, Pallas kernels, exchange(): pl.pallas_call(functools.partial(exchange_kernel, count), out_shape=(jax....  19.8 us
    all_gather x1, blocking collectives, shards(): lax.all_gather(jnp.sum(mixer_wide * mixer_wide, axis=1), 'ctx', axis=0)  18 us
    unnamed x55, local copies, waits for them, and re-layouts  17.5 us
    dot_general x1, matrix products, shards(): jnp.dot(hidden, expert_down[0], preferred_element_type=jnp.float32)  12.3 us
  transfers between devices with their start and end apart: 4, of which 3 were waited for; matrix products, arithmetic and copies ran while one was open for 1% of the time, Pallas kernels for 0%

profile of v1, /device:TPU:1, one launch (start us, length us, event | category | flops | bytes accessed | tf_op | source)
XLA Modules:
  0.0 420.3 jit_solution(11394899510773283218)
XLA Ops:
  7.2 0.9 slice.9
  8.1 4.0 collective-permute-start
  12.2 0.8 copy.38
  13.0 0.8 copy.39
  13.8 0.7 broadcast_select_fusion
  14.6 0.3 broadcast_in_dim.12.b_ref
  14.9 1.0 copy-done.8
  15.9 0.9 copy-done.9
  16.8 1.0 copy-done.11
  17.9 0.8 copy-done.16
  18.6 0.7 copy-done.17
  19.3 0.7 copy-done.18
  20.0 5.3 %prepare.1 = (f32[128,2048]{1,0:T(8,128)S(1)}, f32[128,2048]{1,0:T(8,128)S(1)}, f32[1,2048]{1,0:T(1,128)S(1)}, bf16[16,2048]{1,0:T(8,128)(2,1)S(1)}) custom-call(f32[8,2048]{1,0:T(8,128)S(1)} %pad_convert_fusion.rim_ref, bf16[128,2048]{1,0:T(8,128)(2,1)S(1)} %copy-done.8, bf16[128,2048]{1,0:T(8,128)(2,1)S(1)} %copy-done.11, f32[4,2048]{1,0:T(4,128)S(1)} %copy-done.16, ...), custom_call_target="tpu_custom_call" | custom-call | tf_op jit(solution)/shard_map/prepare/pallas_call | solution.py:336
  25.4 1.0 copy-done.3
  26.3 1.0 copy-done.5
  27.3 0.6 copy-done.15
  28.0 0.6 copy-done.20
  28.6 19.8 %state_exchange.1 = (bf16[16,16,2048]{2,1,0:T(8,128)(2,1)}, f32[16,16,128]{2,1,0:T(8,128)}) custom-call(bf16[16,2048]{1,0:T(8,128)(2,1)} %copy-done.15, f32[16,128]{1,0:T(8,128)} %bitcast.53), custom_call_target="tpu_custom_call" | custom-call | tf_op jit(solution)/shard_map/state_exchange/pallas_call | solution.py:158
  48.4 0.3 broadcast_in_dim.14.c_ref
  48.8 1.2 copy-done.4
  50.0 1.2 copy-done.6
  51.2 1.2 copy-done.7
  52.4 0.9 copy-done.10
  53.3 1.0 copy-done.12
  54.4 0.9 copy-done.13
  55.3 0.9 copy-done.14
  56.2 0.7 copy-done.19
  56.9 7.3 %scan.1.block_ref = bf16[128,2048]{1,0:T(8,128)(2,1)S(1)} custom-call(s32[1]{0:T(128)} %bitcast.place_ref, f32[128,2048]{1,0:T(8,128)S(1)} %copy-done.4, f32[128,2048]{1,0:T(8,128)S(1)} %copy-done.6, bf16[128,2048]{1,0:T(8,128)(2,1)S(1)} %copy-done.12, f32[16,2048]{1,0:T(8,128)S(1)} %copy-done.10, f32[16,2048]{1,0:T(8,128)S(1)} %copy-done.13, ...), custom_call_target="tpu_custom_call" | custom-call | tf_op jit(solution)/shard_map/scan/pallas_call | solution.py:372
  64.2 0.8 copy-done.2
  65.1 51.1 %gather_rows.1 = bf16[2048,2048]{1,0:T(8,128)(2,1)} custom-call(bf16[128,2048]{1,0:T(8,128)(2,1)} %copy-done.2), custom_call_target="tpu_custom_call" | custom-call | tf_op jit(solution)/shard_map/gather_rows/pallas_call | solution.py:277
  116.2 9.2 %convolution_convert_fusion.1 = bf16[2048,512]{1,0:T(8,128)(2,1)} fusion(bf16[2048,2048]{1,0:T(8,128)(2,1)} %gather_rows.1, bf16[2048,512]{1,0:T(8,128)(2,1)S(1)} %copy-done), kind=kOutput, calls=%fused_computation.6 | convolution fusion | flops 4296015872 | bytes 12582912 | tf_op jit(solution)/shard_map/dot_general | solution.py:412
  125.9 1.1 reduce-window.6
  127.1 0.2 slice_reduce_fusion
  127.7 0.2 and_reduce_fusion
  127.9 28.9 %reduce-scatter.3.cloned.1.call-done = bf16[256,512]{1,0:T(8,128)(2,1)} async-done(((bf16[2048,512]{1,0:T(8,128)(2,1)}), bf16[256,512]{1,0:T(8,128)(2,1)}) %reduce-scatter.3.cloned.1.call-update) | async-done | bytes 262160 | tf_op jit(solution)/shard_map/reduce_scatter | solution.py:411
  156.8 1.1 fusion.14
  157.9 18.0 %all-gather.1 = f32[16,1,256]{2,1,0:T(1,128)S(1)} all-gather(f32[1,1,256]{2,1,0:T(1,128)S(1)} %bitcast.58), channel_id=2, replica_groups=mesh['ctx'=16,'exp'=8] {'ctx'}, dimensions={0}, use_global_device_ids=true | all-gather | bytes 17408 | tf_op jit(solution)/shard_map/all_gather | solution.py:424
  175.9 0.5 convolution_convert_fusion.2
  176.4 24.4 %all_to_all.10 = bf16[8,96,512]{2,1,0:T(8,128)(2,1)} all-to-all(bf16[8,96,512]{2,1,0:T(8,128)(2,1)S(1)} %convolution_convert_fusion.2), channel_id=1, replica_groups=mesh['ctx'=16,'exp'=8] {'exp'}, dimensions={0} | all-to-all | bytes 1572864 | tf_op jit(solution)/shard_map/all_to_all | solution.py:447
  200.8 66.7 %gather_columns.1 = bf16[768,8192]{1,0:T(8,128)(2,1)} custom-call(bf16[768,512]{1,0:T(8,128)(2,1)} %bitcast.54), custom_call_target="tpu_custom_call" | custom-call | tf_op jit(solution)/shard_map/gather_columns/pallas_call | solution.py:277
  267.5 12.0 %fusion.3 = f32[768,384]{1,0:T(8,128)S(1)} fusion(bf16[768,8192]{1,0:T(8,128)(2,1)} %gather_columns.1, bf16[1,8192,384]{2,1,0:T(8,128)(2,1)} %param.35), kind=kOutput, calls=%fused_computation.4 | convolution fusion | flops 4831838208 | bytes 20054016 | tf_op jit(solution)/shard_map/dot_general | solution.py:453
  279.5 9.2 %fusion.9 = bf16[768,384]{1,0:T(8,128)(2,1)S(1)} fusion(bf16[768,8192]{1,0:T(8,128)(2,1)S(1)} %copy-done.21, bf16[1,8192,384]{2,1,0:T(8,128)(2,1)} %param.36, f32[768,384]{1,0:T(8,128)S(1)} %fusion.3), kind=kOutput, calls=%fused_computation.12 | convolution fusion | flops 4833607680 | bytes 20643840 | tf_op jit(solution)/shard_map/dot_general | solution.py:454
  288.7 12.3 %convolution_convert_fusion = bf16[768,8192]{1,0:T(8,128)(2,1)} fusion(bf16[768,384]{1,0:T(8,128)(2,1)S(1)} %fusion.9, bf16[1,384,8192]{2,1,0:T(8,128)(2,1)} %param.37), kind=kOutput, calls=%fused_computation | convolution fusion | flops 4838129664 | bytes 19464192 | tf_op jit(solution)/shard_map/dot_general | solution.py:456
  301.0 92.8 %reduce-scatter.5.cloned.1.call-done = bf16[768,512]{1,0:T(8,128)(2,1)} async-done(((bf16[768,8192]{1,0:T(8,128)(2,1)}), bf16[768,512]{1,0:T(8,128)(2,1)}) %reduce-scatter.5.cloned.1.call-update) | async-done | bytes 786448 | tf_op jit(solution)/shard_map/reduce_scatter | solution.py:457
  393.8 5.3 %all-to-all-start.1 = ((bf16[8,96,512]{2,1,0:T(8,128)(2,1)}), bf16[8,96,512]{2,1,0:T(8,128)(2,1)S(1)}, u32[]{:S(2)}, u32[]{:S(2)}) async-start(bf16[8,96,512]{2,1,0:T(8,128)(2,1)} %bitcast.55), calls=%async_computation.3 | async-start | bytes 1572864 | tf_op jit(solution)/shard_map/all_to_all | solution.py:461
  399.1 0.2 fusion.5
  399.3 12.1 %all-to-all-done.1 = bf16[8,96,512]{2,1,0:T(8,128)(2,1)S(1)} async-done(((bf16[8,96,512]{2,1,0:T(8,128)(2,1)}), bf16[8,96,512]{2,1,0:T(8,128)(2,1)S(1)}, u32[]{:S(2)}, u32[]{:S(2)}) %all-to-all-start.1) | async-done | bytes 786464 | tf_op jit(solution)/shard_map/all_to_all | solution.py:461
  411.4 2.0 fusion.13
  (54 shorter events, 1.1 us)
Async XLA Ops:
  7.2 109.0 %copy-start = (bf16[2048,512]{1,0:T(8,128)(2,1)S(1)}, bf16[2048,512]{1,0:T(8,128)(2,1)}, u32[]{:S(2)}) copy-start(bf16[2048,512]{1,0:T(8,128)(2,1)} %param.32) | copy-start | bytes 6291460
  7.2 149.6 %reduce-scatter.3.cloned.1.call-start = ((), (), s32[]{:S(2)}) async-start(), calls=%async_computation.4 | async-start | bytes 2359296 | tf_op jit(solution)/shard_map/reduce_scatter | solution.py:411
  8.1 5.6 %collective-permute-start = (bf16[3,2048]{1,0:T(4,128)(2,1)S(1)}, bf16[3,2048]{1,0:T(4,128)(2,1)S(1)}, u32[]{:S(2)}, u32[]{:S(2)}) collective-permute-start(bf16[3,2048]{1,0:T(4,128)(2,1)S(1)} %slice.9), channel_id=1, source_target_pairs={{0,8},{8,16},{16,24},{24,32},{32,40},{40,48},{48,56},{56,64},{64,7... | collective-permute-start | bytes 36872 | tf_op jit(solution)/shard_map/ppermute | solution.py:297
  14.9 1.0 copy-start.8
  15.9 0.9 copy-start.9
  16.8 1.0 copy-start.11
  17.9 0.8 copy-start.16
  18.6 0.7 copy-start.17
  19.3 0.7 copy-start.18
  25.4 1.0 copy-start.3
  26.3 1.0 copy-start.5
  27.3 0.6 copy-start.15
  28.0 0.6 copy-start.20
  48.8 1.2 copy-start.4
  50.0 1.2 copy-start.6
  51.2 1.2 copy-start.7
  52.4 0.9 copy-start.10
  53.3 1.0 copy-start.12
  54.4 0.9 copy-start.13
  55.3 0.9 copy-start.14
  56.2 0.7 copy-start.19
  64.2 0.8 copy-start.2
  116.2 9.3 %copy-start.24 = (s32[256,2]{0,1:T(2,128)S(1)}, s32[256,2]{0,1:T(2,128)}, u32[]{:S(2)}) copy-start(s32[256,2]{0,1:T(2,128)} %param.38) | copy-start | bytes 6148
  116.2 40.6 %copy-start.22 = (bf16[256,512]{1,0:T(8,128)(2,1)S(1)}, bf16[256,512]{1,0:T(8,128)(2,1)}, u32[]{:S(2)}) copy-start(bf16[256,512]{1,0:T(8,128)(2,1)} %param.33) | copy-start | bytes 786436
  116.2 59.7 %copy-start.26 = (f32[512]{0:T(512)S(1)}, f32[512]{0:T(512)}, u32[]{:S(2)}) copy-start(f32[512]{0:T(512)} %param.34) | copy-start | bytes 6148
  125.4 268.4 %reduce-scatter.5.cloned.1.call-start = ((), (), s32[]{:S(2)}) async-start(), calls=%async_computation.5 | async-start | bytes 13369344 | tf_op jit(solution)/shard_map/reduce_scatter | solution.py:457
  157.9 109.6 %copy-start.23 = (bf16[256,512]{1,0:T(8,128)(2,1)}, bf16[256,512]{1,0:T(8,128)(2,1)S(1)}, u32[]{:S(2)}) copy-start(bf16[256,512]{1,0:T(8,128)(2,1)S(1)} %get-tuple-element.15) | copy-start | bytes 786436
  267.4 12.0 %copy-start.21 = (bf16[768,8192]{1,0:T(8,128)(2,1)S(1)}, bf16[768,8192]{1,0:T(8,128)(2,1)}, u32[]{:S(2)}) copy-start(bf16[768,8192]{1,0:T(8,128)(2,1)} %gather_columns.1) | copy-start | bytes 37748740
  301.0 112.4 %copy-start.1 = (bf16[2048,512]{1,0:T(8,128)(2,1)S(1)}, bf16[2048,512]{1,0:T(8,128)(2,1)}, u32[]{:S(2)}) copy-start(bf16[2048,512]{1,0:T(8,128)(2,1)} %param.32) | copy-start | bytes 6291460
  301.0 98.1 %copy-start.25 = (f32[256,2]{0,1:T(2,128)S(1)}, f32[256,2]{0,1:T(2,128)}, u32[]{:S(2)}) copy-start(f32[256,2]{0,1:T(2,128)} %param.39) | copy-start | bytes 6148
  393.8 17.6 %all-to-all-start.1 = ((bf16[8,96,512]{2,1,0:T(8,128)(2,1)}), bf16[8,96,512]{2,1,0:T(8,128)(2,1)S(1)}, u32[]{:S(2)}, u32[]{:S(2)}) async-start(bf16[8,96,512]{2,1,0:T(8,128)(2,1)} %bitcast.55), calls=%async_computation.3 | async-start | bytes 1572864 | tf_op jit(solution)/shard_map/all_to_all | solution.py:461
Sparse Core Ops, SparseCore 0:
  125.5 31.1 reduce-scatter.2
  301.2 92.6 reduce-scatter.4

commit v2 on v1

--- a/solution.py
+++ b/solution.py
@@ -289,6 +289,431 @@
         ),
         name="gather_columns" if by_columns else "gather_rows",
     )(block)
+
+
+EXPERTS = 8
+FORWARD = ((-1, None), (1, None), (2, 0), (2, 1))
+LINES = {0: 0, -1: 1, 1: 2, 2: 3}
+RING = 4
+
+
+class Torus:
+    def __init__(self):
+        me = lax.axis_index("ctx")
+        self.me = me
+        self.place = (me // SIDE, me % SIDE)
+
+    def index(self, half, first, second):
+        a = lax.rem(self.place[half] + first + 2 * SIDE, SIDE)
+        b = lax.rem(self.place[1 - half] + second + 2 * SIDE, SIDE)
+        return a * SIDE + b if half == 0 else b * SIDE + a
+
+
+def span(rows, half, part=None):
+    start = half * (rows // 2)
+    return (start, rows // 2) if part is None else (start + part * (rows // 4), rows // 4)
+
+
+def expert_kernel(
+    capacity, features,
+    mixer_ref, squares_ref, pick_ref, place_ref, route_ref, gain_ref, gate_ref, up_ref, down_ref,
+    out_ref,
+    blocks, landed, wide, down, total, hidden, outgoing, answer, returned, all_squares,
+    square_sems, dispatch_sems, return_sems, gather_sems, sum_sems, weight_sems,
+):
+    torus = Torus()
+    me, index = torus.me, torus.index
+    own_expert = lax.axis_index("exp")
+    slots, width = answer.shape
+    units = down.shape[0]
+    count = SIDE * SIDE
+
+    weights = [
+        pltpu.make_async_copy(gate_ref.at[0], wide.at[:, pl.ds(0, units)], weight_sems.at[0]),
+        pltpu.make_async_copy(up_ref.at[0], wide.at[:, pl.ds(units, units)], weight_sems.at[1]),
+        pltpu.make_async_copy(down_ref.at[0], down, weight_sems.at[2]),
+    ]
+    for one in weights:
+        one.start()
+
+    barrier = pltpu.get_barrier_semaphore()
+    for k in range(1, count):
+        pl.semaphore_signal(
+            barrier, inc=1, device_id={"ctx": lax.rem(me + k, count)}, device_id_type=MESH
+        )
+    for k in range(1, EXPERTS):
+        pl.semaphore_signal(
+            barrier, inc=1, device_id={"exp": lax.rem(own_expert + k, EXPERTS)}, device_id_type=MESH
+        )
+    pl.semaphore_wait(barrier, count - 1 + EXPERTS - 1)
+
+    square_copies = []
+    for k in range(1, count):
+        square_copies.append(
+            pltpu.make_async_remote_copy(
+                src_ref=squares_ref,
+                dst_ref=all_squares.at[me],
+                send_sem=square_sems.at[0, k - 1],
+                recv_sem=square_sems.at[1, k - 1],
+                device_id={"ctx": lax.rem(me + k, count)},
+                device_id_type=MESH,
+            )
+        )
+        square_copies[-1].start()
+    all_squares[me] = squares_ref[...]
+    for k in range(1, count):
+        source = lax.rem(me + count - k, count)
+        pltpu.make_async_remote_copy(
+            src_ref=squares_ref,
+            dst_ref=all_squares.at[source],
+            send_sem=square_sems.at[0, k - 1],
+            recv_sem=square_sems.at[1, k - 1],
+            device_id={"ctx": me},
+            device_id_type=MESH,
+        ).wait_recv()
+    scale = lax.rsqrt(jnp.sum(all_squares[...], axis=0) / features + 1e-05)
+
+    def pick(chunk, carry):
+        rows = pl.ds(pl.multiple_of(chunk * capacity, 16), capacity)
+        chosen = pick_ref[rows, :]
+        picked = jnp.dot(chosen, mixer_ref[...], preferred_element_type=jnp.float32)
+        chosen = chosen.astype(jnp.float32)
+        row_scale = sum(
+            jnp.sum(
+                chosen[:, k * LANES : (k + 1) * LANES] * scale[k : k + 1], axis=1, keepdims=True
+            )
+            for k in range(chosen.shape[1] // LANES)
+        )
+        outgoing[rows, :] = (picked * row_scale * gain_ref[...]).astype(outgoing.dtype)
+        return carry
+
+    lax.fori_loop(0, EXPERTS, pick, 0)
+
+    def expert_rows(expert):
+        return pl.ds(pl.multiple_of(expert * capacity, 16), capacity)
+
+    def across(sems, source, target_ref):
+        started = []
+        for k in range(1, EXPERTS):
+            peer = lax.rem(own_expert + k, EXPERTS)
+            started.append(
+                pltpu.make_async_remote_copy(
+                    src_ref=source.at[expert_rows(peer), :],
+                    dst_ref=target_ref.at[expert_rows(own_expert), :],
+                    send_sem=sems.at[0, k - 1],
+                    recv_sem=sems.at[1, k - 1],
+                    device_id={"exp": peer},
+                    device_id_type=MESH,
+                )
+            )
+            started[-1].start()
+        target_ref[expert_rows(own_expert), :] = source[expert_rows(own_expert), :]
+        for k in range(1, EXPERTS):
+            origin = lax.rem(own_expert + EXPERTS - k, EXPERTS)
+            pltpu.make_async_remote_copy(
+                src_ref=source.at[expert_rows(origin), :],
+                dst_ref=target_ref.at[expert_rows(origin), :],
+                send_sem=sems.at[0, k - 1],
+                recv_sem=sems.at[1, k - 1],
+                device_id={"exp": own_expert},
+                device_id_type=MESH,
+            ).wait_recv()
+        return started
+
+    crossing = across(dispatch_sems, outgoing, blocks.at[me])
+
+    in_flight = {}
+
+    def moved(half, line, kind, first, second, part, target):
+        start, size = span(slots, half, part)
+        ref = blocks.at[index(half, first, second), pl.ds(start, size), :]
+        return pltpu.make_async_remote_copy(
+            src_ref=ref,
+            dst_ref=ref,
+            send_sem=gather_sems.at[0, half, line, kind],
+            recv_sem=gather_sems.at[1, half, line, kind],
+            device_id={"ctx": target},
+            device_id_type=MESH,
+        )
+
+    def send(half, line, kind, first, second, part, towards):
+        one = moved(half, line, kind, first, second, part, index(half, *towards))
+        one.start()
+        where = (first, second) if half == 0 else (second, first)
+        in_flight.setdefault(where, []).append(one)
+
+    def arrived(half, line, kind, first, second, part):
+        moved(half, line, kind, first, second, part, me).wait_recv()
+
+    def send_line(half, first):
+        send(half, LINES[first], 0, first, 0, None, (0, 1))
+        send(half, LINES[first], 1, first, 0, None, (0, -1))
+
+    def pass_on(half, first):
+        arrived(half, LINES[first], 0, first, -1, None)
+        send(half, LINES[first], 2, first, -1, 0, (0, 1))
+        arrived(half, LINES[first], 1, first, 1, None)
+        send(half, LINES[first], 3, first, 1, 1, (0, -1))
+
+    def last_of(half, first):
+        arrived(half, LINES[first], 2, first, 2, 0)
+        arrived(half, LINES[first], 3, first, 2, 1)
+
+    row_tile = slots // 2
+
+    def over_blocks(where, number, body):
+        def one(step, carry):
+            block, tile = step // 2, step % 2
+            dx, dy = where(block)
+            owner = index(0, dx, dy)
+            body(owner, pl.ds(pl.multiple_of(tile * row_tile, 16), row_tile))
+            return carry
+
+        lax.fori_loop(0, number * 2, one, 0)
+
+    def grow(owner, rows):
+        part = wide[pl.ds(pl.multiple_of(owner * width, 16), width), :]
+        total[rows, :] += jnp.dot(blocks[owner, rows, :], part, preferred_element_type=jnp.float32)
+
+    def sign(i):
+        return 1 - 2 * (i % 2)
+
+    def beside(i):
+        return sign(i) * (1 - i // 2), sign(i) * (i // 2)
+
+    def corner(i):
+        return sign(i), 1 - 2 * (i // 2)
+
+    def knight(i):
+        along = i // 2
+        return sign(i) * (1 - along) + 2 * along, 2 * (1 - along) + sign(i) * along
+
+    def across_ring(i):
+        return 2 * (1 - i), 2 * i
+
+    def single(dx, dy):
+        return lambda i: (dx, dy)
+
+    for half in (0, 1):
+        send(half, RING, 0, 0, 0, None, (1, 0))
+        send(half, RING, 1, 0, 0, None, (-1, 0))
+    for half in (0, 1):
+        send_line(half, 0)
+    total[...] = jnp.zeros_like(total)
+    for one in weights:
+        one.wait()
+    over_blocks(single(0, 0), 1, grow)
+    for half in (0, 1):
+        arrived(half, RING, 0, -1, 0, None)
+        send(half, RING, 2, -1, 0, 0, (1, 0))
+        arrived(half, RING, 1, 1, 0, None)
+        send(half, RING, 3, 1, 0, 1, (-1, 0))
+    for half in (0, 1):
+        send_line(half, -1)
+        send_line(half, 1)
+    for half in (0, 1):
+        pass_on(half, 0)
+    over_blocks(beside, 4, grow)
+    for half in (0, 1):
+        arrived(half, RING, 2, 2, 0, 0)
+        arrived(half, RING, 3, 2, 0, 1)
+        send_line(half, 2)
+    for half in (0, 1):
+        last_of(half, 0)
+    over_blocks(across_ring, 2, grow)
+    for first in (-1, 1):
+        for half in (0, 1):
+            pass_on(half, first)
+    over_blocks(corner, 4, grow)
+    for half in (0, 1):
+        pass_on(half, 2)
+    for first in (-1, 1):
+        for half in (0, 1):
+            last_of(half, first)
+    over_blocks(knight, 4, grow)
+    for half in (0, 1):
+        last_of(half, 2)
+    over_blocks(single(2, 2), 1, grow)
+
+    def activate(step, carry):
+        rows = pl.ds(pl.multiple_of(step * capacity, 16), capacity)
+        gate = total[rows, 0:units]
+        hidden[rows, :] = (gate / (1.0 + jnp.exp(-gate)) * total[rows, units : 2 * units]).astype(
+            hidden.dtype
+        )
+        return carry
+
+    lax.fori_loop(0, EXPERTS, activate, 0)
+
+    def project(owner, rows):
+        part = down[:, pl.ds(pl.multiple_of(owner * width, LANES), width)]
+        blocks[owner, rows, :] = jnp.dot(
+            hidden[rows, :], part, preferred_element_type=jnp.float32
+        ).astype(blocks.dtype)
+
+    def fill(places, where):
+        for place in places:
+            for one in in_flight.pop(place, ()):
+                one.wait_send()
+        over_blocks(where, len(places), project)
+
+    summing = []
+
+    def part_rows(half, part):
+        start, size = span(slots, half, part)
+        return pl.ds(start, size)
+
+    def landing(half, line, kind):
+        if kind < 2:
+            return landed.at[half, line, kind]
+        size = slots // 4
+        return landed.at[half, line, 2, pl.ds((kind - 2) * size, size), :]
+
+    def sum_copy(half, line, kind, first, second, part, target):
+        return pltpu.make_async_remote_copy(
+            src_ref=blocks.at[index(half, first, second), part_rows(half, part), :],
+            dst_ref=landing(half, line, kind),
+            send_sem=sum_sems.at[0, half, line, kind],
+            recv_sem=sum_sems.at[1, half, line, kind],
+            device_id={"ctx": target},
+            device_id_type=MESH,
+        )
+
+    def give(half, line, kind, first, second, part):
+        step = 1 if kind % 2 == 0 else -1
+        target = index(half, step, 0) if line == RING else index(half, 0, step)
+        one = sum_copy(half, line, kind, first, second, part, target)
+        one.start()
+        summing.append(one)
+
+    def taken(half, line, kind):
+        part = None if kind < 2 else kind - 2
+        sum_copy(half, line, kind, 0, 0, part, me).wait_recv()
+
+    def add(half, first, second, part, line, kinds, target=None):
+        for kind in kinds:
+            taken(half, line, kind)
+        start, size = span(slots, half, part)
+        owner = index(half, first, second)
+        tile = 96
+
+        def one(step, carry):
+            offset = pl.multiple_of(step * tile, 16)
+            rows = pl.ds(pl.multiple_of(start + offset, 16), tile)
+            value = blocks[owner, rows, :].astype(jnp.float32)
+            for kind in kinds:
+                value = value + landing(half, line, kind)[pl.ds(offset, tile), :].astype(jnp.float32)
+            value = value.astype(blocks.dtype)
+            if target is None:
+                blocks[owner, rows, :] = value
+            else:
+                target[rows, :] = value
+            return carry
+
+        lax.fori_loop(0, size // tile, one, 0)
+
+    def at(line, offset):
+        return (offset, 0) if line == RING else ({v: k for k, v in LINES.items()}[line], offset)
+
+    def begin(half, line):
+        give(half, line, 2, *at(line, 2), 0)
+        give(half, line, 3, *at(line, 2), 1)
+
+    def middle(half, line):
+        add(half, *at(line, 1), 0, line, (2,))
+        give(half, line, 0, *at(line, 1), None)
+        add(half, *at(line, -1), 1, line, (3,))
+        give(half, line, 1, *at(line, -1), None)
+
+    def finish(half, line, target=None):
+        add(half, *at(line, 0), None, line, (0, 1), target)
+
+    halves = (0, 1)
+    fill([(2, 2)], single(2, 2))
+    for half in halves:
+        begin(half, LINES[2])
+    fill([(1, 2), (-1, 2), (2, 1), (2, -1)], knight)
+    for first in (1, -1):
+        for half in halves:
+            begin(half, LINES[first])
+    fill([(2, 0), (0, 2)], across_ring)
+    for half in halves:
+        begin(half, LINES[0])
+    for half in halves:
+        middle(half, LINES[2])
+    fill([(1, 1), (-1, 1), (1, -1), (-1, -1)], corner)
+    for first in (1, -1):
+        for half in halves:
+            middle(half, LINES[first])
+    fill([(1, 0), (-1, 0), (0, 1), (0, -1)], beside)
+    for half in halves:
+        middle(half, LINES[0])
+    for one in crossing:
+        one.wait_send()
+    fill([(0, 0)], single(0, 0))
+    for half in halves:
+        finish(half, LINES[2])
+        begin(half, RING)
+    for first in (1, -1):
+        for half in halves:
+            finish(half, LINES[first])
+    for half in halves:
+        middle(half, RING)
+    for half in halves:
+        finish(half, LINES[0])
+    for half in halves:
+        finish(half, RING, answer)
+
+    back = across(return_sems, answer, returned)
+    rows = mixer_ref.shape[0]
+    value = mixer_ref[...].astype(jnp.float32)
+    for k in range(route_ref.shape[1]):
+        value = value + route_ref[:, k : k + 1] * jnp.dot(
+            place_ref[k], returned[...], preferred_element_type=jnp.float32
+        )
+    out_ref[...] = value.astype(out_ref.dtype)
+    for one in summing + back + square_copies:
+        one.wait_send()
+
+
+def expert_layer(
+    mixer_out, squares, pick, place, route_gates, gain, expert_gate, expert_up, expert_down, capacity
+):
+    rows, width = mixer_out.shape
+    features, units = expert_gate.shape[1:]
+    slots = EXPERTS * capacity
+    count = SIDE * SIDE
+    here = pl.BlockSpec(memory_space=pltpu.VMEM)
+    away = pl.BlockSpec(memory_space=pl.ANY)
+    bf16, f32 = jnp.bfloat16, jnp.float32
+    return pl.pallas_call(
+        functools.partial(expert_kernel, capacity, features),
+        out_shape=jax.ShapeDtypeStruct((rows, width), bf16),
+        in_specs=[here] * 6 + [away] * 3,
+        out_specs=here,
+        scratch_shapes=[
+            pltpu.VMEM((count, slots, width), bf16),
+            pltpu.VMEM((2, 5, 3, slots // 2, width), bf16),
+            pltpu.VMEM((features, 2 * units), bf16),
+            pltpu.VMEM((units, features), bf16),
+            pltpu.VMEM((slots, 2 * units), f32),
+            pltpu.VMEM((slots, units), bf16),
+            pltpu.VMEM((slots, width), bf16),
+            pltpu.VMEM((slots, width), bf16),
+            pltpu.VMEM((slots, width), bf16),
+            pltpu.VMEM((count,) + squares.shape, f32),
+            pltpu.SemaphoreType.DMA((2, count - 1)),
+            pltpu.SemaphoreType.DMA((2, EXPERTS - 1)),
+            pltpu.SemaphoreType.DMA((2, EXPERTS - 1)),
+            pltpu.SemaphoreType.DMA((2, 2, 5, 4)),
+            pltpu.SemaphoreType.DMA((2, 2, 5, 4)),
+            pltpu.SemaphoreType.DMA((3,)),
+        ],
+        compiler_params=pltpu.CompilerParams(
+            collective_id=3, has_side_effects=True, vmem_limit_bytes=56 * 1024 * 1024
+        ),
+        name="expert_layer",
+    )(mixer_out, squares, pick, place, route_gates, gain, expert_gate, expert_up, expert_down)
 
 
 def from_behind(array, axis, by):
@@ -420,11 +845,7 @@
     ).astype(jnp.float32)
     mixer_out = (residual.astype(jnp.float32) + projected).astype(jnp.bfloat16)
     mixer_wide = mixer_out.astype(jnp.float32)
-    squares = jnp.sum(
-        lax.all_gather(jnp.sum(mixer_wide * mixer_wide, axis=1), "ctx", axis=0), axis=0
-    )
-    norm_scale = lax.rsqrt(squares / D + 1e-05)
-    normed = (mixer_wide * norm_scale[:, None] * norm_gain[None, :]).astype(jnp.bfloat16)
+    squares = jnp.sum(mixer_wide * mixer_wide, axis=1).reshape(-1, LANES)
     experts = expert_gate.shape[0] * lax.axis_size("exp")
     top_count = expert_ids.shape[1]
     capacity = 3 * block_rows * top_count // (2 * experts)
@@ -434,35 +855,14 @@
     )
     earlier_count = jnp.cumsum(owner_hot, axis=0) - owner_hot
     slot_index = jnp.sum(earlier_count * owner_hot, axis=1)
-    matches = (
-        flat_choice[:, None, None] == jnp.arange(experts, dtype=jnp.int32)[None, :, None]
-    ) & (slot_index[:, None, None] == jnp.arange(capacity, dtype=jnp.int32)[None, None, :])
-    picks = matches.reshape(block_rows, top_count, experts, capacity)
-    selector = jnp.any(picks, axis=1).astype(jnp.bfloat16)
-    weights = jnp.sum(picks.astype(jnp.float32) * route_gates[:, :, None, None], axis=1)
-    slot_total = experts * capacity
-    outgoing = jnp.einsum(
-        "tec,td->ecd", selector, normed, preferred_element_type=jnp.float32
-    ).astype(jnp.bfloat16)
-    received = lax.all_to_all(outgoing, "exp", split_axis=0, concat_axis=0, tiled=True)
-    arrived = received.reshape(slot_total, -1)
-    piece_rows = gather(arrived, True, 3)
-    feature_count = piece_rows.shape[1]
-    gate_rows = lax.slice_in_dim(expert_gate[0], 0, feature_count, axis=0)
-    up_rows = lax.slice_in_dim(expert_up[0], 0, feature_count, axis=0)
-    gate_act = jnp.dot(piece_rows, gate_rows, preferred_element_type=jnp.float32)
-    up_act = jnp.dot(piece_rows, up_rows, preferred_element_type=jnp.float32)
-    hidden = (jax.nn.silu(gate_act) * up_act).astype(jnp.bfloat16)
-    partial_value = jnp.dot(hidden, expert_down[0], preferred_element_type=jnp.float32)
-    summed = lax.psum_scatter(
-        partial_value.astype(jnp.bfloat16), "ctx", scatter_dimension=1, tiled=True
+    target = (flat_choice * capacity + slot_index).reshape(block_rows, top_count)
+    every_slot = jnp.arange(experts * capacity, dtype=jnp.int32)
+    place = (target.T[:, :, None] == every_slot[None, None, :]).astype(jnp.bfloat16)
+    pick = jnp.any(target[None, :, :] == every_slot[:, None, None], axis=2).astype(jnp.bfloat16)
+    block_out = expert_layer(
+        mixer_out, squares, pick, place, route_gates, norm_gain[None],
+        expert_gate, expert_up, expert_down, capacity,
     )
-    answer = summed.reshape(experts, capacity, -1)
-    returned = lax.all_to_all(answer, "exp", split_axis=0, concat_axis=0, tiled=True)
-    expert_mix = jnp.einsum(
-        "tec,ecd->td", weights, returned.astype(jnp.float32), preferred_element_type=jnp.float32
-    )
-    block_out = (mixer_wide + expert_mix).astype(jnp.bfloat16)
     return (mixer_out, block_out)
 
 

time: 421 us -> 340 us (0.81)
  waiting for transfers between devices: 134 us -> 25.5 us
  Pallas kernels: 150 us -> 257 us
  blocking collectives: 42.3 us -> 0 us
  matrix products: 45.2 us -> 9.14 us
  starting transfers between devices: 9.38 us -> 4.07 us
    pallas_call x0 -> x1, Pallas kernels: none -> 174 us  [expert_layer(): pl.pallas_call(functools.partial(expert_kernel, capacity, features), out_...]
    reduce_scatter x1 -> x0, waiting for transfers between devices: 92.8 us -> none  [shards(): lax.psum_scatter(partial_value.astype(jnp.bfloat16), 'ctx', scatter_dimen...]
    pallas_call x2 -> x1, Pallas kernels: 118 us -> 51.1 us  [gather(): pl.pallas_call(functools.partial(gather_kernel, by_columns), out_shape=ja...]
    dot_general x5 -> x0, matrix products: 36 us -> none  [the longest x1 12.3 us: shards(): jnp.dot(hidden, expert_down[0], preferred_element_type=jnp.float32)]
    all_to_all x1 -> x0, blocking collectives: 24.4 us -> none  [shards(): lax.all_to_all(outgoing, 'exp', split_axis=0, concat_axis=0, tiled=True)]
    all_gather x1 -> x0, blocking collectives: 18 us -> none  [shards(): lax.all_gather(jnp.sum(mixer_wide * mixer_wide, axis=1), 'ctx', axis=0)]
    all_to_all x1 -> x0, waiting for transfers between devices: 12.1 us -> none  [shards(): lax.all_to_all(answer, 'exp', split_axis=0, concat_axis=0, tiled=True)]
    all_to_all x1 -> x0, starting transfers between devices: 5.27 us -> none  [shards(): lax.all_to_all(answer, 'exp', split_axis=0, concat_axis=0, tiled=True)]
  transfers between devices with their start and end apart: 4 -> 2, of which waited for: 3 -> 1; matrix products, arithmetic and copies ran while one was open for 1% -> 2% of each run, Pallas kernels for 0% -> 0%
where the time goes in v2:
time: 340 us; the launch traced here: 339 us
  Pallas kernels  257 us (76%)
  waiting for transfers between devices  25.5 us (8%)
  local copies, waits for them, and re-layouts  22 us (6%)
  between operations  14.3 us (4%)
  matrix products  9.14 us (3%)
  other arithmetic  6.55 us (2%)
  starting transfers between devices  4.07 us (1%)
    pallas_call x1, Pallas kernels, expert_layer(): pl.pallas_call(functools.partial(expert_kernel, capacity, features), out_...  174 us
    pallas_call x1, Pallas kernels, gather(): pl.pallas_call(functools.partial(gather_kernel, by_columns), out_shape=ja...  51.1 us
    reduce_scatter x1, waiting for transfers between devices, shards(): lax.psum_scatter(jnp.dot(lax.slice_in_dim(gathered, 0, lax.axis_size('exp...  25.5 us
    pallas_call x1, Pallas kernels, exchange(): pl.pallas_call(functools.partial(exchange_kernel, count), out_shape=(jax....  19.8 us
    unnamed x49, local copies, waits for them, and re-layouts  18.1 us
    dot_general x1, matrix products, shards(): jnp.dot(lax.slice_in_dim(gathered, 0, lax.axis_size('exp') * block_rows,...  9.14 us
    pallas_call x1, Pallas kernels, shards(): pl.pallas_call(scan_kernel, grid=strips, out_shape=jax.ShapeDtypeStruct((...  7.32 us
  transfers between devices with their start and end apart: 2, of which 1 were waited for; matrix products, arithmetic and copies ran while one was open for 2% of the time, Pallas kernels for 0%

profile of v2, /device:TPU:1, one launch (start us, length us, event | category | flops | bytes accessed | tf_op | source)
XLA Modules:
  0.0 338.7 jit_solution(4007008756378123231)
XLA Ops:
  7.2 0.0 copy-start
  7.2 0.0 reduce-scatter.2.cloned.1.call-start
  7.2 0.9 slice.9
  8.1 4.0 %collective-permute-start = (bf16[3,2048]{1,0:T(4,128)(2,1)S(1)}, bf16[3,2048]{1,0:T(4,128)(2,1)S(1)}, u32[]{:S(2)}, u32[]{:S(2)}) collective-permute-start(bf16[3,2048]{1,0:T(4,128)(2,1)S(1)} %slice.9), channel_id=1, source_target_pairs={{0,8},{8,16},{16,24},{24,32},{32,40},{40,48},{48,56},{56,64},{64,7... | collective-permute-start | bytes 36872 | tf_op jit(solution)/shard_map/ppermute | solution.py:722
  12.2 0.8 copy.43
  13.0 0.8 copy.44
  13.8 0.7 broadcast_select_fusion
  14.6 0.3 broadcast_in_dim.14.b_ref
  14.9 1.0 copy-done.7
  16.0 0.9 copy-done.8
  16.9 1.0 copy-done.10
  17.9 0.8 copy-done.15
  18.7 0.7 copy-done.16
  19.4 0.7 copy-done.17
  20.1 5.3 %prepare.1 = (f32[128,2048]{1,0:T(8,128)S(1)}, f32[128,2048]{1,0:T(8,128)S(1)}, f32[1,2048]{1,0:T(1,128)S(1)}, bf16[16,2048]{1,0:T(8,128)(2,1)S(1)}) custom-call(f32[8,2048]{1,0:T(8,128)S(1)} %pad_convert_fusion.rim_ref, bf16[128,2048]{1,0:T(8,128)(2,1)S(1)} %copy-done.7, bf16[128,2048]{1,0:T(8,128)(2,1)S(1)} %copy-done.10, f32[4,2048]{1,0:T(4,128)S(1)} %copy-done.15, ...), custom_call_target="tpu_custom_call" | custom-call | tf_op jit(solution)/shard_map/prepare/pallas_call | solution.py:761
  25.4 1.0 copy-done.2
  26.4 1.0 copy-done.4
  27.4 0.6 copy-done.14
  28.0 0.6 copy-done.19
  28.6 19.8 %state_exchange.1 = (bf16[16,16,2048]{2,1,0:T(8,128)(2,1)}, f32[16,16,128]{2,1,0:T(8,128)}) custom-call(bf16[16,2048]{1,0:T(8,128)(2,1)} %copy-done.14, f32[16,128]{1,0:T(8,128)} %bitcast.25), custom_call_target="tpu_custom_call" | custom-call | tf_op jit(solution)/shard_map/state_exchange/pallas_call | solution.py:158
  48.5 0.3 broadcast_in_dim.16.c_ref
  48.8 1.2 copy-done.3
  50.0 1.2 copy-done.5
  51.3 1.2 copy-done.6
  52.5 1.0 copy-done.11
  53.5 0.9 copy-done.13
  54.4 7.3 %scan.1.block_ref = bf16[128,2048]{1,0:T(8,128)(2,1)S(1)} custom-call(s32[1]{0:T(128)} %bitcast.place_ref, f32[128,2048]{1,0:T(8,128)S(1)} %copy-done.3, f32[128,2048]{1,0:T(8,128)S(1)} %copy-done.5, bf16[128,2048]{1,0:T(8,128)(2,1)S(1)} %copy-done.11, f32[16,2048]{1,0:T(8,128)S(1)} %copy-done.9, f32[16,2048]{1,0:T(8,128)S(1)} %copy-done.12, ...), custom_call_target="tpu_custom_call" | custom-call | tf_op jit(solution)/shard_map/scan/pallas_call | solution.py:797
  61.8 0.8 copy-done.1
  62.6 51.1 %gather_rows.1 = bf16[2048,2048]{1,0:T(8,128)(2,1)} custom-call(bf16[128,2048]{1,0:T(8,128)(2,1)} %copy-done.1), custom_call_target="tpu_custom_call" | custom-call | tf_op jit(solution)/shard_map/gather_rows/pallas_call | solution.py:277
  113.7 9.1 %convolution_convert_fusion = bf16[2048,512]{1,0:T(8,128)(2,1)} fusion(bf16[2048,2048]{1,0:T(8,128)(2,1)} %gather_rows.1, bf16[2048,512]{1,0:T(8,128)(2,1)S(1)} %copy-done), kind=kOutput, calls=%fused_computation | convolution fusion | flops 4296015872 | bytes 12582912 | tf_op jit(solution)/shard_map/dot_general | solution.py:837
  122.9 0.0 reduce-scatter.2.cloned.1.call-update
  122.9 0.7 copy-done.21
  123.6 0.1 copy.45
  123.7 0.1 eq.59
  123.8 0.1 eq.55
  124.0 1.1 reduce-window.6
  125.1 0.2 slice_reduce_fusion
  125.4 0.1 fusion.3
  125.5 0.1 reduce_sum.22
  125.6 0.1 copy.47
  125.7 0.3 fusion
  126.0 0.8 convert_element_type.36.pick_ref
  126.9 0.8 copy.48.route_ref
  127.7 1.1 fusion.1.place_ref
  128.8 25.5 %reduce-scatter.2.cloned.1.call-done = bf16[256,512]{1,0:T(8,128)(2,1)} async-done(((bf16[2048,512]{1,0:T(8,128)(2,1)}), bf16[256,512]{1,0:T(8,128)(2,1)}) %reduce-scatter.2.cloned.1.call-update) | async-done | bytes 262160 | tf_op jit(solution)/shard_map/reduce_scatter | solution.py:836
  154.3 2.3 multiply_reduce_fusion
  156.6 173.6 %expert_layer.1 = bf16[256,512]{1,0:T(8,128)(2,1)} custom-call(bf16[256,512]{1,0:T(8,128)(2,1)} %get-tuple-element.18.mixer_ref, f32[2,128]{1,0:T(2,128)} %bitcast.29, bf16[768,256]{1,0:T(8,128)(2,1)} %convert_element_type.36.pick_ref, bf16[2,256,768]{2,1,0:T(8,128)(2,1)} %fusion.1.place_ref, f32[256,2]{1,0:T(8,128)} %copy.48.route_ref, f32[1,512]{1,0:T(1,128)} %bitcast.30, ...), custom_call_target="tpu_custom_call" | custom-call | tf_op jit(solution)/shard_map/expert_layer/pallas_call | solution.py:689
  330.2 1.7 copy.50
  (34 shorter events, 0.1 us)
Async XLA Ops:
  7.2 106.6 %copy-start = (bf16[2048,512]{1,0:T(8,128)(2,1)S(1)}, bf16[2048,512]{1,0:T(8,128)(2,1)}, u32[]{:S(2)}) copy-start(bf16[2048,512]{1,0:T(8,128)(2,1)} %param.32) | copy-start | bytes 6291460
  7.2 147.1 %reduce-scatter.2.cloned.1.call-start = ((), (), s32[]{:S(2)}) async-start(), calls=%async_computation.1 | async-start | bytes 2359296 | tf_op jit(solution)/shard_map/reduce_scatter | solution.py:836
  8.1 5.6 %collective-permute-start = (bf16[3,2048]{1,0:T(4,128)(2,1)S(1)}, bf16[3,2048]{1,0:T(4,128)(2,1)S(1)}, u32[]{:S(2)}, u32[]{:S(2)}) collective-permute-start(bf16[3,2048]{1,0:T(4,128)(2,1)S(1)} %slice.9), channel_id=1, source_target_pairs={{0,8},{8,16},{16,24},{24,32},{32,40},{40,48},{48,56},{56,64},{64,7... | collective-permute-start | bytes 36872 | tf_op jit(solution)/shard_map/ppermute | solution.py:722
  14.5 34.2 %copy-start.9 = (f32[16,2048]{1,0:T(8,128)S(1)}, f32[16,2048]{1,0:T(8,128)}, u32[]{:S(2)}) copy-start(f32[16,2048]{1,0:T(8,128)} %decay_ref.3) | copy-start | bytes 393220
  14.6 34.2 %copy-start.12 = (f32[16,2048]{1,0:T(8,128)S(1)}, f32[16,2048]{1,0:T(8,128)}, u32[]{:S(2)}) copy-start(f32[16,2048]{1,0:T(8,128)} %prefix_ref.1) | copy-start | bytes 393220
  14.6 34.2 %copy-start.18 = (f32[2048]{0:T(1024)S(1)}, f32[2048]{0:T(1024)}, u32[]{:S(2)}) copy-start(f32[2048]{0:T(1024)} %param.29) | copy-start | bytes 24580
  14.9 1.0 copy-start.7
  16.0 0.9 copy-start.8
  16.9 1.0 copy-start.10
  17.9 0.8 copy-start.15
  18.7 0.7 copy-start.16
  19.4 0.7 copy-start.17
  25.4 1.0 copy-start.2
  26.4 1.0 copy-start.4
  27.4 0.6 copy-start.14
  28.0 0.6 copy-start.19
  48.8 1.2 copy-start.3
  50.0 1.2 copy-start.5
  51.3 1.2 copy-start.6
  52.5 1.0 copy-start.11
  53.5 0.9 copy-start.13
  61.8 0.8 copy-start.1
  122.9 0.7 copy-start.21
  122.9 4.0 %copy-start.22 = (f32[256,2]{0,1:T(2,128)S(1)}, f32[256,2]{0,1:T(2,128)}, u32[]{:S(2)}) copy-start(f32[256,2]{0,1:T(2,128)} %param.39) | copy-start | bytes 6148
  122.9 31.4 %copy-start.20 = (bf16[256,512]{1,0:T(8,128)(2,1)S(1)}, bf16[256,512]{1,0:T(8,128)(2,1)}, u32[]{:S(2)}) copy-start(bf16[256,512]{1,0:T(8,128)(2,1)} %param.33) | copy-start | bytes 786436
Sparse Core Ops, SparseCore 0:
  123.0 31.1 reduce-scatter.1

commit v3 on v2

v3 whole, which is shorter than its diff:
```python
import functools
import math

import jax
import jax.numpy as jnp
from jax import lax
from jax.experimental import pallas as pl
from jax.experimental.pallas import tpu as pltpu
from jax.sharding import PartitionSpec as P

SIDE = 4
STATES = 16
LANES = 128
STRIP = 512
LOG2E = math.log2(math.e)
MESH = pl.DeviceIdType.MESH


EXPERTS = 8
LINES = {0: 0, -1: 1, 1: 2, 2: 3}
RING = 4


class Torus:
    def __init__(self):
        me = lax.axis_index("ctx")
        self.me = me
        self.place = (me // SIDE, me % SIDE)

    def index(self, half, first, second):
        a = lax.rem(self.place[half] + first + 2 * SIDE, SIDE)
        b = lax.rem(self.place[1 - half] + second + 2 * SIDE, SIDE)
        return a * SIDE + b if half == 0 else b * SIDE + a


def span(rows, half, part=None):
    start = half * (rows // 2)
    return (start, rows // 2) if part is None else (start + part * (rows // 4), rows // 4)


SLOTS = (
    (0, 0),
    (1, 0), (-1, 0), (0, 1), (0, -1),
    (2, 0), (0, 2),
    (1, 1), (-1, 1), (1, -1), (-1, -1),
    (1, 2), (-1, 2), (2, 1), (2, -1),
    (2, 2),
)


def lane_parts(value):
    return tuple(value[:, k * LANES : (k + 1) * LANES] for k in range(value.shape[1] // LANES))


def sign(i):
    return 1 - 2 * (i % 2)


def beside(i):
    return sign(i) * (1 - i // 2), sign(i) * (i // 2)


def across_ring(i):
    return 2 * (1 - i), 2 * i


def corner(i):
    return sign(i), 1 - 2 * (i // 2)


def knight(i):
    along = i // 2
    return sign(i) * (1 - along) + 2 * along, 2 * (1 - along) + sign(i) * along


def single(dx, dy):
    return lambda i: (dx, dy)


def mixer_kernel(
    mixer_ref, gate_ref, delta_ref, b_ref, c_ref, taps_ref, bias_ref, delta_bias_ref, decay_ref,
    gain_ref, prefix_ref, tail_ref, weight_ref, residual_ref,
    out_ref, squares_ref,
    rim, padded, act, step, drive, summed, b_wide, c_wide, ends, spans, line_ends, line_spans,
    rows_all, weight, parts, got, landed,
    rim_sems, end_sems, gather_sems, pair_sems, sum_sems, weight_sem,
):
    torus = Torus()
    me, index = torus.me, torus.index
    x, y = torus.place
    own = lax.axis_index("exp")
    z, core = own // 2, own % 2
    count = SIDE * SIDE
    tokens, channels = mixer_ref.shape
    strips = channels // STRIP
    f32 = jnp.float32

    def strip_lanes(strip):
        return pl.ds(pl.multiple_of(strip * STRIP, STRIP), STRIP)

    load = pltpu.make_async_copy(weight_ref, weight, weight_sem)
    load.start()
    barrier = pltpu.get_barrier_semaphore()
    for k in range(1, count):
        pl.semaphore_signal(
            barrier, inc=1, device_id={"ctx": lax.rem(me + k, count)}, device_id_type=MESH
        )
    for k in range(1, EXPERTS):
        pl.semaphore_signal(
            barrier, inc=1, device_id={"exp": lax.rem(own + k, EXPERTS)}, device_id_type=MESH
        )
    pl.semaphore_wait(barrier, count - 1 + EXPERTS - 1)

    def rim_copy(target):
        return pltpu.make_async_remote_copy(
            src_ref=mixer_ref.at[pl.ds(tokens - 16, 16), :],
            dst_ref=rim,
            send_sem=rim_sems.at[0],
            recv_sem=rim_sems.at[1],
            device_id={"ctx": target},
            device_id_type=MESH,
        )

    @pl.when(me < count - 1)
    def _():
        rim_copy(me + 1).start()

    for t in range(tokens):
        b_wide[t] = jnp.broadcast_to(b_ref[:, t : t + 1], (STATES, LANES))
        c_wide[t] = jnp.broadcast_to(c_ref[:, t : t + 1], (STATES, LANES))

    def find_step(strip, carry):
        lanes = strip_lanes(strip)
        value = jnp.log(1.0 + jnp.exp(delta_ref[:, lanes].astype(f32) + delta_bias_ref[:, lanes]))
        step[:, lanes] = value
        spans[:, lanes] = jnp.sum(value, axis=0, keepdims=True)
        return carry

    lax.fori_loop(0, strips, find_step, 0)

    @pl.when(me > 0)
    def _():
        rim_copy(me).wait_recv()

    @pl.when(me == 0)
    def _():
        rim[...] = tail_ref[...]

    def rates(lanes):
        return -jnp.exp(decay_ref[:, lanes]) * LOG2E

    def advance(rate, state, steps, drives, i, b_column):
        return tuple(
            jnp.exp2(r * s) * h + b_column * d
            for r, s, h, d in zip(
                rate, lane_parts(steps[i : i + 1]), state, lane_parts(drives[i : i + 1])
            )
        )

    def prepare(strip, carry):
        lanes = strip_lanes(strip)
        padded[0:8] = rim[:, lanes].astype(f32)[8:16]
        padded[8 : 8 + tokens] = mixer_ref[:, lanes].astype(f32)
        convolved = bias_ref[:, lanes]
        for k in range(4):
            convolved = convolved + taps_ref[k : k + 1, lanes] * padded[5 + k : 5 + k + tokens]
        value = convolved / (1.0 + jnp.exp(-convolved))
        act[:, lanes] = value
        drive[:, lanes] = value * step[:, lanes]
        rate = lane_parts(rates(lanes))

        def group(number, state):
            base = pl.multiple_of(number * 8, 8)
            steps, drives = step[pl.ds(base, 8), lanes], drive[pl.ds(base, 8), lanes]
            for i in range(8):
                state = advance(rate, state, steps, drives, i, b_wide[base + i])
            return state

        zero = jnp.zeros((STATES, LANES), f32)
        state = lax.fori_loop(0, tokens // 8, group, (zero,) * (STRIP // LANES))
        ends[:, lanes] = jnp.concatenate(state, axis=1).astype(ends.dtype)
        return carry

    lax.fori_loop(0, strips, prepare, 0)

    def end_copies(stage, k, place, target):
        pairs = ((ends, line_ends), (spans, line_spans))
        return [
            pltpu.make_async_remote_copy(
                src_ref=mine,
                dst_ref=whole.at[stage, place],
                send_sem=end_sems.at[0, stage, k - 1, part],
                recv_sem=end_sems.at[1, stage, k - 1, part],
                device_id={"ctx": target},
                device_id_type=MESH,
            )
            for part, (mine, whole) in enumerate(pairs)
        ]

    leaving = []
    for k in range(1, SIDE):
        leaving += end_copies(0, k, y, index(0, 0, k))
    for one in leaving:
        one.start()
    line_ends[0, y] = ends[...]
    line_spans[0, y] = spans[...]
    for k in range(1, SIDE):
        for one in end_copies(0, k, lax.rem(y + SIDE - k, SIDE), me):
            one.wait_recv()
    for one in leaving:
        one.wait_send()

    def follow(stage):
        def one(strip, source, state):
            lanes = strip_lanes(strip)
            return (
                jnp.exp2(rates(lanes) * line_spans[stage, source, :, lanes]) * state
                + line_ends[stage, source, :, lanes].astype(f32)
            )

        return one

    def line_end(strip, carry):
        lanes = strip_lanes(strip)
        state = lax.fori_loop(
            0, SIDE, functools.partial(follow(0), strip), jnp.zeros((STATES, STRIP), f32)
        )
        ends[:, lanes] = state.astype(ends.dtype)
        spans[:, lanes] = sum(line_spans[0, source, :, lanes] for source in range(SIDE))
        return carry

    lax.fori_loop(0, strips, line_end, 0)
    for k in range(1, SIDE):

        @pl.when(x + k < SIDE)
        def _():
            for one in end_copies(1, k, x, (x + k) * SIDE + y):
                one.start()

    for k in range(1, SIDE):

        @pl.when(x >= k)
        def _():
            for one in end_copies(1, k, x - k, me):
                one.wait_recv()

    in_flight = []

    def moved(half, line, kind, first, second, part, towards, target):
        def rows(a, b):
            where = (a, b) if half == 0 else (b, a)
            where = tuple((v + 1) % SIDE - 1 for v in where)
            start, size = (0, tokens) if part is None else (part * (tokens // 2), tokens // 2)
            return rows_all.at[half, pl.ds(SLOTS.index(where) * tokens + start, size), :]

        return pltpu.make_async_remote_copy(
            src_ref=rows(first, second),
            dst_ref=rows(first - towards[0], second - towards[1]),
            send_sem=gather_sems.at[0, half, line, kind],
            recv_sem=gather_sems.at[1, half, line, kind],
            device_id={"ctx": target},
            device_id_type=MESH,
        )

    def send(half, line, kind, first, second, part, towards):
        one = moved(half, line, kind, first, second, part, towards, index(half, *towards))
        one.start()
        in_flight.append(one)

    def arrived(half, line, kind, first, second, part):
        moved(half, line, kind, first, second, part, (0, 0), me).wait_recv()

    def send_line(half, first):
        send(half, LINES[first], 0, first, 0, None, (0, 1))
        send(half, LINES[first], 1, first, 0, None, (0, -1))

    def pass_on(half, first):
        arrived(half, LINES[first], 0, first, -1, None)
        send(half, LINES[first], 2, first, -1, 0, (0, 1))
        arrived(half, LINES[first], 1, first, 1, None)
        send(half, LINES[first], 3, first, 1, 1, (0, -1))

    def last_of(half, first):
        arrived(half, LINES[first], 2, first, 2, 0)
        arrived(half, LINES[first], 3, first, 2, 1)

    per_half = strips // 2

    def scan(half, strip, carry):
        lanes = strip_lanes(half * per_half + strip)
        rate = lane_parts(rates(lanes))
        state = prefix_ref[:, lanes]
        state = lax.fori_loop(
            0, x, functools.partial(follow(1), half * per_half + strip), state
        )
        state = lax.fori_loop(
            0, y, functools.partial(follow(0), half * per_half + strip), state
        )

        def group(number, state):
            base = pl.multiple_of(number * 8, 8)
            steps, drives = step[pl.ds(base, 8), lanes], drive[pl.ds(base, 8), lanes]
            found = []
            for i in range(8):
                state = advance(rate, state, steps, drives, i, b_wide[base + i])
                c_column = c_wide[base + i]
                found.append(
                    jnp.concatenate(
                        [jnp.sum(c_column * h, axis=0, keepdims=True) for h in state], axis=1
                    )
                )
            summed[pl.ds(base, 8), :] = jnp.concatenate(found, axis=0)
            return state

        lax.fori_loop(0, tokens // 8, group, lane_parts(state))
        gate = gate_ref[:, lanes].astype(f32)
        mixed = summed[...] + gain_ref[:, lanes] * act[:, lanes]
        rows_all[half, 0:tokens, strip_lanes(strip)] = (
            mixed * (gate / (1.0 + jnp.exp(-gate)))
        ).astype(rows_all.dtype)
        return carry

    for half in (0, 1):
        lax.fori_loop(0, per_half, functools.partial(scan, half), 0)
        send(half, RING, 0, 0, 0, None, (1, 0))
        send(half, RING, 1, 0, 0, None, (-1, 0))
        send_line(half, 0)

    width = weight.shape[1]
    half_channels = channels // 2

    def pair_copy(column, part, target):
        rows = pl.ds(pl.multiple_of(part * tokens, tokens), tokens)
        return pltpu.make_async_remote_copy(
            src_ref=parts.at[1 - core, column, rows, :],
            dst_ref=got.at[column, rows, :],
            send_sem=pair_sems.at[0, column, part],
            recv_sem=pair_sems.at[1, column, part],
            device_id={"exp": target},
            device_id_type=MESH,
        )

    sibling = own + 1 - 2 * core

    def project(where, number, first_slot):
        together = min(number, 2)

        def one(pair, carry):
            rows = pl.ds(pl.multiple_of((first_slot + pair * together) * tokens, tokens), together * tokens)
            value = jnp.dot(
                rows_all[0, rows, :], weight[0:half_channels], preferred_element_type=f32
            ) + jnp.dot(
                rows_all[1, rows, :], weight[half_channels:], preferred_element_type=f32
            )
            for k in range(together):
                dx, dy = where(pair * together + k)
                column = lax.rem(x + dx + SIDE, SIDE)
                line = lax.rem(y + dy + SIDE, SIDE)
                owner, part = line // 2, line % 2
                parts[owner, column, pl.ds(pl.multiple_of(part * tokens, tokens), tokens), :] = value[
                    k * tokens : (k + 1) * tokens
                ].astype(parts.dtype)

                @pl.when(owner != core)
                def _():
                    pair_copy(column, part, sibling).start()

            return carry

        lax.fori_loop(0, number // together, one, 0)

    load.wait()
    project(single(0, 0), 1, 0)
    for half in (0, 1):
        arrived(half, RING, 0, -1, 0, None)
        send(half, RING, 2, -1, 0, 0, (1, 0))
        arrived(half, RING, 1, 1, 0, None)
        send(half, RING, 3, 1, 0, 1, (-1, 0))
        send_line(half, -1)
        send_line(half, 1)
    for half in (0, 1):
        pass_on(half, 0)
    project(beside, 4, 1)
    for half in (0, 1):
        arrived(half, RING, 2, 2, 0, 0)
        arrived(half, RING, 3, 2, 0, 1)
        send_line(half, 2)
    for half in (0, 1):
        last_of(half, 0)
    project(across_ring, 2, 5)
    for first in (-1, 1):
        for half in (0, 1):
            pass_on(half, first)
    project(corner, 4, 7)
    for half in (0, 1):
        pass_on(half, 2)
    for first in (-1, 1):
        for half in (0, 1):
            last_of(half, first)
    project(knight, 4, 11)
    for half in (0, 1):
        last_of(half, 2)
    project(single(2, 2), 1, 15)

    def column_at(offset):
        return lax.rem(z + offset + SIDE, SIDE)

    def pair_sum(offset):
        column = column_at(offset)
        for part in (0, 1):
            pair_copy(column, part, own).wait_recv()
        value = parts[core, column].astype(f32) + got[column].astype(f32)
        return value

    def settle(offset):
        parts[core, column_at(offset)] = pair_sum(offset).astype(parts.dtype)

    summing = []

    def sum_copy(kind, offset, target):
        size = tokens
        rows = pl.ds(0, 2 * size) if kind < 2 else pl.ds((kind - 2) * size, size)
        return pltpu.make_async_remote_copy(
            src_ref=parts.at[core, column_at(offset), rows, :],
            dst_ref=landed.at[min(kind, 2), rows, :],
            send_sem=sum_sems.at[0, kind],
            recv_sem=sum_sems.at[1, kind],
            device_id={"exp": target},
            device_id_type=MESH,
        )

    def give(kind, offset):
        step_z = 1 if kind % 2 == 0 else -1
        one = sum_copy(kind, offset, column_at(step_z) * 2 + core)
        one.start()
        summing.append(one)

    settle(2)
    give(2, 2)
    give(3, 2)
    settle(1)
    settle(-1)
    for kind, offset in ((2, 1), (3, -1)):
        sum_copy(kind, 0, own).wait_recv()
        rows = pl.ds((kind - 2) * tokens, tokens)
        column = column_at(offset)
        parts[core, column, rows, :] = (
            parts[core, column, rows, :].astype(f32) + landed[2, rows, :].astype(f32)
        ).astype(parts.dtype)
        give(kind - 2, offset)
    value = pair_sum(0) + residual_ref[...].astype(f32)
    for kind in (0, 1):
        sum_copy(kind, 0, own).wait_recv()
    value = value + landed[0].astype(f32) + landed[1].astype(f32)
    value = value.astype(out_ref.dtype)
    out_ref[...] = value
    value = value.astype(f32)
    value = value * value
    ones = jnp.ones((16, width), jnp.bfloat16)
    found = jnp.zeros((16, value.shape[0]), f32)
    for _ in range(3):
        term = value.astype(jnp.bfloat16)
        value = value - term.astype(f32)
        found = found + lax.dot_general(
            ones, term, (((1,), (1,)), ((), ())), preferred_element_type=f32
        )
    squares_ref[...] = found[0:8]

    @pl.when(me < count - 1)
    def _():
        rim_copy(me + 1).wait_send()

    for k in range(1, SIDE):

        @pl.when(x + k < SIDE)
        def _():
            for one in end_copies(1, k, x, (x + k) * SIDE + y):
                one.wait_send()

    for column in range(SIDE):
        for part in (0, 1):
            pair_copy(column, part, sibling).wait_send()
    for one in in_flight + summing:
        one.wait_send()


def mixer(
    mixer_in, gate_in, delta_in, b_proj, c_proj, conv_kernel, conv_bias, delta_bias, decay_log,
    skip_gain, prefix_state, prefix_tail, out_proj, residual,
):
    tokens, channels = mixer_in.shape
    rows, width = residual.shape
    count = SIDE * SIDE
    tail = jnp.concatenate(
        [jnp.zeros((16 - prefix_tail.shape[0], channels), prefix_tail.dtype), prefix_tail]
    )
    here = pl.BlockSpec(memory_space=pltpu.VMEM)
    away = pl.BlockSpec(memory_space=pl.ANY)
    bf16, f32 = jnp.bfloat16, jnp.float32
    return pl.pallas_call(
        mixer_kernel,
        out_shape=(
            jax.ShapeDtypeStruct((rows, width), bf16),
            jax.ShapeDtypeStruct((8, rows), f32),
        ),
        in_specs=[here] * 12 + [away, here],
        out_specs=(here, here),
        scratch_shapes=[
            pltpu.VMEM((16, channels), bf16),
            pltpu.VMEM((8 + tokens, STRIP), f32),
            pltpu.VMEM((tokens, channels), f32),
            pltpu.VMEM((tokens, channels), f32),
            pltpu.VMEM((tokens, channels), f32),
            pltpu.VMEM((tokens, STRIP), f32),
            pltpu.VMEM((tokens, STATES, LANES), f32),
            pltpu.VMEM((tokens, STATES, LANES), f32),
            pltpu.VMEM((STATES, channels), bf16),
            pltpu.VMEM((1, channels), f32),
            pltpu.VMEM((2, SIDE, STATES, channels), bf16),
            pltpu.VMEM((2, SIDE, 1, channels), f32),
            pltpu.VMEM((2, count * tokens, channels // 2), bf16),
            pltpu.VMEM((channels, width), bf16),
            pltpu.VMEM((2, SIDE, rows, width), bf16),
            pltpu.VMEM((SIDE, rows, width), bf16),
            pltpu.VMEM((3, rows, width), bf16),
            pltpu.SemaphoreType.DMA((2,)),
            pltpu.SemaphoreType.DMA((2, 2, SIDE - 1, 2)),
            pltpu.SemaphoreType.DMA((2, 2, 5, 4)),
            pltpu.SemaphoreType.DMA((2, SIDE, 2)),
            pltpu.SemaphoreType.DMA((2, 4)),
            pltpu.SemaphoreType.DMA,
        ],
        compiler_params=pltpu.CompilerParams(
            collective_id=1, has_side_effects=True, vmem_limit_bytes=56 * 1024 * 1024
        ),
        name="mixer",
    )(
        mixer_in, gate_in, delta_in, b_proj, c_proj, conv_kernel, conv_bias[None], delta_bias[None],
        decay_log, skip_gain[None], prefix_state, tail, out_proj, residual,
    )


def expert_kernel(
    capacity, features,
    mixer_ref, squares_ref, pick_ref, place_ref, route_ref, gain_ref, gate_ref, up_ref, down_ref,
    out_ref,
    blocks, landed, wide, down, total, hidden, outgoing, answer, returned, all_squares,
    square_sems, dispatch_sems, return_sems, gather_sems, sum_sems, weight_sems,
):
    torus = Torus()
    me, index = torus.me, torus.index
    own_expert = lax.axis_index("exp")
    slots, width = answer.shape
    units = down.shape[0]
    count = SIDE * SIDE

    weights = [
        pltpu.make_async_copy(gate_ref.at[0], wide.at[:, pl.ds(0, units)], weight_sems.at[0]),
        pltpu.make_async_copy(up_ref.at[0], wide.at[:, pl.ds(units, units)], weight_sems.at[1]),
        pltpu.make_async_copy(down_ref.at[0], down, weight_sems.at[2]),
    ]
    for one in weights:
        one.start()

    barrier = pltpu.get_barrier_semaphore()
    for k in range(1, count):
        pl.semaphore_signal(
            barrier, inc=1, device_id={"ctx": lax.rem(me + k, count)}, device_id_type=MESH
        )
    for k in range(1, EXPERTS):
        pl.semaphore_signal(
            barrier, inc=1, device_id={"exp": lax.rem(own_expert + k, EXPERTS)}, device_id_type=MESH
        )
    pl.semaphore_wait(barrier, count - 1 + EXPERTS - 1)

    square_copies = []
    for k in range(1, count):
        square_copies.append(
            pltpu.make_async_remote_copy(
                src_ref=squares_ref,
                dst_ref=all_squares.at[me],
                send_sem=square_sems.at[0, k - 1],
                recv_sem=square_sems.at[1, k - 1],
                device_id={"ctx": lax.rem(me + k, count)},
                device_id_type=MESH,
            )
        )
        square_copies[-1].start()
    all_squares[me] = squares_ref[...]
    for k in range(1, count):
        source = lax.rem(me + count - k, count)
        pltpu.make_async_remote_copy(
            src_ref=squares_ref,
            dst_ref=all_squares.at[source],
            send_sem=square_sems.at[0, k - 1],
            recv_sem=square_sems.at[1, k - 1],
            device_id={"ctx": me},
            device_id_type=MESH,
        ).wait_recv()
    scale = lax.rsqrt(jnp.sum(all_squares[...], axis=0)[0:1] / features + 1e-05)

    def pick(chunk, carry):
        rows = pl.ds(pl.multiple_of(chunk * capacity, 16), capacity)
        chosen = pick_ref[rows, :]
        picked = jnp.dot(chosen, mixer_ref[...], preferred_element_type=jnp.float32)
        chosen = chosen.astype(jnp.float32)
        row_scale = jnp.sum(chosen * scale, axis=1, keepdims=True)
        outgoing[rows, :] = (picked * row_scale * gain_ref[...]).astype(outgoing.dtype)
        return carry

    lax.fori_loop(0, EXPERTS, pick, 0)

    def expert_rows(expert):
        return pl.ds(pl.multiple_of(expert * capacity, 16), capacity)

    def across(sems, source, target_ref):
        started = []
        for k in range(1, EXPERTS):
            peer = lax.rem(own_expert + k, EXPERTS)
            started.append(
                pltpu.make_async_remote_copy(
                    src_ref=source.at[expert_rows(peer), :],
                    dst_ref=target_ref.at[expert_rows(own_expert), :],
                    send_sem=sems.at[0, k - 1],
                    recv_sem=sems.at[1, k - 1],
                    device_id={"exp": peer},
                    device_id_type=MESH,
                )
            )
            started[-1].start()
        target_ref[expert_rows(own_expert), :] = source[expert_rows(own_expert), :]
        for k in range(1, EXPERTS):
            origin = lax.rem(own_expert + EXPERTS - k, EXPERTS)
            pltpu.make_async_remote_copy(
                src_ref=source.at[expert_rows(origin), :],
                dst_ref=target_ref.at[expert_rows(origin), :],
                send_sem=sems.at[0, k - 1],
                recv_sem=sems.at[1, k - 1],
                device_id={"exp": own_expert},
                device_id_type=MESH,
            ).wait_recv()
        return started

    crossing = across(dispatch_sems, outgoing, blocks.at[me])

    in_flight = {}

    def moved(half, line, kind, first, second, part, target):
        start, size = span(slots, half, part)
        ref = blocks.at[index(half, first, second), pl.ds(start, size), :]
        return pltpu.make_async_remote_copy(
            src_ref=ref,
            dst_ref=ref,
            send_sem=gather_sems.at[0, half, line, kind],
            recv_sem=gather_sems.at[1, half, line, kind],
            device_id={"ctx": target},
            device_id_type=MESH,
        )

    def send(half, line, kind, first, second, part, towards):
        one = moved(half, line, kind, first, second, part, index(half, *towards))
        one.start()
        where = (first, second) if half == 0 else (second, first)
        in_flight.setdefault(where, []).append(one)

    def arrived(half, line, kind, first, second, part):
        moved(half, line, kind, first, second, part, me).wait_recv()

    def send_line(half, first):
        send(half, LINES[first], 0, first, 0, None, (0, 1))
        send(half, LINES[first], 1, first, 0, None, (0, -1))

    def pass_on(half, first):
        arrived(half, LINES[first], 0, first, -1, None)
        send(half, LINES[first], 2, first, -1, 0, (0, 1))
        arrived(half, LINES[first], 1, first, 1, None)
        send(half, LINES[first], 3, first, 1, 1, (0, -1))

    def last_of(half, first):
        arrived(half, LINES[first], 2, first, 2, 0)
        arrived(half, LINES[first], 3, first, 2, 1)

    row_tile = slots // 2

    def over_blocks(where, number, body):
        def one(step, carry):
            block, tile = step // 2, step % 2
            dx, dy = where(block)
            owner = index(0, dx, dy)
            body(owner, pl.ds(pl.multiple_of(tile * row_tile, 16), row_tile))
            return carry

        lax.fori_loop(0, number * 2, one, 0)

    def grow(owner, rows):
        part = wide[pl.ds(pl.multiple_of(owner * width, 16), width), :]
        total[rows, :] += jnp.dot(blocks[owner, rows, :], part, preferred_element_type=jnp.float32)

    for half in (0, 1):
        send(half, RING, 0, 0, 0, None, (1, 0))
        send(half, RING, 1, 0, 0, None, (-1, 0))
    for half in (0, 1):
        send_line(half, 0)
    total[...] = jnp.zeros_like(total)
    for one in weights:
        one.wait()
    over_blocks(single(0, 0), 1, grow)
    for half in (0, 1):
        arrived(half, RING, 0, -1, 0, None)
        send(half, RING, 2, -1, 0, 0, (1, 0))
        arrived(half, RING, 1, 1, 0, None)
        send(half, RING, 3, 1, 0, 1, (-1, 0))
    for half in (0, 1):
        send_line(half, -1)
        send_line(half, 1)
    for half in (0, 1):
        pass_on(half, 0)
    over_blocks(beside, 4, grow)
    for half in (0, 1):
        arrived(half, RING, 2, 2, 0, 0)
        arrived(half, RING, 3, 2, 0, 1)
        send_line(half, 2)
    for half in (0, 1):
        last_of(half, 0)
    over_blocks(across_ring, 2, grow)
    for first in (-1, 1):
        for half in (0, 1):
            pass_on(half, first)
    over_blocks(corner, 4, grow)
    for half in (0, 1):
        pass_on(half, 2)
    for first in (-1, 1):
        for half in (0, 1):
            last_of(half, first)
    over_blocks(knight, 4, grow)
    for half in (0, 1):
        last_of(half, 2)
    over_blocks(single(2, 2), 1, grow)

    def activate(step, carry):
        rows = pl.ds(pl.multiple_of(step * capacity, 16), capacity)
        gate = total[rows, 0:units]
        hidden[rows, :] = (gate / (1.0 + jnp.exp(-gate)) * total[rows, units : 2 * units]).astype(
            hidden.dtype
        )
        return carry

    lax.fori_loop(0, EXPERTS, activate, 0)

    def project(owner, rows):
        part = down[:, pl.ds(pl.multiple_of(owner * width, LANES), width)]
        blocks[owner, rows, :] = jnp.dot(
            hidden[rows, :], part, preferred_element_type=jnp.float32
        ).astype(blocks.dtype)

    def fill(places, where):
        for place in places:
            for one in in_flight.pop(place, ()):
                one.wait_send()
        over_blocks(where, len(places), project)

    summing = []

    def part_rows(half, part):
        start, size = span(slots, half, part)
        return pl.ds(start, size)

    def landing(half, line, kind):
        if kind < 2:
            return landed.at[half, line, kind]
        size = slots // 4
        return landed.at[half, line, 2, pl.ds((kind - 2) * size, size), :]

    def sum_copy(half, line, kind, first, second, part, target):
        return pltpu.make_async_remote_copy(
            src_ref=blocks.at[index(half, first, second), part_rows(half, part), :],
            dst_ref=landing(half, line, kind),
            send_sem=sum_sems.at[0, half, line, kind],
            recv_sem=sum_sems.at[1, half, line, kind],
            device_id={"ctx": target},
            device_id_type=MESH,
        )

    def give(half, line, kind, first, second, part):
        step = 1 if kind % 2 == 0 else -1
        target = index(half, step, 0) if line == RING else index(half, 0, step)
        one = sum_copy(half, line, kind, first, second, part, target)
        one.start()
        summing.append(one)

    def taken(half, line, kind):
        part = None if kind < 2 else kind - 2
        sum_copy(half, line, kind, 0, 0, part, me).wait_recv()

    def add(half, first, second, part, line, kinds, target=None):
        for kind in kinds:
            taken(half, line, kind)
        start, size = span(slots, half, part)
        owner = index(half, first, second)
        tile = 96

        def one(step, carry):
            offset = pl.multiple_of(step * tile, 16)
            rows = pl.ds(pl.multiple_of(start + offset, 16), tile)
            value = blocks[owner, rows, :].astype(jnp.float32)
            for kind in kinds:
                value = value + landing(half, line, kind)[pl.ds(offset, tile), :].astype(jnp.float32)
            value = value.astype(blocks.dtype)
            if target is None:
                blocks[owner, rows, :] = value
            else:
                target[rows, :] = value
            return carry

        lax.fori_loop(0, size // tile, one, 0)

    def at(line, offset):
        return (offset, 0) if line == RING else ({v: k for k, v in LINES.items()}[line], offset)

    def begin(half, line):
        give(half, line, 2, *at(line, 2), 0)
        give(half, line, 3, *at(line, 2), 1)

    def middle(half, line):
        add(half, *at(line, 1), 0, line, (2,))
        give(half, line, 0, *at(line, 1), None)
        add(half, *at(line, -1), 1, line, (3,))
        give(half, line, 1, *at(line, -1), None)

    def finish(half, line, target=None):
        add(half, *at(line, 0), None, line, (0, 1), target)

    halves = (0, 1)
    fill([(2, 2)], single(2, 2))
    for half in halves:
        begin(half, LINES[2])
    fill([(1, 2), (-1, 2), (2, 1), (2, -1)], knight)
    for first in (1, -1):
        for half in halves:
            begin(half, LINES[first])
    fill([(2, 0), (0, 2)], across_ring)
    for half in halves:
        begin(half, LINES[0])
    for half in halves:
        middle(half, LINES[2])
    fill([(1, 1), (-1, 1), (1, -1), (-1, -1)], corner)
    for first in (1, -1):
        for half in halves:
            middle(half, LINES[first])
    fill([(1, 0), (-1, 0), (0, 1), (0, -1)], beside)
    for half in halves:
        middle(half, LINES[0])
    for one in crossing:
        one.wait_send()
    fill([(0, 0)], single(0, 0))
    for half in halves:
        finish(half, LINES[2])
        begin(half, RING)
    for first in (1, -1):
        for half in halves:
            finish(half, LINES[first])
    for half in halves:
        middle(half, RING)
    for half in halves:
        finish(half, LINES[0])
    for half in halves:
        finish(half, RING, answer)

    back = across(return_sems, answer, returned)
    rows = mixer_ref.shape[0]
    value = mixer_ref[...].astype(jnp.float32)
    for k in range(route_ref.shape[1]):
        value = value + route_ref[:, k : k + 1] * jnp.dot(
            place_ref[k], returned[...], preferred_element_type=jnp.float32
        )
    out_ref[...] = value.astype(out_ref.dtype)
    for one in summing + back + square_copies:
        one.wait_send()


def expert_layer(
    mixer_out, squares, pick, place, route_gates, gain, expert_gate, expert_up, expert_down, capacity
):
    rows, width = mixer_out.shape
    features, units = expert_gate.shape[1:]
    slots = EXPERTS * capacity
    count = SIDE * SIDE
    here = pl.BlockSpec(memory_space=pltpu.VMEM)
    away = pl.BlockSpec(memory_space=pl.ANY)
    bf16, f32 = jnp.bfloat16, jnp.float32
    return pl.pallas_call(
        functools.partial(expert_kernel, capacity, features),
        out_shape=jax.ShapeDtypeStruct((rows, width), bf16),
        in_specs=[here] * 6 + [away] * 3,
        out_specs=here,
        scratch_shapes=[
            pltpu.VMEM((count, slots, width), bf16),
            pltpu.VMEM((2, 5, 3, slots // 2, width), bf16),
            pltpu.VMEM((features, 2 * units), bf16),
            pltpu.VMEM((units, features), bf16),
            pltpu.VMEM((slots, 2 * units), f32),
            pltpu.VMEM((slots, units), bf16),
            pltpu.VMEM((slots, width), bf16),
            pltpu.VMEM((slots, width), bf16),
            pltpu.VMEM((slots, width), bf16),
            pltpu.VMEM((count,) + squares.shape, f32),
            pltpu.SemaphoreType.DMA((2, count - 1)),
            pltpu.SemaphoreType.DMA((2, EXPERTS - 1)),
            pltpu.SemaphoreType.DMA((2, EXPERTS - 1)),
            pltpu.SemaphoreType.DMA((2, 2, 5, 4)),
            pltpu.SemaphoreType.DMA((2, 2, 5, 4)),
            pltpu.SemaphoreType.DMA((3,)),
        ],
        compiler_params=pltpu.CompilerParams(
            collective_id=3, has_side_effects=True, vmem_limit_bytes=56 * 1024 * 1024
        ),
        name="expert_layer",
    )(mixer_out, squares, pick, place, route_gates, gain, expert_gate, expert_up, expert_down)


def shards(
    mixer_in,
    gate_in,
    delta_in,
    b_proj,
    c_proj,
    conv_kernel,
    conv_bias,
    delta_bias,
    decay_log,
    skip_gain,
    prefix_state,
    prefix_tail,
    out_proj,
    residual,
    norm_gain,
    expert_gate,
    expert_up,
    expert_down,
    expert_ids,
    route_gates,
):
    mixer_out, squares = mixer(
        mixer_in, gate_in, delta_in, b_proj, c_proj, conv_kernel, conv_bias, delta_bias, decay_log,
        skip_gain, prefix_state, prefix_tail, out_proj, residual,
    )
    block_rows = residual.shape[0]
    experts = expert_gate.shape[0] * lax.axis_size("exp")
    top_count = expert_ids.shape[1]
    capacity = 3 * block_rows * top_count // (2 * experts)
    flat_choice = expert_ids.reshape(-1)
    owner_hot = (flat_choice[:, None] == jnp.arange(experts, dtype=jnp.int32)[None, :]).astype(
        jnp.int32
    )
    earlier_count = jnp.cumsum(owner_hot, axis=0) - owner_hot
    slot_index = jnp.sum(earlier_count * owner_hot, axis=1)
    target = (flat_choice * capacity + slot_index).reshape(block_rows, top_count)
    every_slot = jnp.arange(experts * capacity, dtype=jnp.int32)
    place = (target.T[:, :, None] == every_slot[None, None, :]).astype(jnp.bfloat16)
    pick = jnp.any(target[None, :, :] == every_slot[:, None, None], axis=2).astype(jnp.bfloat16)
    block_out = expert_layer(
        mixer_out, squares, pick, place, route_gates, norm_gain[None],
        expert_gate, expert_up, expert_down, capacity,
    )
    return (mixer_out, block_out)


def solution(mesh):
    placed = (
        P("ctx", "exp"),
        P("ctx", "exp"),
        P("ctx", "exp"),
        P(None, "ctx"),
        P(None, "ctx"),
        P(None, "exp"),
        P("exp"),
        P("exp"),
        P(None, "exp"),
        P("exp"),
        P(None, "exp"),
        P(None, "exp"),
        P("exp", "ctx"),
        P("exp", "ctx"),
        P("ctx"),
        P("exp", None, "ctx"),
        P("exp", None, "ctx"),
        P("exp", "ctx", None),
        P("exp", None),
        P("exp", None),
    )
    return jax.shard_map(
        shards,
        mesh=mesh,
        in_specs=placed,
        out_specs=(P("exp", "ctx"), P("exp", "ctx")),
        check_vma=False,
    )
```

time: 340 us -> 272 us (0.80)
  waiting for transfers between devices: 25.5 us -> 0 us
  local copies, waits for them, and re-layouts: 22 us -> 5.37 us
  between operations: 14.3 us -> 0.71 us
  matrix products: 9.14 us -> 0 us
  Pallas kernels: 257 us -> 262 us
  starting transfers between devices: 4.07 us -> 0 us
    reduce_scatter x1 -> x0, waiting for transfers between devices: 25.5 us -> none  [shards(): lax.psum_scatter(jnp.dot(lax.slice_in_dim(gathered, 0, lax.axis_size('exp...]
    unnamed x49 -> x10, local copies, waits for them, and re-layouts: 18.1 us -> 4 us
    dot_general x1 -> x0, matrix products: 9.14 us -> none  [shards(): jnp.dot(lax.slice_in_dim(gathered, 0, lax.axis_size('exp') * block_rows,...]
    pallas_call x4 -> x1, Pallas kernels: 83.6 us -> 88.4 us  [mixer(): pl.pallas_call(mixer_kernel, out_shape=(jax.ShapeDtypeStruct((rows, width...]
    ppermute x1 -> x0, starting transfers between devices: 4.03 us -> none  [from_behind(): return lax.ppermute(array, axis, pairs)]
  transfers between devices with their start and end apart: 2 -> 0, of which waited for: 1 -> 0; matrix products, arithmetic and copies ran while one was open for 2% -> 0% of each run, Pallas kernels for 0% -> 0%
where the time goes in v3:
time: 272 us
  Pallas kernels  262 us (96%)
  local copies, waits for them, and re-layouts  5.37 us (2%)
  other arithmetic  4.15 us (2%)
    pallas_call x1, Pallas kernels, expert_layer(): pl.pallas_call(functools.partial(expert_kernel, capacity, features), out_...  173 us
    pallas_call x1, Pallas kernels, mixer(): pl.pallas_call(mixer_kernel, out_shape=(jax.ShapeDtypeStruct((rows, width...  88.4 us

profile of v3, /device:TPU:1, one launch (start us, length us, event | category | flops | bytes accessed | tf_op | source)
XLA Modules:
  0.0 271.8 jit_solution(10171869146853723757)
XLA Ops:
  0.6 0.0 copy-start.1
  0.6 0.8 copy.37
  1.5 0.1 eq.55
  1.6 1.1 reduce-window.6
  2.8 0.2 slice_reduce_fusion
  3.0 0.1 eq.51
  3.2 0.1 fusion.3
  3.3 0.1 reduce_sum.12
  3.4 0.1 copy.39
  3.5 0.7 multiply_add_fusion
  4.2 1.1 fusion.1.place_ref
  5.3 0.3 fusion
  5.5 0.8 convert_element_type.15.pick_ref
  6.4 0.0 copy-done.1
  6.4 0.6 concatenate.3.tail_ref
  7.0 0.0 copy-start.2
  7.0 88.4 %mixer.1 = (bf16[256,512]{1,0:T(8,128)(2,1)}, f32[8,256]{1,0:T(8,128)}) custom-call(bf16[128,2048]{1,0:T(8,128)(2,1)} %mixer_ref.1, bf16[128,2048]{1,0:T(8,128)(2,1)} %gate_ref.2, bf16[128,2048]{1,0:T(8,128)(2,1)} %delta_ref.1, f32[16,128]{1,0:T(8,128)} %b_ref.1, f32[16,128]{1,0:T(8,128)} %c_ref.1, f32[4,2048]{1,0:T(4,128)} %taps_ref.1, f32[1,2048]{1,0:T(1,128)} %bitcast.14, ...), custom_call_target="tpu_custom_call" | custom-call | tf_op jit(solution)/shard_map/mixer/pallas_call | solution.py:500
  95.4 0.0 copy-done.2
  95.4 0.8 copy.40.route_ref
  96.2 0.0 copy-start
  96.2 173.1 %expert_layer.1 = bf16[256,512]{1,0:T(8,128)(2,1)} custom-call(bf16[256,512]{1,0:T(8,128)(2,1)} %get-tuple-element.8.mixer_ref, f32[8,256]{1,0:T(8,128)} %get-tuple-element.5.squares_ref, bf16[768,256]{1,0:T(8,128)(2,1)} %convert_element_type.15.pick_ref, bf16[2,256,768]{2,1,0:T(8,128)(2,1)} %fusion.1.place_ref, f32[256,2]{1,0:T(8,128)} %copy.40.route_ref, ...), custom_call_target="tpu_custom_call" | custom-call | tf_op jit(solution)/shard_map/expert_layer/pallas_call | solution.py:891
  269.4 0.0 copy-done
  269.4 0.7 copy.43
  270.1 1.7 copy.44
  (3 shorter events, 0.0 us)
Async XLA Ops:
  0.6 5.7 %copy-start.1 = (bf16[3,2048]{1,0:T(4,128)(2,1)S(1)}, bf16[3,2048]{1,0:T(4,128)(2,1)}, u32[]{:S(2)}) copy-start(bf16[3,2048]{1,0:T(4,128)(2,1)} %param.31) | copy-start | bytes 36868
  7.0 88.4 %copy-start.2 = (f32[256,2]{0,1:T(2,128)S(1)}, f32[256,2]{0,1:T(2,128)}, u32[]{:S(2)}) copy-start(f32[256,2]{0,1:T(2,128)} %param.39) | copy-start | bytes 6148
  96.2 173.1 %copy-start = (bf16[256,512]{1,0:T(8,128)(2,1)S(1)}, bf16[256,512]{1,0:T(8,128)(2,1)}, u32[]{:S(2)}) copy-start(bf16[256,512]{1,0:T(8,128)(2,1)} %get-tuple-element.8.mixer_ref) | copy-start | bytes 786436

commit v4 on v3

v4 whole, which is shorter than its diff:
```python
import functools
import math

import jax
import jax.numpy as jnp
from jax import lax
from jax.experimental import pallas as pl
from jax.experimental.pallas import tpu as pltpu
from jax.sharding import PartitionSpec as P

SIDE = 4
STATES = 16
LANES = 128
STRIP = 512
LOG2E = math.log2(math.e)
MESH = pl.DeviceIdType.MESH


EXPERTS = 8
LINES = {0: 0, -1: 1, 1: 2, 2: 3}
RING = 4


class Torus:
    def __init__(self):
        me = lax.axis_index("ctx")
        self.me = me
        self.place = (me // SIDE, me % SIDE)

    def index(self, half, first, second):
        a = lax.rem(self.place[half] + first + 2 * SIDE, SIDE)
        b = lax.rem(self.place[1 - half] + second + 2 * SIDE, SIDE)
        return a * SIDE + b if half == 0 else b * SIDE + a


PEERS = ((1, 0), (1, 1), (2, 0), (2, 1), (0, 0), (0, 1), (-1, 0), (-1, 1))
OWN = 4
UNITS = (0, 1, 2, 3)


def span(rows, unit, part=None):
    size = rows // len(UNITS)
    return (unit * size, size) if part is None else (unit * size + part * (size // 2), size // 2)


SLOTS = (
    (0, 0),
    (1, 0), (-1, 0), (0, 1), (0, -1),
    (2, 0), (0, 2),
    (1, 1), (-1, 1), (1, -1), (-1, -1),
    (1, 2), (-1, 2), (2, 1), (2, -1),
    (2, 2),
)


def lane_parts(value):
    return tuple(value[:, k * LANES : (k + 1) * LANES] for k in range(value.shape[1] // LANES))


def sign(i):
    return 1 - 2 * (i % 2)


def beside(i):
    return sign(i) * (1 - i // 2), sign(i) * (i // 2)


def across_ring(i):
    return 2 * (1 - i), 2 * i


def corner(i):
    return sign(i), 1 - 2 * (i // 2)


def knight(i):
    along = i // 2
    return sign(i) * (1 - along) + 2 * along, 2 * (1 - along) + sign(i) * along


def single(dx, dy):
    return lambda i: (dx, dy)


def mixer_kernel(
    mixer_ref, gate_ref, delta_ref, b_ref, c_ref, taps_ref, bias_ref, delta_bias_ref, decay_ref,
    gain_ref, prefix_ref, tail_ref, weight_ref, residual_ref,
    out_ref, squares_ref,
    rim, padded, act, step, drive, summed, b_wide, c_wide, ends, spans, line_ends, line_spans,
    rows_all, weight, parts, got, landed, home,
    rim_sems, end_sems, gather_sems, pair_sems, sum_send_sems, sum_sems, weight_sem,
):
    torus = Torus()
    me, index = torus.me, torus.index
    x, y = torus.place
    own = lax.axis_index("exp")
    z, core = own // 2, own % 2
    count = SIDE * SIDE
    tokens, channels = mixer_ref.shape
    strips = channels // STRIP
    f32 = jnp.float32

    def strip_lanes(strip):
        return pl.ds(pl.multiple_of(strip * STRIP, STRIP), STRIP)

    load = pltpu.make_async_copy(weight_ref, weight, weight_sem)
    load.start()
    barrier = pltpu.get_barrier_semaphore()
    for k in range(1, count):
        pl.semaphore_signal(
            barrier, inc=1, device_id={"ctx": lax.rem(me + k, count)}, device_id_type=MESH
        )
    for k in range(1, EXPERTS):
        pl.semaphore_signal(
            barrier, inc=1, device_id={"exp": lax.rem(own + k, EXPERTS)}, device_id_type=MESH
        )
    pl.semaphore_wait(barrier, count - 1 + EXPERTS - 1)

    def rim_copy(target):
        return pltpu.make_async_remote_copy(
            src_ref=mixer_ref.at[pl.ds(tokens - 16, 16), :],
            dst_ref=rim,
            send_sem=rim_sems.at[0],
            recv_sem=rim_sems.at[1],
            device_id={"ctx": target},
            device_id_type=MESH,
        )

    @pl.when(me < count - 1)
    def _():
        rim_copy(me + 1).start()

    for t in range(tokens):
        b_wide[t] = jnp.broadcast_to(b_ref[:, t : t + 1], (STATES, LANES))
        c_wide[t] = jnp.broadcast_to(c_ref[:, t : t + 1], (STATES, LANES))

    def find_step(strip, carry):
        lanes = strip_lanes(strip)
        value = jnp.log(1.0 + jnp.exp(delta_ref[:, lanes].astype(f32) + delta_bias_ref[:, lanes]))
        step[:, lanes] = value
        spans[0, :, lanes] = jnp.sum(value, axis=0, keepdims=True)
        return carry

    lax.fori_loop(0, strips, find_step, 0)

    @pl.when(me > 0)
    def _():
        rim_copy(me).wait_recv()

    @pl.when(me == 0)
    def _():
        rim[...] = jnp.zeros_like(rim)

    def rates(lanes):
        return -jnp.exp(decay_ref[:, lanes]) * LOG2E

    def advance(rate, state, steps, drives, i, b_column):
        return tuple(
            jnp.exp2(r * s) * h + b_column * d
            for r, s, h, d in zip(
                rate, lane_parts(steps[i : i + 1]), state, lane_parts(drives[i : i + 1])
            )
        )

    def prepare(strip, carry):
        lanes = strip_lanes(strip)
        padded[0:8] = rim[:, lanes].astype(f32)[8:16]
        padded[8 : 8 + tokens] = mixer_ref[:, lanes].astype(f32)

        @pl.when(me == 0)
        def _():
            padded[5:8] = tail_ref[:, lanes].astype(f32)

        convolved = bias_ref[:, lanes]
        for k in range(4):
            convolved = convolved + taps_ref[k : k + 1, lanes] * padded[5 + k : 5 + k + tokens]
        value = convolved / (1.0 + jnp.exp(-convolved))
        act[:, lanes] = value
        drive[:, lanes] = value * step[:, lanes]
        rate = lane_parts(rates(lanes))

        def group(number, state):
            base = pl.multiple_of(number * 8, 8)
            steps, drives = step[pl.ds(base, 8), lanes], drive[pl.ds(base, 8), lanes]
            for i in range(8):
                state = advance(rate, state, steps, drives, i, b_wide[base + i])
            return state

        zero = jnp.zeros((STATES, LANES), f32)
        state = lax.fori_loop(0, tokens // 8, group, (zero,) * (STRIP // LANES))
        ends[0, :, lanes] = jnp.concatenate(state, axis=1).astype(ends.dtype)
        return carry

    half_channels = channels // 2
    per_half = strips // 2

    def end_copies(stage, half, k, place, target):
        lanes = pl.ds(half * half_channels, half_channels)
        pairs = ((ends, line_ends), (spans, line_spans))
        return [
            pltpu.make_async_remote_copy(
                src_ref=mine.at[stage, :, lanes],
                dst_ref=whole.at[stage, place, :, lanes],
                send_sem=end_sems.at[0, stage, half, k - 1, part],
                recv_sem=end_sems.at[1, stage, half, k - 1, part],
                device_id={"ctx": target},
                device_id_type=MESH,
            )
            for part, (mine, whole) in enumerate(pairs)
        ]

    def follow(stage, strip):
        lanes = strip_lanes(strip)

        def one(source, state):
            return (
                jnp.exp2(rates(lanes) * line_spans[stage, source, :, lanes]) * state
                + line_ends[stage, source, :, lanes].astype(f32)
            )

        return one

    def line_end(half, number, carry):
        strip = half * per_half + number
        lanes = strip_lanes(strip)
        state = lax.fori_loop(0, SIDE, follow(0, strip), jnp.zeros((STATES, STRIP), f32))
        ends[1, :, lanes] = state.astype(ends.dtype)
        spans[1, :, lanes] = sum(line_spans[0, source, :, lanes] for source in range(SIDE))
        return carry

    leaving = []
    for half in (0, 1):
        lax.fori_loop(half * per_half, (half + 1) * per_half, prepare, 0)
        lanes = pl.ds(half * half_channels, half_channels)
        for k in range(1, SIDE):
            leaving += end_copies(0, half, k, y, index(0, 0, k))
            for one in leaving[-2:]:
                one.start()
        line_ends[0, y, :, lanes] = ends[0, :, lanes]
        line_spans[0, y, :, lanes] = spans[0, :, lanes]
    for half in (0, 1):
        for k in range(1, SIDE):
            for one in end_copies(0, half, k, lax.rem(y + SIDE - k, SIDE), me):
                one.wait_recv()
        lax.fori_loop(0, per_half, functools.partial(line_end, half), 0)
        for k in range(1, SIDE):

            @pl.when(x + k < SIDE)
            def _():
                for one in end_copies(1, half, k, x, (x + k) * SIDE + y):
                    one.start()

    in_flight = []

    def moved(half, line, kind, first, second, part, towards, target):
        def rows(a, b):
            where = (a, b) if half == 0 else (b, a)
            where = tuple((v + 1) % SIDE - 1 for v in where)
            start, size = (0, tokens) if part is None else (part * (tokens // 2), tokens // 2)
            return rows_all.at[half, pl.ds(SLOTS.index(where) * tokens + start, size), :]

        return pltpu.make_async_remote_copy(
            src_ref=rows(first, second),
            dst_ref=rows(first - towards[0], second - towards[1]),
            send_sem=gather_sems.at[0, half, line, kind],
            recv_sem=gather_sems.at[1, half, line, kind],
            device_id={"ctx": target},
            device_id_type=MESH,
        )

    def send(half, line, kind, first, second, part, towards):
        one = moved(half, line, kind, first, second, part, towards, index(half, *towards))
        one.start()
        in_flight.append(one)

    def arrived(half, line, kind, first, second, part):
        moved(half, line, kind, first, second, part, (0, 0), me).wait_recv()

    def send_line(half, first):
        send(half, LINES[first], 0, first, 0, None, (0, 1))
        send(half, LINES[first], 1, first, 0, None, (0, -1))

    def pass_on(half, first):
        arrived(half, LINES[first], 0, first, -1, None)
        send(half, LINES[first], 2, first, -1, 0, (0, 1))
        arrived(half, LINES[first], 1, first, 1, None)
        send(half, LINES[first], 3, first, 1, 1, (0, -1))

    def last_of(half, first):
        arrived(half, LINES[first], 2, first, 2, 0)
        arrived(half, LINES[first], 3, first, 2, 1)

    def scan(half, strip, carry):
        lanes = strip_lanes(half * per_half + strip)
        rate = lane_parts(rates(lanes))
        state = prefix_ref[:, lanes]
        state = lax.fori_loop(0, x, follow(1, half * per_half + strip), state)
        state = lax.fori_loop(0, y, follow(0, half * per_half + strip), state)

        def group(number, state):
            base = pl.multiple_of(number * 8, 8)
            steps, drives = step[pl.ds(base, 8), lanes], drive[pl.ds(base, 8), lanes]
            found = []
            for i in range(8):
                state = advance(rate, state, steps, drives, i, b_wide[base + i])
                c_column = c_wide[base + i]
                found.append(
                    jnp.concatenate(
                        [jnp.sum(c_column * h, axis=0, keepdims=True) for h in state], axis=1
                    )
                )
            summed[pl.ds(base, 8), :] = jnp.concatenate(found, axis=0)
            return state

        lax.fori_loop(0, tokens // 8, group, lane_parts(state))
        gate = gate_ref[:, lanes].astype(f32)
        mixed = summed[...] + gain_ref[:, lanes] * act[:, lanes]
        rows_all[half, 0:tokens, strip_lanes(strip)] = (
            mixed * (gate / (1.0 + jnp.exp(-gate)))
        ).astype(rows_all.dtype)
        return carry

    for half in (0, 1):
        for k in range(1, SIDE):

            @pl.when(x >= k)
            def _():
                for one in end_copies(1, half, k, x - k, me):
                    one.wait_recv()

        lax.fori_loop(0, per_half, functools.partial(scan, half), 0)
        send(half, RING, 0, 0, 0, None, (1, 0))
        send(half, RING, 1, 0, 0, None, (-1, 0))
        send_line(half, 0)

    width = weight.shape[1]
    sibling = own + 1 - 2 * core

    def of_slot(where, number):
        dx, dy = where(number)
        line = lax.rem(y + dy + SIDE, SIDE)
        return lax.rem(x + dx + SIDE, SIDE), line // 2, line % 2

    def pair_copy(slot, target):
        return pltpu.make_async_remote_copy(
            src_ref=parts.at[slot],
            dst_ref=got.at[slot],
            send_sem=pair_sems.at[0, slot],
            recv_sem=pair_sems.at[1, slot],
            device_id={"exp": target},
            device_id_type=MESH,
        )

    def part_rows(part):
        return pl.ds(pl.multiple_of(part * tokens, tokens), tokens)

    def sum_copy(slot, column, part):
        behind = lax.rem(column - z + SIDE, SIDE) - 1
        return pltpu.make_async_remote_copy(
            src_ref=parts.at[slot],
            dst_ref=landed.at[behind, part_rows(part), :],
            send_sem=sum_send_sems.at[slot],
            recv_sem=sum_sems.at[behind, part],
            device_id={"exp": column * 2 + core},
            device_id_type=MESH,
        )

    def project(where, number, first_slot):
        together = min(number, 2)

        def one(pair, carry):
            first = first_slot + pair * together
            rows = pl.ds(pl.multiple_of(first * tokens, tokens), together * tokens)
            value = jnp.dot(
                rows_all[0, rows, :], weight[0:half_channels], preferred_element_type=f32
            ) + jnp.dot(
                rows_all[1, rows, :], weight[half_channels:], preferred_element_type=f32
            )
            for k in range(together):
                column, owner, part = of_slot(where, pair * together + k)
                parts[first + k] = value[k * tokens : (k + 1) * tokens].astype(parts.dtype)

                @pl.when(owner != core)
                def _():
                    pair_copy(first + k, sibling).start()

            return carry

        lax.fori_loop(0, number // together, one, 0)

    def settle(where, number, first_slot):
        def one(k, carry):
            slot = first_slot + k
            column, owner, part = of_slot(where, k)

            @pl.when(owner == core)
            def _():
                pair_copy(slot, own).wait_recv()
                value = parts[slot].astype(f32) + got[slot].astype(f32)

                @pl.when(column == z)
                def _():
                    home[part_rows(part), :] = value

                @pl.when(column != z)
                def _():
                    parts[slot] = value.astype(parts.dtype)
                    sum_copy(slot, column, part).start()

            return carry

        lax.fori_loop(0, number, one, 0)

    def clear(where, number, first_slot):
        def one(k, carry):
            slot = first_slot + k
            column, owner, part = of_slot(where, k)

            @pl.when(owner != core)
            def _():
                pair_copy(slot, sibling).wait_send()

            @pl.when((owner == core) & (column != z))
            def _():
                sum_copy(slot, column, part).wait_send()

            return carry

        lax.fori_loop(0, number, one, 0)

    load.wait()
    project(single(0, 0), 1, 0)
    for half in (0, 1):
        arrived(half, RING, 0, -1, 0, None)
        send(half, RING, 2, -1, 0, 0, (1, 0))
        arrived(half, RING, 1, 1, 0, None)
        send(half, RING, 3, 1, 0, 1, (-1, 0))
        send_line(half, -1)
        send_line(half, 1)
    for half in (0, 1):
        pass_on(half, 0)
    project(beside, 4, 1)
    settle(single(0, 0), 1, 0)
    for half in (0, 1):
        arrived(half, RING, 2, 2, 0, 0)
        arrived(half, RING, 3, 2, 0, 1)
        send_line(half, 2)
    for half in (0, 1):
        last_of(half, 0)
    project(across_ring, 2, 5)
    settle(beside, 4, 1)
    for first in (-1, 1):
        for half in (0, 1):
            pass_on(half, first)
    project(corner, 4, 7)
    settle(across_ring, 2, 5)
    for half in (0, 1):
        pass_on(half, 2)
    for first in (-1, 1):
        for half in (0, 1):
            last_of(half, first)
    project(knight, 4, 11)
    settle(corner, 4, 7)
    for half in (0, 1):
        last_of(half, 2)
    project(single(2, 2), 1, 15)
    settle(knight, 4, 11)

    settle(single(2, 2), 1, 15)
    value = home[...] + residual_ref[...].astype(f32)
    for behind in range(SIDE - 1):
        for part in (0, 1):
            rows = pl.ds(part * tokens, tokens)
            pltpu.make_async_remote_copy(
                src_ref=landed.at[behind, rows, :],
                dst_ref=landed.at[behind, rows, :],
                send_sem=sum_send_sems.at[0],
                recv_sem=sum_sems.at[behind, part],
                device_id={"exp": own},
                device_id_type=MESH,
            ).wait_recv()
        value = value + landed[behind].astype(f32)
    value = value.astype(out_ref.dtype)
    out_ref[...] = value
    value = value.astype(f32)
    value = value * value
    ones = jnp.ones((16, width), jnp.bfloat16)
    found = jnp.zeros((16, value.shape[0]), f32)
    for _ in range(3):
        term = value.astype(jnp.bfloat16)
        value = value - term.astype(f32)
        found = found + lax.dot_general(
            ones, term, (((1,), (1,)), ((), ())), preferred_element_type=f32
        )
    squares_ref[...] = found[0:8]

    @pl.when(me < count - 1)
    def _():
        rim_copy(me + 1).wait_send()

    for half in (0, 1):
        for k in range(1, SIDE):

            @pl.when(x + k < SIDE)
            def _():
                for one in end_copies(1, half, k, x, (x + k) * SIDE + y):
                    one.wait_send()

    clear(single(0, 0), 1, 0)
    clear(beside, 4, 1)
    clear(across_ring, 2, 5)
    clear(corner, 4, 7)
    clear(knight, 4, 11)
    clear(single(2, 2), 1, 15)
    for one in in_flight + leaving:
        one.wait_send()


def mixer(
    mixer_in, gate_in, delta_in, b_proj, c_proj, conv_kernel, conv_bias, delta_bias, decay_log,
    skip_gain, prefix_state, prefix_tail, out_proj, residual,
):
    tokens, channels = mixer_in.shape
    rows, width = residual.shape
    count = SIDE * SIDE
    here = pl.BlockSpec(memory_space=pltpu.VMEM)
    away = pl.BlockSpec(memory_space=pl.ANY)
    bf16, f32 = jnp.bfloat16, jnp.float32
    return pl.pallas_call(
        mixer_kernel,
        out_shape=(
            jax.ShapeDtypeStruct((rows, width), bf16),
            jax.ShapeDtypeStruct((8, rows), f32),
        ),
        in_specs=[here] * 12 + [away, here],
        out_specs=(here, here),
        scratch_shapes=[
            pltpu.VMEM((16, channels), bf16),
            pltpu.VMEM((8 + tokens, STRIP), f32),
            pltpu.VMEM((tokens, channels), f32),
            pltpu.VMEM((tokens, channels), f32),
            pltpu.VMEM((tokens, channels), f32),
            pltpu.VMEM((tokens, STRIP), f32),
            pltpu.VMEM((tokens, STATES, LANES), f32),
            pltpu.VMEM((tokens, STATES, LANES), f32),
            pltpu.VMEM((2, STATES, channels), bf16),
            pltpu.VMEM((2, 1, channels), f32),
            pltpu.VMEM((2, SIDE, STATES, channels), bf16),
            pltpu.VMEM((2, SIDE, 1, channels), f32),
            pltpu.VMEM((2, count * tokens, channels // 2), bf16),
            pltpu.VMEM((channels, width), bf16),
            pltpu.VMEM((count, tokens, width), bf16),
            pltpu.VMEM((count, tokens, width), bf16),
            pltpu.VMEM((SIDE - 1, rows, width), bf16),
            pltpu.VMEM((rows, width), f32),
            pltpu.SemaphoreType.DMA((2,)),
            pltpu.SemaphoreType.DMA((2, 2, 2, SIDE - 1, 2)),
            pltpu.SemaphoreType.DMA((2, 2, 5, 4)),
            pltpu.SemaphoreType.DMA((2, count)),
            pltpu.SemaphoreType.DMA((count,)),
            pltpu.SemaphoreType.DMA((SIDE - 1, 2)),
            pltpu.SemaphoreType.DMA,
        ],
        compiler_params=pltpu.CompilerParams(
            collective_id=1, has_side_effects=True, vmem_limit_bytes=56 * 1024 * 1024
        ),
        name="mixer",
    )(
        mixer_in, gate_in, delta_in, b_proj, c_proj, conv_kernel, conv_bias[None], delta_bias[None],
        decay_log, skip_gain[None], prefix_state, prefix_tail, out_proj, residual,
    )


def expert_kernel(
    capacity, features,
    mixer_ref, squares_ref, ids_ref, route_ref, gain_ref, gate_ref, up_ref, down_ref,
    out_ref,
    blocks, landed, wide, down, total, hidden, outgoing, answer, returned, all_squares, pick_all, routing,
    square_sems, dispatch_sems, return_sems, gather_sems, sum_sems, weight_sems,
):
    torus = Torus()
    me, index = torus.me, torus.index
    own_expert = lax.axis_index("exp")
    slots, width = answer.shape
    units = down.shape[0]
    count = SIDE * SIDE

    weights = [
        pltpu.make_async_copy(gate_ref.at[0], wide.at[:, pl.ds(0, units)], weight_sems.at[0]),
        pltpu.make_async_copy(up_ref.at[0], wide.at[:, pl.ds(units, units)], weight_sems.at[1]),
        pltpu.make_async_copy(down_ref.at[0], down, weight_sems.at[2]),
    ]
    for one in weights:
        one.start()

    barrier = pltpu.get_barrier_semaphore()
    for k in range(1, count):
        pl.semaphore_signal(
            barrier, inc=1, device_id={"ctx": lax.rem(me + k, count)}, device_id_type=MESH
        )
    for k in range(1, EXPERTS):
        pl.semaphore_signal(
            barrier, inc=1, device_id={"exp": lax.rem(own_expert + k, EXPERTS)}, device_id_type=MESH
        )

    tokens = mixer_ref.shape[0]
    z, core = own_expert // 2, own_expert % 2

    def at_peer(number, way):
        dz, dc = PEERS[number]
        other = core + dc - 2 * core * dc
        return lax.rem(z + way * dz + 2 * SIDE, SIDE) * 2 + other

    experts_wide = lax.broadcasted_iota(jnp.int32, (16, tokens), 0)
    named, gates_wide = jnp.zeros((16, tokens), jnp.float32), jnp.zeros((16, tokens), jnp.float32)
    for k in range(ids_ref.shape[0]):
        here = ids_ref[k : k + 1, :] == experts_wide
        named = jnp.where(here, 1.0, named)
        gates_wide = jnp.where(here, route_ref[k : k + 1, :], gates_wide)
    before = lax.broadcasted_iota(jnp.int32, (tokens, tokens), 0)
    after = lax.broadcasted_iota(jnp.int32, (tokens, tokens), 1)
    routing[0] = named[0:EXPERTS]
    routing[1] = jnp.dot(
        named.astype(jnp.bfloat16),
        (before < after).astype(jnp.float32).astype(jnp.bfloat16),
        preferred_element_type=jnp.float32,
    )[0:EXPERTS]
    first = lax.broadcasted_iota(jnp.int32, (16, LANES), 0)
    second = lax.broadcasted_iota(jnp.int32, (16, LANES), 1)
    turn = (first == second).astype(jnp.float32).astype(jnp.bfloat16)
    gates = jnp.zeros((tokens, LANES), jnp.float32)
    for _ in range(3):
        term = gates_wide.astype(jnp.bfloat16)
        gates_wide = gates_wide - term.astype(jnp.float32)
        gates = gates + lax.dot_general(
            term, turn, (((0,), (0,)), ((), ())), preferred_element_type=jnp.float32
        )

    for number in range(len(PEERS)):
        expert = pl.ds(at_peer(number, 1), 1)
        slot = lax.broadcasted_iota(jnp.int32, (capacity, tokens), 0).astype(jnp.float32)
        chosen = (routing[1, expert, :] == slot) & (routing[0, expert, :] > 0.5)
        pick_all[number * capacity : (number + 1) * capacity, :] = chosen.astype(
            jnp.float32
        ).astype(jnp.bfloat16)
    pl.semaphore_wait(barrier, count - 1 + EXPERTS - 1)

    square_copies = []
    for k in range(1, count):
        square_copies.append(
            pltpu.make_async_remote_copy(
                src_ref=squares_ref,
                dst_ref=all_squares.at[me],
                send_sem=square_sems.at[0, k - 1],
                recv_sem=square_sems.at[1, k - 1],
                device_id={"ctx": lax.rem(me + k, count)},
                device_id_type=MESH,
            )
        )
        square_copies[-1].start()
    all_squares[me] = squares_ref[...]
    for k in range(1, count):
        source = lax.rem(me + count - k, count)
        pltpu.make_async_remote_copy(
            src_ref=squares_ref,
            dst_ref=all_squares.at[source],
            send_sem=square_sems.at[0, k - 1],
            recv_sem=square_sems.at[1, k - 1],
            device_id={"ctx": me},
            device_id_type=MESH,
        ).wait_recv()
    scale = lax.rsqrt(jnp.sum(all_squares[...], axis=0)[0:1] / features + 1e-05)

    def pick(chunk, carry):
        rows = pl.ds(pl.multiple_of(chunk * capacity, 16), capacity)
        chosen = pick_all[rows, :]
        picked = jnp.dot(chosen, mixer_ref[...], preferred_element_type=jnp.float32)
        chosen = chosen.astype(jnp.float32)
        row_scale = jnp.sum(chosen * scale, axis=1, keepdims=True)
        outgoing[rows, :] = (picked * row_scale * gain_ref[...]).astype(outgoing.dtype)
        return carry

    lax.fori_loop(0, EXPERTS, pick, 0)

    def rows_of(number):
        return pl.ds(number * capacity, capacity)

    def dispatch(number, target):
        return pltpu.make_async_remote_copy(
            src_ref=outgoing.at[rows_of(number), :],
            dst_ref=blocks.at[me, rows_of(number), :],
            send_sem=dispatch_sems.at[0, number],
            recv_sem=dispatch_sems.at[1, number],
            device_id={"exp": target},
            device_id_type=MESH,
        )

    crossing = [dispatch(n, at_peer(n, 1)) for n in (5, 6, 7, 0, 1, 2, 3)]
    for one in crossing:
        one.start()
    blocks[me, rows_of(OWN), :] = outgoing[rows_of(OWN), :]

    in_flight = {}

    def moved(unit, line, kind, first, second, part, target):
        half = unit % 2
        start, size = span(slots, unit, part)
        ref = blocks.at[index(half, first, second), pl.ds(start, size), :]
        return pltpu.make_async_remote_copy(
            src_ref=ref,
            dst_ref=ref,
            send_sem=gather_sems.at[0, unit, line, kind],
            recv_sem=gather_sems.at[1, unit, line, kind],
            device_id={"ctx": target},
            device_id_type=MESH,
        )

    def send(unit, line, kind, first, second, part, towards):
        one = moved(unit, line, kind, first, second, part, index(unit % 2, *towards))
        one.start()
        where = (first, second) if unit % 2 == 0 else (second, first)
        in_flight.setdefault((unit // 2,) + where, []).append(one)

    def arrived(unit, line, kind, first, second, part):
        moved(unit, line, kind, first, second, part, me).wait_recv()

    def send_line(unit, first):
        send(unit, LINES[first], 0, first, 0, None, (0, 1))
        send(unit, LINES[first], 1, first, 0, None, (0, -1))

    def pass_on(unit, first):
        arrived(unit, LINES[first], 0, first, -1, None)
        send(unit, LINES[first], 2, first, -1, 0, (0, 1))
        arrived(unit, LINES[first], 1, first, 1, None)
        send(unit, LINES[first], 3, first, 1, 1, (0, -1))

    def last_of(unit, first):
        arrived(unit, LINES[first], 2, first, 2, 0)
        arrived(unit, LINES[first], 3, first, 2, 1)

    def open_unit(unit):
        for number in (2 * unit, 2 * unit + 1):
            if number != OWN:
                dispatch(number, own_expert).wait_recv()
        send(unit, RING, 0, 0, 0, None, (1, 0))
        send(unit, RING, 1, 0, 0, None, (-1, 0))
        send_line(unit, 0)

    def ring_one(unit):
        arrived(unit, RING, 0, -1, 0, None)
        send(unit, RING, 2, -1, 0, 0, (1, 0))
        arrived(unit, RING, 1, 1, 0, None)
        send(unit, RING, 3, 1, 0, 1, (-1, 0))
        send_line(unit, -1)
        send_line(unit, 1)
        pass_on(unit, 0)

    def ring_two(unit):
        arrived(unit, RING, 2, 2, 0, 0)
        arrived(unit, RING, 3, 2, 0, 1)
        send_line(unit, 2)
        last_of(unit, 0)

    def lines_one(unit):
        pass_on(unit, -1)
        pass_on(unit, 1)

    def lines_two(unit):
        pass_on(unit, 2)
        last_of(unit, -1)
        last_of(unit, 1)

    row_tile = slots // 2

    def over_blocks(group, where, number, body):
        rows = pl.ds(group * row_tile, row_tile)

        def one(block, carry):
            body(index(0, *where(block)), rows)
            return carry

        lax.fori_loop(0, number, one, 0)

    def grow(owner, rows):
        part = wide[pl.ds(pl.multiple_of(owner * width, 16), width), :]
        total[rows, :] += jnp.dot(blocks[owner, rows, :], part, preferred_element_type=jnp.float32)

    open_unit(2)
    open_unit(3)
    total[...] = jnp.zeros_like(total)
    open_unit(0)
    ring_one(2)
    ring_one(3)
    open_unit(1)
    for one in weights:
        one.wait()
    over_blocks(1, single(0, 0), 1, grow)
    over_blocks(1, beside, 4, grow)
    for unit in (2, 3):
        ring_two(unit)
    ring_one(0)
    ring_one(1)
    over_blocks(0, single(0, 0), 1, grow)
    over_blocks(1, across_ring, 2, grow)
    for unit in (2, 3):
        lines_one(unit)
    over_blocks(0, beside, 4, grow)
    for unit in (0, 1):
        ring_two(unit)
    for unit in (2, 3):
        lines_two(unit)
    over_blocks(1, corner, 4, grow)
    over_blocks(0, across_ring, 2, grow)
    for unit in (0, 1):
        lines_one(unit)
    over_blocks(1, knight, 4, grow)
    for unit in (2, 3):
        last_of(unit, 2)
    over_blocks(1, single(2, 2), 1, grow)
    over_blocks(0, corner, 4, grow)
    for unit in (0, 1):
        lines_two(unit)
    over_blocks(0, knight, 4, grow)
    for unit in (0, 1):
        last_of(unit, 2)
    over_blocks(0, single(2, 2), 1, grow)

    def activate(group):
        def one(step, carry):
            rows = pl.ds(pl.multiple_of(group * row_tile + step * capacity, 16), capacity)
            gate = total[rows, 0:units]
            hidden[rows, :] = (
                gate / (1.0 + jnp.exp(-gate)) * total[rows, units : 2 * units]
            ).astype(hidden.dtype)
            return carry

        lax.fori_loop(0, row_tile // capacity, one, 0)

    def project(owner, rows):
        part = down[:, pl.ds(pl.multiple_of(owner * width, LANES), width)]
        blocks[owner, rows, :] = jnp.dot(
            hidden[rows, :], part, preferred_element_type=jnp.float32
        ).astype(blocks.dtype)

    def fill(group, where, number):
        for block in range(number):
            for one in in_flight.pop((group,) + where(block), ()):
                one.wait_send()
        over_blocks(group, where, number, project)

    summing = []

    def part_rows(unit, part):
        start, size = span(slots, unit, part)
        return pl.ds(start, size)

    def landing(unit, line, kind):
        if kind < 2:
            return landed.at[unit, line, kind]
        size = span(slots, unit, 0)[1]
        return landed.at[unit, line, 2, pl.ds((kind - 2) * size, size), :]

    def sum_copy(unit, line, kind, first, second, part, target):
        return pltpu.make_async_remote_copy(
            src_ref=blocks.at[index(unit % 2, first, second), part_rows(unit, part), :],
            dst_ref=landing(unit, line, kind),
            send_sem=sum_sems.at[0, unit, line, kind],
            recv_sem=sum_sems.at[1, unit, line, kind],
            device_id={"ctx": target},
            device_id_type=MESH,
        )

    def give(unit, line, kind, first, second, part):
        step = 1 if kind % 2 == 0 else -1
        half = unit % 2
        target = index(half, step, 0) if line == RING else index(half, 0, step)
        one = sum_copy(unit, line, kind, first, second, part, target)
        one.start()
        summing.append(one)

    def taken(unit, line, kind):
        part = None if kind < 2 else kind - 2
        sum_copy(unit, line, kind, 0, 0, part, me).wait_recv()

    def add(unit, first, second, part, line, kinds):
        for kind in kinds:
            taken(unit, line, kind)
        owner = index(unit % 2, first, second)
        start, size = span(slots, unit, part)

        def one(step, carry):
            offset = pl.multiple_of(step * capacity, 16)
            rows = pl.ds(pl.multiple_of(start + offset, 16), capacity)
            value = blocks[owner, rows, :].astype(jnp.float32)
            for kind in kinds:
                value = value + landing(unit, line, kind)[pl.ds(offset, capacity), :].astype(
                    jnp.float32
                )
            blocks[owner, rows, :] = value.astype(blocks.dtype)
            return carry

        lax.fori_loop(0, size // capacity, one, 0)

    def at(line, offset):
        return (offset, 0) if line == RING else ({v: k for k, v in LINES.items()}[line], offset)

    def begin(unit, line):
        give(unit, line, 2, *at(line, 2), 0)
        give(unit, line, 3, *at(line, 2), 1)

    def middle(unit, line):
        add(unit, *at(line, 1), 0, line, (2,))
        give(unit, line, 0, *at(line, 1), None)
        add(unit, *at(line, -1), 1, line, (3,))
        give(unit, line, 1, *at(line, -1), None)

    def finish(unit, line):
        add(unit, *at(line, 0), None, line, (0, 1))

    def back(number, target):
        return pltpu.make_async_remote_copy(
            src_ref=answer.at[rows_of(number), :],
            dst_ref=returned.at[rows_of(number), :],
            send_sem=return_sems.at[0, number],
            recv_sem=return_sems.at[1, number],
            device_id={"exp": target},
            device_id_type=MESH,
        )

    def hand_back(unit):
        for kind in (0, 1):
            taken(unit, RING, kind)
        owner = index(0, 0, 0)
        for step in (0, 1):
            number = 2 * unit + step
            rows = rows_of(number)
            there = pl.ds(step * capacity, capacity)
            value = blocks[owner, rows, :].astype(jnp.float32)
            for kind in (0, 1):
                value = value + landed[unit, RING, kind, there, :].astype(jnp.float32)
            if number == OWN:
                returned[rows, :] = value.astype(returned.dtype)
            else:
                answer[rows, :] = value.astype(answer.dtype)
                one = back(number, at_peer(number, -1))
                one.start()
                summing.append(one)

    def start_lines(group):
        units = (2 * group, 2 * group + 1)
        fill(group, single(2, 2), 1)
        for unit in units:
            begin(unit, LINES[2])
        fill(group, knight, 4)
        for first in (1, -1):
            for unit in units:
                begin(unit, LINES[first])
        fill(group, across_ring, 2)
        for unit in units:
            begin(unit, LINES[0])

    def middle_lines(group):
        units = (2 * group, 2 * group + 1)
        for unit in units:
            middle(unit, LINES[2])
        fill(group, corner, 4)
        for first in (1, -1):
            for unit in units:
                middle(unit, LINES[first])
        fill(group, beside, 4)
        for unit in units:
            middle(unit, LINES[0])

    def finish_lines(group):
        units = (2 * group, 2 * group + 1)
        fill(group, single(0, 0), 1)
        for unit in units:
            finish(unit, LINES[2])
            begin(unit, RING)
        for first in (1, -1):
            for unit in units:
                finish(unit, LINES[first])
        for unit in units:
            middle(unit, RING)
        for unit in units:
            finish(unit, LINES[0])

    activate(0)
    start_lines(0)
    activate(1)
    middle_lines(0)
    for one in crossing:
        one.wait_send()
    start_lines(1)
    finish_lines(0)
    middle_lines(1)
    for unit in (1, 0):
        hand_back(unit)
    finish_lines(1)
    for unit in (3, 2):
        hand_back(unit)

    lane = lax.broadcasted_iota(jnp.int32, (tokens, LANES), 1)

    def mixed(number):
        rows = rows_of(number)
        gate = jnp.sum(jnp.where(lane == at_peer(number, 1), gates, 0.0), axis=1, keepdims=True)
        return gate * lax.dot_general(
            pick_all[rows, :],
            returned[rows, :],
            (((0,), (0,)), ((), ())),
            preferred_element_type=jnp.float32,
        )

    value = mixer_ref[...].astype(jnp.float32) + mixed(OWN)
    for number in (2, 3, 0, 1, 5, 6, 7):
        back(number, own_expert).wait_recv()
        value = value + mixed(number)
    out_ref[...] = value.astype(out_ref.dtype)
    for one in summing + square_copies:
        one.wait_send()


def expert_layer(
    mixer_out, squares, ids, route_gates, gain, expert_gate, expert_up, expert_down, capacity
):
    rows, width = mixer_out.shape
    features, units = expert_gate.shape[1:]
    slots = EXPERTS * capacity
    count = SIDE * SIDE
    here = pl.BlockSpec(memory_space=pltpu.VMEM)
    away = pl.BlockSpec(memory_space=pl.ANY)
    bf16, f32 = jnp.bfloat16, jnp.float32
    return pl.pallas_call(
        functools.partial(expert_kernel, capacity, features),
        out_shape=jax.ShapeDtypeStruct((rows, width), bf16),
        in_specs=[here] * 5 + [away] * 3,
        out_specs=here,
        scratch_shapes=[
            pltpu.VMEM((count, slots, width), bf16),
            pltpu.VMEM((len(UNITS), 5, 3, slots // len(UNITS), width), bf16),
            pltpu.VMEM((features, 2 * units), bf16),
            pltpu.VMEM((units, features), bf16),
            pltpu.VMEM((slots, 2 * units), f32),
            pltpu.VMEM((slots, units), bf16),
            pltpu.VMEM((slots, width), bf16),
            pltpu.VMEM((slots, width), bf16),
            pltpu.VMEM((slots, width), bf16),
            pltpu.VMEM((count,) + squares.shape, f32),
            pltpu.VMEM((slots, rows), bf16),
            pltpu.VMEM((2, EXPERTS, rows), f32),
            pltpu.SemaphoreType.DMA((2, count - 1)),
            pltpu.SemaphoreType.DMA((2, EXPERTS)),
            pltpu.SemaphoreType.DMA((2, EXPERTS)),
            pltpu.SemaphoreType.DMA((2, len(UNITS), 5, 4)),
            pltpu.SemaphoreType.DMA((2, len(UNITS), 5, 4)),
            pltpu.SemaphoreType.DMA((3,)),
        ],
        compiler_params=pltpu.CompilerParams(
            collective_id=3, has_side_effects=True, vmem_limit_bytes=56 * 1024 * 1024
        ),
        name="expert_layer",
    )(mixer_out, squares, ids, route_gates, gain, expert_gate, expert_up, expert_down)


def shards(
    mixer_in,
    gate_in,
    delta_in,
    b_proj,
    c_proj,
    conv_kernel,
    conv_bias,
    delta_bias,
    decay_log,
    skip_gain,
    prefix_state,
    prefix_tail,
    out_proj,
    residual,
    norm_gain,
    expert_gate,
    expert_up,
    expert_down,
    expert_ids,
    route_gates,
):
    mixer_out, squares = mixer(
        mixer_in, gate_in, delta_in, b_proj, c_proj, conv_kernel, conv_bias, delta_bias, decay_log,
        skip_gain, prefix_state, prefix_tail, out_proj, residual,
    )
    block_rows = residual.shape[0]
    experts = expert_gate.shape[0] * lax.axis_size("exp")
    top_count = expert_ids.shape[1]
    capacity = 3 * block_rows * top_count // (2 * experts)
    block_out = expert_layer(
        mixer_out, squares, expert_ids.T, route_gates.T, norm_gain[None],
        expert_gate, expert_up, expert_down, capacity,
    )
    return (mixer_out, block_out)


def solution(mesh):
    placed = (
        P("ctx", "exp"),
        P("ctx", "exp"),
        P("ctx", "exp"),
        P(None, "ctx"),
        P(None, "ctx"),
        P(None, "exp"),
        P("exp"),
        P("exp"),
        P(None, "exp"),
        P("exp"),
        P(None, "exp"),
        P(None, "exp"),
        P("exp", "ctx"),
        P("exp", "ctx"),
        P("ctx"),
        P("exp", None, "ctx"),
        P("exp", None, "ctx"),
        P("exp", "ctx", None),
        P("exp", None),
        P("exp", None),
    )
    return jax.shard_map(
        shards,
        mesh=mesh,
        in_specs=placed,
        out_specs=(P("exp", "ctx"), P("exp", "ctx")),
        check_vma=False,
    )
```

time: 272 us -> 251 us (0.923)
  Pallas kernels: 262 us -> 248 us
  other arithmetic: 4.15 us -> 0 us
  local copies, waits for them, and re-layouts: 5.37 us -> 2.38 us
    pallas_call x1, Pallas kernels: 88.4 us -> 79.9 us  [mixer(): pl.pallas_call(mixer_kernel, out_shape=(jax.ShapeDtypeStruct((rows, width...]
    pallas_call x1, Pallas kernels: 173 us -> 168 us  [expert_layer(): pl.pallas_call(functools.partial(expert_kernel, capacity, features), out_...]
where the time goes in v4:
time: 251 us
  Pallas kernels  248 us (99%)
    pallas_call x1, Pallas kernels, expert_layer(): pl.pallas_call(functools.partial(expert_kernel, capacity, features), out_...  168 us
    pallas_call x1, Pallas kernels, mixer(): pl.pallas_call(mixer_kernel, out_shape=(jax.ShapeDtypeStruct((rows, width...  79.9 us

profile of v4, /device:TPU:1, one launch (start us, length us, event | category | flops | bytes accessed | tf_op | source)
XLA Modules:
  0.0 251.3 jit_solution(1339944145455230575)
XLA Ops:
  0.6 79.9 %mixer.1 = (bf16[256,512]{1,0:T(8,128)(2,1)}, f32[8,256]{1,0:T(8,128)}) custom-call(bf16[128,2048]{1,0:T(8,128)(2,1)} %mixer_ref.1, bf16[128,2048]{1,0:T(8,128)(2,1)} %gate_ref.2, bf16[128,2048]{1,0:T(8,128)(2,1)} %delta_ref.1, f32[16,128]{1,0:T(8,128)} %b_ref.1, f32[16,128]{1,0:T(8,128)} %c_ref.1, f32[4,2048]{1,0:T(4,128)} %taps_ref.1, f32[1,2048]{1,0:T(1,128)} %bitcast.6, ...), custom_call_target="tpu_custom_call" | custom-call | tf_op jit(solution)/shard_map/mixer/pallas_call | solution.py:529
  80.5 0.0 copy-start
  80.5 168.4 %expert_layer.1 = bf16[256,512]{1,0:T(8,128)(2,1)} custom-call(bf16[256,512]{1,0:T(8,128)(2,1)} %get-tuple-element.8.mixer_ref, f32[8,256]{1,0:T(8,128)} %get-tuple-element.5.squares_ref, s32[2,256]{1,0:T(2,128)} %bitcast.9, f32[2,256]{1,0:T(2,128)} %bitcast.10, f32[1,512]{1,0:T(1,128)} %bitcast.11, bf16[1,8192,384]{2,1,0:T(8,128)(2,1)} %gate_ref.3, ...), custom_call_target="tpu_custom_call" | custom-call | tf_op jit(solution)/shard_map/expert_layer/pallas_call | solution.py:1034
  248.9 0.0 copy-done
  248.9 0.7 copy.24
  249.6 1.7 copy.25
Async XLA Ops:
  80.5 168.4 %copy-start = (bf16[256,512]{1,0:T(8,128)(2,1)S(1)}, bf16[256,512]{1,0:T(8,128)(2,1)}, u32[]{:S(2)}) copy-start(bf16[256,512]{1,0:T(8,128)(2,1)} %get-tuple-element.8.mixer_ref) | copy-start | bytes 786436

commit v5 on v4

--- a/solution.py
+++ b/solution.py
@@ -33,8 +33,8 @@
         return a * SIDE + b if half == 0 else b * SIDE + a
 
 
-PEERS = ((1, 0), (1, 1), (2, 0), (2, 1), (0, 0), (0, 1), (-1, 0), (-1, 1))
-OWN = 4
+PEERS = ((0, 0), (0, 1), (2, 0), (2, 1), (1, 0), (1, 1), (-1, 0), (-1, 1))
+OWN = 0
 UNITS = (0, 1, 2, 3)
 
 
@@ -114,6 +114,10 @@
         pl.semaphore_signal(
             barrier, inc=1, device_id={"exp": lax.rem(own + k, EXPERTS)}, device_id_type=MESH
         )
+    for t in range(tokens):
+        b_wide[t] = jnp.broadcast_to(b_ref[:, t : t + 1], (STATES, LANES))
+        c_wide[t] = jnp.broadcast_to(c_ref[:, t : t + 1], (STATES, LANES))
+
     pl.semaphore_wait(barrier, count - 1 + EXPERTS - 1)
 
     def rim_copy(target):
@@ -129,10 +133,6 @@
     @pl.when(me < count - 1)
     def _():
         rim_copy(me + 1).start()
-
-    for t in range(tokens):
-        b_wide[t] = jnp.broadcast_to(b_ref[:, t : t + 1], (STATES, LANES))
-        c_wide[t] = jnp.broadcast_to(c_ref[:, t : t + 1], (STATES, LANES))
 
     def find_step(strip, carry):
         lanes = strip_lanes(strip)
@@ -575,8 +575,8 @@
     capacity, features,
     mixer_ref, squares_ref, ids_ref, route_ref, gain_ref, gate_ref, up_ref, down_ref,
     out_ref,
-    blocks, landed, wide, down, total, hidden, outgoing, answer, returned, all_squares, pick_all, routing,
-    square_sems, dispatch_sems, return_sems, gather_sems, sum_sems, weight_sems,
+    blocks, landed, wide, down, total, hidden, outgoing, answer, returned, all_squares, pick_all, routing, scales_out, scales,
+    square_sems, scale_sems, dispatch_sems, return_sems, gather_sems, sum_sems, weight_sems,
 ):
     torus = Torus()
     me, index = torus.me, torus.index
@@ -640,9 +640,10 @@
         expert = pl.ds(at_peer(number, 1), 1)
         slot = lax.broadcasted_iota(jnp.int32, (capacity, tokens), 0).astype(jnp.float32)
         chosen = (routing[1, expert, :] == slot) & (routing[0, expert, :] > 0.5)
-        pick_all[number * capacity : (number + 1) * capacity, :] = chosen.astype(
-            jnp.float32
-        ).astype(jnp.bfloat16)
+        rows = pl.ds(number * capacity, capacity)
+        pick_all[rows, :] = chosen.astype(jnp.float32).astype(jnp.bfloat16)
+        picked = jnp.dot(pick_all[rows, :], mixer_ref[...], preferred_element_type=jnp.float32)
+        outgoing[rows, :] = (picked * gain_ref[...]).astype(outgoing.dtype)
     pl.semaphore_wait(barrier, count - 1 + EXPERTS - 1)
 
     square_copies = []
@@ -658,29 +659,6 @@
             )
         )
         square_copies[-1].start()
-    all_squares[me] = squares_ref[...]
-    for k in range(1, count):
-        source = lax.rem(me + count - k, count)
-        pltpu.make_async_remote_copy(
-            src_ref=squares_ref,
-            dst_ref=all_squares.at[source],
-            send_sem=square_sems.at[0, k - 1],
-            recv_sem=square_sems.at[1, k - 1],
-            device_id={"ctx": me},
-            device_id_type=MESH,
-        ).wait_recv()
-    scale = lax.rsqrt(jnp.sum(all_squares[...], axis=0)[0:1] / features + 1e-05)
-
-    def pick(chunk, carry):
-        rows = pl.ds(pl.multiple_of(chunk * capacity, 16), capacity)
-        chosen = pick_all[rows, :]
-        picked = jnp.dot(chosen, mixer_ref[...], preferred_element_type=jnp.float32)
-        chosen = chosen.astype(jnp.float32)
-        row_scale = jnp.sum(chosen * scale, axis=1, keepdims=True)
-        outgoing[rows, :] = (picked * row_scale * gain_ref[...]).astype(outgoing.dtype)
-        return carry
-
-    lax.fori_loop(0, EXPERTS, pick, 0)
 
     def rows_of(number):
         return pl.ds(number * capacity, capacity)
@@ -695,10 +673,45 @@
             device_id_type=MESH,
         )
 
-    crossing = [dispatch(n, at_peer(n, 1)) for n in (5, 6, 7, 0, 1, 2, 3)]
+    crossing = [dispatch(n, at_peer(n, 1)) for n in range(1, len(PEERS))]
     for one in crossing:
         one.start()
     blocks[me, rows_of(OWN), :] = outgoing[rows_of(OWN), :]
+
+    def scale_copy(number, target):
+        return pltpu.make_async_remote_copy(
+            src_ref=scales_out.at[number],
+            dst_ref=scales.at[number],
+            send_sem=scale_sems.at[0, number],
+            recv_sem=scale_sems.at[1, number],
+            device_id={"exp": target},
+            device_id_type=MESH,
+        )
+
+    def send_scales():
+        all_squares[me] = squares_ref[...]
+        for k in range(1, count):
+            source = lax.rem(me + count - k, count)
+            pltpu.make_async_remote_copy(
+                src_ref=squares_ref,
+                dst_ref=all_squares.at[source],
+                send_sem=square_sems.at[0, k - 1],
+                recv_sem=square_sems.at[1, k - 1],
+                device_id={"ctx": me},
+                device_id_type=MESH,
+            ).wait_recv()
+        scale = lax.rsqrt(jnp.sum(all_squares[...], axis=0)[0:1] / features + 1e-05)
+        for number in range(len(PEERS)):
+            chosen = pick_all[rows_of(number), :].astype(jnp.float32)
+            row_scale = jnp.sum(chosen * scale, axis=1, keepdims=True)
+            row_scale = jnp.broadcast_to(row_scale, (capacity, LANES))
+            if number == OWN:
+                scales[number] = row_scale
+            else:
+                scales_out[number] = row_scale
+                one = scale_copy(number, at_peer(number, 1))
+                one.start()
+                crossing.append(one)
 
     in_flight = {}
 
@@ -785,56 +798,22 @@
         part = wide[pl.ds(pl.multiple_of(owner * width, 16), width), :]
         total[rows, :] += jnp.dot(blocks[owner, rows, :], part, preferred_element_type=jnp.float32)
 
-    open_unit(2)
-    open_unit(3)
-    total[...] = jnp.zeros_like(total)
-    open_unit(0)
-    ring_one(2)
-    ring_one(3)
-    open_unit(1)
-    for one in weights:
-        one.wait()
-    over_blocks(1, single(0, 0), 1, grow)
-    over_blocks(1, beside, 4, grow)
-    for unit in (2, 3):
-        ring_two(unit)
-    ring_one(0)
-    ring_one(1)
-    over_blocks(0, single(0, 0), 1, grow)
-    over_blocks(1, across_ring, 2, grow)
-    for unit in (2, 3):
-        lines_one(unit)
-    over_blocks(0, beside, 4, grow)
-    for unit in (0, 1):
-        ring_two(unit)
-    for unit in (2, 3):
-        lines_two(unit)
-    over_blocks(1, corner, 4, grow)
-    over_blocks(0, across_ring, 2, grow)
-    for unit in (0, 1):
-        lines_one(unit)
-    over_blocks(1, knight, 4, grow)
-    for unit in (2, 3):
-        last_of(unit, 2)
-    over_blocks(1, single(2, 2), 1, grow)
-    over_blocks(0, corner, 4, grow)
-    for unit in (0, 1):
-        lines_two(unit)
-    over_blocks(0, knight, 4, grow)
-    for unit in (0, 1):
-        last_of(unit, 2)
-    over_blocks(0, single(2, 2), 1, grow)
-
     def activate(group):
+        together = len(PEERS) // 2
+        for number in range(group * together, (group + 1) * together):
+            if number != OWN:
+                scale_copy(number, own_expert).wait_recv()
+
         def one(step, carry):
-            rows = pl.ds(pl.multiple_of(group * row_tile + step * capacity, 16), capacity)
-            gate = total[rows, 0:units]
-            hidden[rows, :] = (
-                gate / (1.0 + jnp.exp(-gate)) * total[rows, units : 2 * units]
-            ).astype(hidden.dtype)
+            number = group * together + step
+            rows = pl.ds(pl.multiple_of(number * capacity, 16), capacity)
+            scale = jnp.concatenate([scales[number]] * (units // LANES), axis=1)
+            gate = total[rows, 0:units] * scale
+            up = total[rows, units : 2 * units] * scale
+            hidden[rows, :] = (gate / (1.0 + jnp.exp(-gate)) * up).astype(hidden.dtype)
             return carry
 
-        lax.fori_loop(0, row_tile // capacity, one, 0)
+        lax.fori_loop(0, together, one, 0)
 
     def project(owner, rows):
         part = down[:, pl.ds(pl.multiple_of(owner * width, LANES), width)]
@@ -946,59 +925,85 @@
                 one.start()
                 summing.append(one)
 
-    def start_lines(group):
-        units = (2 * group, 2 * group + 1)
-        fill(group, single(2, 2), 1)
-        for unit in units:
-            begin(unit, LINES[2])
-        fill(group, knight, 4)
-        for first in (1, -1):
-            for unit in units:
-                begin(unit, LINES[first])
-        fill(group, across_ring, 2)
-        for unit in units:
-            begin(unit, LINES[0])
-
-    def middle_lines(group):
-        units = (2 * group, 2 * group + 1)
-        for unit in units:
-            middle(unit, LINES[2])
-        fill(group, corner, 4)
-        for first in (1, -1):
-            for unit in units:
-                middle(unit, LINES[first])
-        fill(group, beside, 4)
-        for unit in units:
-            middle(unit, LINES[0])
+    def both(group, step, *where):
+        for unit in (2 * group, 2 * group + 1):
+            step(unit, *where)
 
     def finish_lines(group):
-        units = (2 * group, 2 * group + 1)
         fill(group, single(0, 0), 1)
-        for unit in units:
+        for unit in (2 * group, 2 * group + 1):
             finish(unit, LINES[2])
             begin(unit, RING)
         for first in (1, -1):
-            for unit in units:
-                finish(unit, LINES[first])
-        for unit in units:
-            middle(unit, RING)
-        for unit in units:
-            finish(unit, LINES[0])
-
+            both(group, finish, LINES[first])
+        both(group, middle, RING)
+        both(group, finish, LINES[0])
+
+    open_unit(0)
+    send_scales()
+    open_unit(1)
+    ring_one(0)
+    open_unit(2)
+    open_unit(3)
+    ring_one(1)
+    total[...] = jnp.zeros_like(total)
+    for one in weights:
+        one.wait()
+    over_blocks(0, single(0, 0), 1, grow)
+    over_blocks(0, beside, 4, grow)
+    both(0, ring_two)
+    both(1, ring_one)
+    both(0, lines_one)
+    over_blocks(0, across_ring, 2, grow)
+    over_blocks(1, single(0, 0), 1, grow)
+    both(0, lines_two)
+    both(1, ring_two)
+    over_blocks(0, corner, 4, grow)
+    over_blocks(1, beside, 4, grow)
+    both(0, last_of, 2)
+    both(1, lines_one)
+    over_blocks(0, knight, 4, grow)
+    over_blocks(0, single(2, 2), 1, grow)
     activate(0)
-    start_lines(0)
+    fill(0, single(2, 2), 1)
+    both(0, begin, LINES[2])
+    both(1, lines_two)
+    fill(0, knight, 4)
+    both(0, begin, LINES[1])
+    both(0, begin, LINES[-1])
+    fill(0, across_ring, 2)
+    both(0, begin, LINES[0])
+    over_blocks(1, across_ring, 2, grow)
+    over_blocks(1, corner, 4, grow)
+    both(0, middle, LINES[2])
+    both(1, last_of, 2)
+    fill(0, corner, 4)
+    both(0, middle, LINES[1])
+    both(0, middle, LINES[-1])
+    over_blocks(1, knight, 4, grow)
+    over_blocks(1, single(2, 2), 1, grow)
     activate(1)
-    middle_lines(0)
+    fill(0, beside, 4)
+    both(0, middle, LINES[0])
     for one in crossing:
         one.wait_send()
-    start_lines(1)
+    fill(1, single(2, 2), 1)
+    both(1, begin, LINES[2])
+    fill(1, knight, 4)
+    both(1, begin, LINES[1])
+    both(1, begin, LINES[-1])
+    fill(1, across_ring, 2)
+    both(1, begin, LINES[0])
     finish_lines(0)
-    middle_lines(1)
-    for unit in (1, 0):
-        hand_back(unit)
+    both(1, middle, LINES[2])
+    fill(1, corner, 4)
+    both(1, middle, LINES[1])
+    both(1, middle, LINES[-1])
+    fill(1, beside, 4)
+    both(1, middle, LINES[0])
+    both(0, hand_back)
     finish_lines(1)
-    for unit in (3, 2):
-        hand_back(unit)
+    both(1, hand_back)
 
     lane = lax.broadcasted_iota(jnp.int32, (tokens, LANES), 1)
 
@@ -1013,7 +1018,7 @@
         )
 
     value = mixer_ref[...].astype(jnp.float32) + mixed(OWN)
-    for number in (2, 3, 0, 1, 5, 6, 7):
+    for number in range(1, len(PEERS)):
         back(number, own_expert).wait_recv()
         value = value + mixed(number)
     out_ref[...] = value.astype(out_ref.dtype)
@@ -1049,7 +1054,10 @@
             pltpu.VMEM((count,) + squares.shape, f32),
             pltpu.VMEM((slots, rows), bf16),
             pltpu.VMEM((2, EXPERTS, rows), f32),
+            pltpu.VMEM((EXPERTS, capacity, LANES), f32),
+            pltpu.VMEM((EXPERTS, capacity, LANES), f32),
             pltpu.SemaphoreType.DMA((2, count - 1)),
+            pltpu.SemaphoreType.DMA((2, EXPERTS)),
             pltpu.SemaphoreType.DMA((2, EXPERTS)),
             pltpu.SemaphoreType.DMA((2, EXPERTS)),
             pltpu.SemaphoreType.DMA((2, len(UNITS), 5, 4)),

time: 251 us -> 239 us (0.952)
  Pallas kernels: 248 us -> 236 us
    pallas_call x1, Pallas kernels: 168 us -> 156 us  [expert_layer(): pl.pallas_call(functools.partial(expert_kernel, capacity, features), out_...]
where the time goes in v5:
time: 239 us
  Pallas kernels  236 us (99%)
    pallas_call x1, Pallas kernels, expert_layer(): pl.pallas_call(functools.partial(expert_kernel, capacity, features), out_...  156 us
    pallas_call x1, Pallas kernels, mixer(): pl.pallas_call(mixer_kernel, out_shape=(jax.ShapeDtypeStruct((rows, width...  79.9 us

profile of v5, /device:TPU:1, one launch (start us, length us, event | category | flops | bytes accessed | tf_op | source)
XLA Modules:
  0.0 238.7 jit_solution(6416435350434623499)
XLA Ops:
  0.6 79.9 %mixer.1 = (bf16[256,512]{1,0:T(8,128)(2,1)}, f32[8,256]{1,0:T(8,128)}) custom-call(bf16[128,2048]{1,0:T(8,128)(2,1)} %mixer_ref.1, bf16[128,2048]{1,0:T(8,128)(2,1)} %gate_ref.2, bf16[128,2048]{1,0:T(8,128)(2,1)} %delta_ref.1, f32[16,128]{1,0:T(8,128)} %b_ref.1, f32[16,128]{1,0:T(8,128)} %c_ref.1, f32[4,2048]{1,0:T(4,128)} %taps_ref.1, f32[1,2048]{1,0:T(1,128)} %bitcast.6, ...), custom_call_target="tpu_custom_call" | custom-call | tf_op jit(solution)/shard_map/mixer/pallas_call | solution.py:529
  80.5 0.0 copy-start
  80.5 155.8 %expert_layer.1 = bf16[256,512]{1,0:T(8,128)(2,1)} custom-call(bf16[256,512]{1,0:T(8,128)(2,1)} %get-tuple-element.8.mixer_ref, f32[8,256]{1,0:T(8,128)} %get-tuple-element.5.squares_ref, s32[2,256]{1,0:T(2,128)} %bitcast.9, f32[2,256]{1,0:T(2,128)} %bitcast.10, f32[1,512]{1,0:T(1,128)} %bitcast.11, bf16[1,8192,384]{2,1,0:T(8,128)(2,1)} %gate_ref.3, ...), custom_call_target="tpu_custom_call" | custom-call | tf_op jit(solution)/shard_map/expert_layer/pallas_call | solution.py:1039
  236.4 0.0 copy-done
  236.4 0.7 copy.24
  237.1 1.7 copy.25
Async XLA Ops:
  80.5 155.8 %copy-start = (bf16[256,512]{1,0:T(8,128)(2,1)S(1)}, bf16[256,512]{1,0:T(8,128)(2,1)}, u32[]{:S(2)}) copy-start(bf16[256,512]{1,0:T(8,128)(2,1)} %get-tuple-element.8.mixer_ref) | copy-start | bytes 786436

commit v6 on v5

--- a/solution.py
+++ b/solution.py
@@ -101,7 +101,7 @@
     f32 = jnp.float32
 
     def strip_lanes(strip):
-        return pl.ds(pl.multiple_of(strip * STRIP, STRIP), STRIP)
+        return pl.ds(strip * STRIP if isinstance(strip, int) else pl.multiple_of(strip * STRIP, STRIP), STRIP)
 
     load = pltpu.make_async_copy(weight_ref, weight, weight_sem)
     load.start()
@@ -162,7 +162,7 @@
             )
         )
 
-    def prepare(strip, carry):
+    def prepare(strip):
         lanes = strip_lanes(strip)
         padded[0:8] = rim[:, lanes].astype(f32)[8:16]
         padded[8 : 8 + tokens] = mixer_ref[:, lanes].astype(f32)
@@ -189,20 +189,16 @@
         zero = jnp.zeros((STATES, LANES), f32)
         state = lax.fori_loop(0, tokens // 8, group, (zero,) * (STRIP // LANES))
         ends[0, :, lanes] = jnp.concatenate(state, axis=1).astype(ends.dtype)
-        return carry
-
-    half_channels = channels // 2
-    per_half = strips // 2
-
-    def end_copies(stage, half, k, place, target):
-        lanes = pl.ds(half * half_channels, half_channels)
+
+    def end_copies(stage, strip, k, place, target):
+        lanes = strip_lanes(strip)
         pairs = ((ends, line_ends), (spans, line_spans))
         return [
             pltpu.make_async_remote_copy(
                 src_ref=mine.at[stage, :, lanes],
                 dst_ref=whole.at[stage, place, :, lanes],
-                send_sem=end_sems.at[0, stage, half, k - 1, part],
-                recv_sem=end_sems.at[1, stage, half, k - 1, part],
+                send_sem=end_sems.at[0, stage, strip, k - 1, part],
+                recv_sem=end_sems.at[1, stage, strip, k - 1, part],
                 device_id={"ctx": target},
                 device_id_type=MESH,
             )
@@ -220,82 +216,113 @@
 
         return one
 
-    def line_end(half, number, carry):
-        strip = half * per_half + number
+    leaving = []
+
+    def open_strip(strip):
+        prepare(strip)
+        for k in range(1, SIDE):
+            for one in end_copies(0, strip, k, y, index(0, 0, k)):
+                one.start()
+                leaving.append(one)
+        lanes = strip_lanes(strip)
+        line_ends[0, y, :, lanes] = ends[0, :, lanes]
+        line_spans[0, y, :, lanes] = spans[0, :, lanes]
+
+    def close_line(strip):
+        for k in range(1, SIDE):
+            for one in end_copies(0, strip, k, lax.rem(y + SIDE - k, SIDE), me):
+                one.wait_recv()
         lanes = strip_lanes(strip)
         state = lax.fori_loop(0, SIDE, follow(0, strip), jnp.zeros((STATES, STRIP), f32))
         ends[1, :, lanes] = state.astype(ends.dtype)
         spans[1, :, lanes] = sum(line_spans[0, source, :, lanes] for source in range(SIDE))
-        return carry
-
-    leaving = []
-    for half in (0, 1):
-        lax.fori_loop(half * per_half, (half + 1) * per_half, prepare, 0)
-        lanes = pl.ds(half * half_channels, half_channels)
-        for k in range(1, SIDE):
-            leaving += end_copies(0, half, k, y, index(0, 0, k))
-            for one in leaving[-2:]:
-                one.start()
-        line_ends[0, y, :, lanes] = ends[0, :, lanes]
-        line_spans[0, y, :, lanes] = spans[0, :, lanes]
-    for half in (0, 1):
-        for k in range(1, SIDE):
-            for one in end_copies(0, half, k, lax.rem(y + SIDE - k, SIDE), me):
-                one.wait_recv()
-        lax.fori_loop(0, per_half, functools.partial(line_end, half), 0)
         for k in range(1, SIDE):
 
             @pl.when(x + k < SIDE)
             def _():
-                for one in end_copies(1, half, k, x, (x + k) * SIDE + y):
+                for one in end_copies(1, strip, k, x, (x + k) * SIDE + y):
                     one.start()
 
     in_flight = []
 
-    def moved(half, line, kind, first, second, part, towards, target):
+    def moved(strip, line, kind, first, second, part, towards, target):
+        half = strip % 2
+
         def rows(a, b):
             where = (a, b) if half == 0 else (b, a)
             where = tuple((v + 1) % SIDE - 1 for v in where)
             start, size = (0, tokens) if part is None else (part * (tokens // 2), tokens // 2)
-            return rows_all.at[half, pl.ds(SLOTS.index(where) * tokens + start, size), :]
+            return rows_all.at[strip, pl.ds(SLOTS.index(where) * tokens + start, size), :]
 
         return pltpu.make_async_remote_copy(
             src_ref=rows(first, second),
             dst_ref=rows(first - towards[0], second - towards[1]),
-            send_sem=gather_sems.at[0, half, line, kind],
-            recv_sem=gather_sems.at[1, half, line, kind],
+            send_sem=gather_sems.at[0, strip, line, kind],
+            recv_sem=gather_sems.at[1, strip, line, kind],
             device_id={"ctx": target},
             device_id_type=MESH,
         )
 
-    def send(half, line, kind, first, second, part, towards):
-        one = moved(half, line, kind, first, second, part, towards, index(half, *towards))
+    def send(strip, line, kind, first, second, part, towards):
+        target = index(strip % 2, *towards)
+        one = moved(strip, line, kind, first, second, part, towards, target)
         one.start()
         in_flight.append(one)
 
-    def arrived(half, line, kind, first, second, part):
-        moved(half, line, kind, first, second, part, (0, 0), me).wait_recv()
-
-    def send_line(half, first):
-        send(half, LINES[first], 0, first, 0, None, (0, 1))
-        send(half, LINES[first], 1, first, 0, None, (0, -1))
-
-    def pass_on(half, first):
-        arrived(half, LINES[first], 0, first, -1, None)
-        send(half, LINES[first], 2, first, -1, 0, (0, 1))
-        arrived(half, LINES[first], 1, first, 1, None)
-        send(half, LINES[first], 3, first, 1, 1, (0, -1))
-
-    def last_of(half, first):
-        arrived(half, LINES[first], 2, first, 2, 0)
-        arrived(half, LINES[first], 3, first, 2, 1)
-
-    def scan(half, strip, carry):
-        lanes = strip_lanes(half * per_half + strip)
+    def arrived(strip, line, kind, first, second, part):
+        moved(strip, line, kind, first, second, part, (0, 0), me).wait_recv()
+
+    def send_line(strip, first):
+        send(strip, LINES[first], 0, first, 0, None, (0, 1))
+        send(strip, LINES[first], 1, first, 0, None, (0, -1))
+
+    def pass_on(strip, first):
+        arrived(strip, LINES[first], 0, first, -1, None)
+        send(strip, LINES[first], 2, first, -1, 0, (0, 1))
+        arrived(strip, LINES[first], 1, first, 1, None)
+        send(strip, LINES[first], 3, first, 1, 1, (0, -1))
+
+    def last_of(strip, first):
+        arrived(strip, LINES[first], 2, first, 2, 0)
+        arrived(strip, LINES[first], 3, first, 2, 1)
+
+    def ring_one(strip):
+        arrived(strip, RING, 0, -1, 0, None)
+        send(strip, RING, 2, -1, 0, 0, (1, 0))
+        arrived(strip, RING, 1, 1, 0, None)
+        send(strip, RING, 3, 1, 0, 1, (-1, 0))
+        send_line(strip, -1)
+        send_line(strip, 1)
+        pass_on(strip, 0)
+
+    def ring_two(strip):
+        arrived(strip, RING, 2, 2, 0, 0)
+        arrived(strip, RING, 3, 2, 0, 1)
+        send_line(strip, 2)
+        last_of(strip, 0)
+
+    def lines_one(strip):
+        pass_on(strip, -1)
+        pass_on(strip, 1)
+
+    def lines_two(strip):
+        pass_on(strip, 2)
+        last_of(strip, -1)
+        last_of(strip, 1)
+
+    def scan(strip):
+        for k in range(1, SIDE):
+
+            @pl.when(x >= k)
+            def _():
+                for one in end_copies(1, strip, k, x - k, me):
+                    one.wait_recv()
+
+        lanes = strip_lanes(strip)
         rate = lane_parts(rates(lanes))
         state = prefix_ref[:, lanes]
-        state = lax.fori_loop(0, x, follow(1, half * per_half + strip), state)
-        state = lax.fori_loop(0, y, follow(0, half * per_half + strip), state)
+        state = lax.fori_loop(0, x, follow(1, strip), state)
+        state = lax.fori_loop(0, y, follow(0, strip), state)
 
         def group(number, state):
             base = pl.multiple_of(number * 8, 8)
@@ -315,23 +342,25 @@
         lax.fori_loop(0, tokens // 8, group, lane_parts(state))
         gate = gate_ref[:, lanes].astype(f32)
         mixed = summed[...] + gain_ref[:, lanes] * act[:, lanes]
-        rows_all[half, 0:tokens, strip_lanes(strip)] = (
-            mixed * (gate / (1.0 + jnp.exp(-gate)))
-        ).astype(rows_all.dtype)
-        return carry
-
-    for half in (0, 1):
-        for k in range(1, SIDE):
-
-            @pl.when(x >= k)
-            def _():
-                for one in end_copies(1, half, k, x - k, me):
-                    one.wait_recv()
-
-        lax.fori_loop(0, per_half, functools.partial(scan, half), 0)
-        send(half, RING, 0, 0, 0, None, (1, 0))
-        send(half, RING, 1, 0, 0, None, (-1, 0))
-        send_line(half, 0)
+        rows_all[strip, 0:tokens, :] = (mixed * (gate / (1.0 + jnp.exp(-gate)))).astype(
+            rows_all.dtype
+        )
+        send(strip, RING, 0, 0, 0, None, (1, 0))
+        send(strip, RING, 1, 0, 0, None, (-1, 0))
+        send_line(strip, 0)
+
+    open_strip(0)
+    for strip in range(1, strips):
+        open_strip(strip)
+        close_line(strip - 1)
+    scan(0)
+    close_line(strips - 1)
+    for strip in range(1, strips - 1):
+        scan(strip)
+    ring_one(0)
+    scan(strips - 1)
+    for strip in range(1, strips):
+        ring_one(strip)
 
     width = weight.shape[1]
     sibling = own + 1 - 2 * core
@@ -371,10 +400,13 @@
         def one(pair, carry):
             first = first_slot + pair * together
             rows = pl.ds(pl.multiple_of(first * tokens, tokens), together * tokens)
-            value = jnp.dot(
-                rows_all[0, rows, :], weight[0:half_channels], preferred_element_type=f32
-            ) + jnp.dot(
-                rows_all[1, rows, :], weight[half_channels:], preferred_element_type=f32
+            value = sum(
+                jnp.dot(
+                    rows_all[strip, rows, :],
+                    weight[strip * STRIP : (strip + 1) * STRIP],
+                    preferred_element_type=f32,
+                )
+                for strip in range(strips)
             )
             for k in range(together):
                 column, owner, part = of_slot(where, pair * together + k)
@@ -430,42 +462,24 @@
 
     load.wait()
     project(single(0, 0), 1, 0)
-    for half in (0, 1):
-        arrived(half, RING, 0, -1, 0, None)
-        send(half, RING, 2, -1, 0, 0, (1, 0))
-        arrived(half, RING, 1, 1, 0, None)
-        send(half, RING, 3, 1, 0, 1, (-1, 0))
-        send_line(half, -1)
-        send_line(half, 1)
-    for half in (0, 1):
-        pass_on(half, 0)
     project(beside, 4, 1)
     settle(single(0, 0), 1, 0)
-    for half in (0, 1):
-        arrived(half, RING, 2, 2, 0, 0)
-        arrived(half, RING, 3, 2, 0, 1)
-        send_line(half, 2)
-    for half in (0, 1):
-        last_of(half, 0)
+    for strip in range(strips):
+        ring_two(strip)
     project(across_ring, 2, 5)
     settle(beside, 4, 1)
-    for first in (-1, 1):
-        for half in (0, 1):
-            pass_on(half, first)
+    for strip in range(strips):
+        lines_one(strip)
     project(corner, 4, 7)
     settle(across_ring, 2, 5)
-    for half in (0, 1):
-        pass_on(half, 2)
-    for first in (-1, 1):
-        for half in (0, 1):
-            last_of(half, first)
+    for strip in range(strips):
+        lines_two(strip)
     project(knight, 4, 11)
     settle(corner, 4, 7)
-    for half in (0, 1):
-        last_of(half, 2)
+    for strip in range(strips):
+        last_of(strip, 2)
     project(single(2, 2), 1, 15)
     settle(knight, 4, 11)
-
     settle(single(2, 2), 1, 15)
     value = home[...] + residual_ref[...].astype(f32)
     for behind in range(SIDE - 1):
@@ -498,12 +512,12 @@
     def _():
         rim_copy(me + 1).wait_send()
 
-    for half in (0, 1):
+    for strip in range(strips):
         for k in range(1, SIDE):
 
             @pl.when(x + k < SIDE)
             def _():
-                for one in end_copies(1, half, k, x, (x + k) * SIDE + y):
+                for one in end_copies(1, strip, k, x, (x + k) * SIDE + y):
                     one.wait_send()
 
     clear(single(0, 0), 1, 0)
@@ -547,15 +561,15 @@
             pltpu.VMEM((2, 1, channels), f32),
             pltpu.VMEM((2, SIDE, STATES, channels), bf16),
             pltpu.VMEM((2, SIDE, 1, channels), f32),
-            pltpu.VMEM((2, count * tokens, channels // 2), bf16),
+            pltpu.VMEM((channels // STRIP, count * tokens, STRIP), bf16),
             pltpu.VMEM((channels, width), bf16),
             pltpu.VMEM((count, tokens, width), bf16),
             pltpu.VMEM((count, tokens, width), bf16),
             pltpu.VMEM((SIDE - 1, rows, width), bf16),
             pltpu.VMEM((rows, width), f32),
             pltpu.SemaphoreType.DMA((2,)),
-            pltpu.SemaphoreType.DMA((2, 2, 2, SIDE - 1, 2)),
-            pltpu.SemaphoreType.DMA((2, 2, 5, 4)),
+            pltpu.SemaphoreType.DMA((2, 2, channels // STRIP, SIDE - 1, 2)),
+            pltpu.SemaphoreType.DMA((2, channels // STRIP, 5, 4)),
             pltpu.SemaphoreType.DMA((2, count)),
             pltpu.SemaphoreType.DMA((count,)),
             pltpu.SemaphoreType.DMA((SIDE - 1, 2)),
@@ -939,29 +953,26 @@
         both(group, middle, RING)
         both(group, finish, LINES[0])
 
-    open_unit(0)
+    for unit in UNITS:
+        open_unit(unit)
     send_scales()
-    open_unit(1)
-    ring_one(0)
-    open_unit(2)
-    open_unit(3)
-    ring_one(1)
+    both(0, ring_one)
+    both(1, ring_one)
     total[...] = jnp.zeros_like(total)
     for one in weights:
         one.wait()
     over_blocks(0, single(0, 0), 1, grow)
     over_blocks(0, beside, 4, grow)
     both(0, ring_two)
-    both(1, ring_one)
     both(0, lines_one)
+    both(1, ring_two)
     over_blocks(0, across_ring, 2, grow)
     over_blocks(1, single(0, 0), 1, grow)
     both(0, lines_two)
-    both(1, ring_two)
+    both(1, lines_one)
     over_blocks(0, corner, 4, grow)
     over_blocks(1, beside, 4, grow)
     both(0, last_of, 2)
-    both(1, lines_one)
     over_blocks(0, knight, 4, grow)
     over_blocks(0, single(2, 2), 1, grow)
     activate(0)
@@ -1002,9 +1013,6 @@
     fill(1, beside, 4)
     both(1, middle, LINES[0])
     both(0, hand_back)
-    finish_lines(1)
-    both(1, hand_back)
-
     lane = lax.broadcasted_iota(jnp.int32, (tokens, LANES), 1)
 
     def mixed(number):
@@ -1017,8 +1025,11 @@
             preferred_element_type=jnp.float32,
         )
 
+    finish_lines(1)
     value = mixer_ref[...].astype(jnp.float32) + mixed(OWN)
     for number in range(1, len(PEERS)):
+        if number == len(PEERS) // 2:
+            both(1, hand_back)
         back(number, own_expert).wait_recv()
         value = value + mixed(number)
     out_ref[...] = value.astype(out_ref.dtype)

time: 239 us -> 239 us (level)
  no operation moved by 1% of the time
where the time goes in v6:
time: 239 us
  Pallas kernels  236 us (99%)
    pallas_call x1, Pallas kernels, expert_layer(): pl.pallas_call(functools.partial(expert_kernel, capacity, features), out_...  156 us
    pallas_call x1, Pallas kernels, mixer(): pl.pallas_call(mixer_kernel, out_shape=(jax.ShapeDtypeStruct((rows, width...  79.9 us

profile of v6, /device:TPU:1, one launch (start us, length us, event | category | flops | bytes accessed | tf_op | source)
XLA Modules:
  0.0 238.6 jit_solution(6355510863186607837)
XLA Ops:
  0.6 79.9 %mixer.1 = (bf16[256,512]{1,0:T(8,128)(2,1)}, f32[8,256]{1,0:T(8,128)}) custom-call(bf16[128,2048]{1,0:T(8,128)(2,1)} %mixer_ref.1, bf16[128,2048]{1,0:T(8,128)(2,1)} %gate_ref.2, bf16[128,2048]{1,0:T(8,128)(2,1)} %delta_ref.1, f32[16,128]{1,0:T(8,128)} %b_ref.1, f32[16,128]{1,0:T(8,128)} %c_ref.1, f32[4,2048]{1,0:T(4,128)} %taps_ref.1, f32[1,2048]{1,0:T(1,128)} %bitcast.6, ...), custom_call_target="tpu_custom_call" | custom-call | tf_op jit(solution)/shard_map/mixer/pallas_call | solution.py:543
  80.6 0.0 copy-start
  80.6 155.6 %expert_layer.1 = bf16[256,512]{1,0:T(8,128)(2,1)} custom-call(bf16[256,512]{1,0:T(8,128)(2,1)} %get-tuple-element.8.mixer_ref, f32[8,256]{1,0:T(8,128)} %get-tuple-element.5.squares_ref, s32[2,256]{1,0:T(2,128)} %bitcast.9, f32[2,256]{1,0:T(2,128)} %bitcast.10, f32[1,512]{1,0:T(1,128)} %bitcast.11, bf16[1,8192,384]{2,1,0:T(8,128)(2,1)} %gate_ref.3, ...), custom_call_target="tpu_custom_call" | custom-call | tf_op jit(solution)/shard_map/expert_layer/pallas_call | solution.py:1050
  236.2 0.0 copy-done
  236.2 0.7 copy.24
  236.9 1.7 copy.25
Async XLA Ops:
  80.6 155.7 %copy-start = (bf16[256,512]{1,0:T(8,128)(2,1)S(1)}, bf16[256,512]{1,0:T(8,128)(2,1)}, u32[]{:S(2)}) copy-start(bf16[256,512]{1,0:T(8,128)(2,1)} %get-tuple-element.8.mixer_ref) | copy-start | bytes 786436
